TPU v7x, 32 devices: a whole 2x2x4 slice. The times are simulated.
32 devices in a mesh: ctx: 16 (over z, x, core), dp: 2 (over y).
Axes of the slice: x: 2, y: 2, z: 4, core: 2. Of those that a mesh axis runs over, the one named last changes fastest.
Arguments:
- queries: bfloat16 [4096, 4096], P(('dp', 'ctx')), parts along dimension 0, may hold values from -16 to 16
- key_rows: bfloat16 [4096, 4096], P(('dp', 'ctx')), parts along dimension 0, may hold values from -16 to 16
- value_rows: bfloat16 [4096, 4096], P(('dp', 'ctx')), parts along dimension 0, may hold values from -6 to 6
- lengths: int32 [20], P('dp'), parts along dimension 0, may hold values from 1 to 256, 2048 in all
- norm_gain: float32 [4096], replicated, may hold values from 0.1 to 1.9
- filters: bfloat16 [256, 128], replicated, may hold values from -0.5 to 0.5
- bypass: float32 [4096], replicated, may hold values from -4 to 4
Outputs:
- mixed: bfloat16 [4096, 4096], P(('dp', 'ctx')), parts along dimension 0
There are 2 independent parts, one for each index of `dp`. A program takes and returns all parts, laid end to end along the dimension named above; an argument that names none is the same for every part. Nothing has to cross between parts.
Inputs may be any that keep to these rules, and one draw needn't show every extreme that they name: The lengths sum to 2048; one of them is exactly 256.
All inputs are finite; a program needn't handle non-finite values.
Results may differ from a plain program's by a relative error of at most 0.012.
Values may be sent and summed in bfloat16 or wider, within the bound.
No kernel may reach another device: no remote copies, remote signals or barrier semaphores. Data moves between devices by JAX's collectives and lax.ppermute only.
A program may use at most 64 MiB of HBM per device.

v0:
```python
import math

import jax
import jax.numpy as jnp
from jax import lax
from jax.sharding import PartitionSpec as P

HEAD_DIM = 128


def passed_along(x, axis, by):
    length = lax.axis_size(axis)
    pairs = [(i, i + by) for i in range(length) if 0 <= i + by < length]
    return lax.ppermute(x, axis, pairs)


def doc_starts(lengths, first_row, count):
    ends = jnp.cumsum(lengths)
    position = first_row + jnp.arange(count, dtype=jnp.int32)
    passed = ends[None, :] <= position[:, None]
    return jnp.sum(jnp.where(passed, lengths[None, :], 0), axis=1)


def attend(queries, key_block, value_block, key_first, starts, first_row):
    count = queries.shape[0]
    width = queries.shape[1]
    heads = width // HEAD_DIM
    span = key_block.shape[0]
    query_heads = queries.reshape(count, heads, HEAD_DIM)
    key_heads = key_block.reshape(span, heads, HEAD_DIM)
    value_heads = value_block.reshape(span, heads, HEAD_DIM)
    scores = jnp.einsum("thd,uhd->htu", query_heads, key_heads, preferred_element_type=jnp.float32)
    scores = scores * (1.0 / math.sqrt(HEAD_DIM))
    query_pos = first_row + jnp.arange(count, dtype=jnp.int32)
    key_pos = key_first + jnp.arange(span, dtype=jnp.int32)
    valid = (key_pos[None, :] >= starts[:, None]) & (key_pos[None, :] <= query_pos[:, None])
    scores = jnp.where(valid[None], scores, jnp.float32(-1e30))
    top = jnp.max(scores, axis=2, keepdims=True)
    raised = jnp.where(valid[None], jnp.exp(scores - top), jnp.float32(0.0))
    weights = (raised / jnp.sum(raised, axis=2, keepdims=True)).astype(jnp.bfloat16)
    result = jnp.einsum("htu,uhd->thd", weights, value_heads, preferred_element_type=jnp.float32)
    return result.astype(jnp.bfloat16).reshape(count, width)


def banded_conv(window, filters, out_first, out_starts):
    groups = filters.shape[0]
    taps = filters.shape[1]
    span = window.shape[0]
    count = span - taps + 1
    width = window.shape[1]
    group_size = width // groups
    in_position = out_first - (taps - 1) + jnp.arange(span, dtype=jnp.int32)
    keeper = (in_position[None, :] >= out_starts[:, None]).astype(jnp.bfloat16)
    block_size = math.gcd(groups, 32)
    grouped = jnp.transpose(window.reshape(span, groups, group_size), (1, 2, 0))

    def one_block(block_index):
        begin = block_index * block_size
        filter_block = lax.dynamic_slice_in_dim(filters, begin, block_size, 0)
        data_block = lax.dynamic_slice_in_dim(grouped, begin, block_size, 0)
        padded = jnp.concatenate(
            [filter_block[:, ::-1], jnp.zeros((block_size, count), filters.dtype)], axis=1
        )
        tiled = jnp.tile(padded, (1, count))[:, : count * span].reshape(block_size, count, span)
        matrix = tiled * keeper[None]
        return jnp.einsum("gts,gcs->gct", matrix, data_block, preferred_element_type=jnp.float32)

    pieces = lax.map(one_block, jnp.arange(groups // block_size, dtype=jnp.int32))
    joined = pieces.reshape(groups * group_size, count)
    return jnp.transpose(joined, (1, 0))


def shards(queries, key_rows, value_rows, lengths, norm_gain, filters, bypass):
    row_count = queries.shape[0]
    taps = filters.shape[1]
    first_row = lax.axis_index("ctx") * row_count
    starts = doc_starts(lengths, first_row, row_count)
    near_keys, near_values = passed_along((key_rows, value_rows), "ctx", 1)
    far_keys, far_values = passed_along((near_keys, near_values), "ctx", 1)
    all_keys = jnp.concatenate([far_keys, near_keys, key_rows], axis=0)
    all_values = jnp.concatenate([far_values, near_values, value_rows], axis=0)
    attended = attend(queries, all_keys, all_values, first_row - 2 * row_count, starts, first_row)
    attended32 = attended.astype(jnp.float32)
    squares = jnp.mean(attended32 * attended32, axis=1, keepdims=True)
    normed = (attended32 * lax.rsqrt(squares + 1e-06) * norm_gain[None, :]).astype(jnp.bfloat16)
    received = passed_along(normed[row_count - (taps - 1) :], "ctx", 1)
    window = jnp.concatenate([received, normed], axis=0)
    convolved = banded_conv(window, filters, first_row, starts)
    return (convolved + bypass[None, :] * normed.astype(jnp.float32)).astype(jnp.bfloat16)


def solution(mesh):
    in_specs = (
        P(("dp", "ctx"), None),
        P(("dp", "ctx"), None),
        P(("dp", "ctx"), None),
        P("dp"),
        P(),
        P(),
        P(),
    )
    out_specs = P(("dp", "ctx"), None)
    return jax.shard_map(shards, mesh=mesh, in_specs=in_specs, out_specs=out_specs, check_vma=False)
```

profile of v0, /device:TPU:28, one launch (start us, length us, event | category | flops | bytes accessed | tf_op | source)
XLA Modules:
  0.0 206.7 jit_solution(9553974565047140175)
XLA Ops:
  3.7 3.5 %collective-permute-start.2 = (bf16[128,4096]{0,1:T(8,128)(2,1)S(1)}, bf16[128,4096]{0,1:T(8,128)(2,1)S(1)}, u32[]{:S(2)}, u32[]{:S(2)}) collective-permute-start(bf16[128,4096]{0,1:T(8,128)(2,1)S(1)} %copy.22), channel_id=1, source_target_pairs={{0,2},{2,4},{4,6},{6,8},{8,10},{10,12},{12,14},{14,16},{16,18},{18... | collective-permute-start | bytes 3145736 | tf_op jit(solution)/shard_map/ppermute | solution.py:14
  7.2 10.3 %collective-permute-done = bf16[128,4096]{1,0:T(8,128)(2,1)} collective-permute-done((bf16[128,4096]{1,0:T(8,128)(2,1)}, bf16[128,4096]{1,0:T(8,128)(2,1)}, u32[]{:S(2)}, u32[]{:S(2)}) %collective-permute-start) | collective-permute-done | bytes 1048608 | tf_op jit(solution)/shard_map/ppermute | solution.py:14
  20.2 8.4 %collective-permute-done.2 = bf16[128,4096]{0,1:T(8,128)(2,1)S(1)} collective-permute-done((bf16[128,4096]{0,1:T(8,128)(2,1)S(1)}, bf16[128,4096]{0,1:T(8,128)(2,1)S(1)}, u32[]{:S(2)}, u32[]{:S(2)}) %collective-permute-start.2) | collective-permute-done | bytes 1048608 | tf_op jit(solution)/shard_map/ppermute | solution.py:14
  31.4 8.5 %collective-permute-done.1 = bf16[128,4096]{1,0:T(8,128)(2,1)} collective-permute-done((bf16[128,4096]{1,0:T(8,128)(2,1)}, bf16[128,4096]{1,0:T(8,128)(2,1)}, u32[]{:S(2)}, u32[]{:S(2)}) %collective-permute-start.1) | collective-permute-done | bytes 1048608 | tf_op jit(solution)/shard_map/ppermute | solution.py:14
  39.9 3.2 %pad_maximum_fusion = bf16[384,4096]{1,0:T(8,128)(2,1)} fusion(bf16[128,4096]{1,0:T(8,128)(2,1)} %param.11, bf16[128,4096]{1,0:T(8,128)(2,1)} %collective-permute-done, bf16[128,4096]{1,0:T(8,128)(2,1)} %collective-permute-done.1), kind=kLoop, calls=%fused_computation.15 | loop fusion | flops 9437184 | bytes 6291456 | tf_op jit(solution)/shard_map/concatenate | solution.py:81
  43.1 4.7 %copy.21 = bf16[384,4096]{0,1:T(8,128)(2,1)} copy(bf16[384,4096]{1,0:T(8,128)(2,1)} %pad_maximum_fusion) | data formatting | bytes 6291456 | tf_op jit(solution)/shard_map/concatenate | solution.py:81
  47.8 3.4 %collective-permute-done.3 = bf16[128,4096]{0,1:T(8,128)(2,1)} collective-permute-done((bf16[128,4096]{0,1:T(8,128)(2,1)S(1)}, bf16[128,4096]{0,1:T(8,128)(2,1)}, u32[]{:S(2)}, u32[]{:S(2)}) %collective-permute-start.3) | collective-permute-done | bytes 1048608 | tf_op jit(solution)/shard_map/ppermute | solution.py:14
  53.9 2.4 %fusion.29 = (f32[32,128]{1,0:T(8,128)S(1)}, f32[32,128,384]{1,2,0:T(8,128)S(1)}) fusion(f32[32,384,128]{2,1,0:T(8,128)S(1)} %fusion.24, pred[128,384]{0,1:T(8,128)(4,1)S(1)} %compare_and_fusion), kind=kOutput, calls=%fused_computation.41 | output fusion | flops 11010431 | bytes 12648448 | tf_op jit(solution)/shard_map/sub | solution.py:39
  62.0 15.0 %collective-permute-done.4 = bf16[127,4096]{0,1:T(8,128)(2,1)} collective-permute-done((bf16[127,4096]{0,1:T(8,128)(2,1)S(1)}, bf16[127,4096]{0,1:T(8,128)(2,1)}, u32[]{:S(2)}, u32[]{:S(2)}) %collective-permute-start.4) | collective-permute-done | bytes 1040416 | tf_op jit(solution)/shard_map/ppermute | solution.py:14
  77.0 3.4 %pad_maximum_fusion.2 = bf16[255,4096]{0,1:T(8,128)(2,1)} fusion(bf16[128,4096]{0,1:T(8,128)(2,1)S(1)} %fusion.21, bf16[127,4096]{0,1:T(8,128)(2,1)} %collective-permute-done.4), kind=kLoop, calls=%fused_computation.21 | loop fusion | flops 4177920 | bytes 4177920 | tf_op jit(solution)/shard_map/concatenate | solution.py:87
  80.4 122.2 %while.11 = (s32[]{:T(128)}, f32[8,32,16,128]{3,2,1,0:T(8,128)}, s32[8]{0:T(128)S(1)}, bf16[256,16,255]{2,1,0:T(8,128)(2,1)}, bf16[256,128]{1,0:T(8,128)(2,1)}, ...) while((s32[]{:T(128)}, f32[8,32,16,128]{3,2,1,0:T(8,128)}, ...), condition=%wide.region_6.7_spmd.clone, body=%wide.region_5.6_spmd.clone.sunk | while | flops 34533124 | bytes 17467060 | solution.py:68
  85.2 8.0 %reshape.141 = bf16[32,128,255]{2,1,0:T(8,128)(2,1)S(1)} reshape(bf16[32,32640]{1,0:T(8,128)(2,1)} %slice.11) | data formatting | bytes 4177920 | tf_op jit(solution)/shard_map/while/body/eval_jaxpr/reshape | solution.py:64
  100.4 8.0 %reshape.141 = bf16[32,128,255]{2,1,0:T(8,128)(2,1)S(1)} reshape(bf16[32,32640]{1,0:T(8,128)(2,1)} %slice.11) | data formatting | bytes 4177920 | tf_op jit(solution)/shard_map/while/body/eval_jaxpr/reshape | solution.py:64
  115.7 8.0 %reshape.141 = bf16[32,128,255]{2,1,0:T(8,128)(2,1)S(1)} reshape(bf16[32,32640]{1,0:T(8,128)(2,1)} %slice.11) | data formatting | bytes 4177920 | tf_op jit(solution)/shard_map/while/body/eval_jaxpr/reshape | solution.py:64
  131.0 8.0 %reshape.141 = bf16[32,128,255]{2,1,0:T(8,128)(2,1)S(1)} reshape(bf16[32,32640]{1,0:T(8,128)(2,1)} %slice.11) | data formatting | bytes 4177920 | tf_op jit(solution)/shard_map/while/body/eval_jaxpr/reshape | solution.py:64
  139.1 2.3 %fusion.38 = f32[8,32,16,128]{3,2,1,0:T(8,128)} fusion(f32[8,32,16,128]{3,2,1,0:T(8,128)} %get-tuple-element.130, s32[]{:T(128)} %get-tuple-element.129, bf16[32,128,255]{2,1,0:T(8,128)(2,1)S(1)} %reshape.141, bf16[128,255]{1,0:T(8,128)(2,1)S(1)} %compare_convert_fusion.2, bf16[256,16,255]{2,1,0:T(8,128)(2,1)} %get-tuple-element.144, s32[]{:T(128)S(6)} %select_n.32), kind=kOutput, calls=%fused_computation.4.clone.1 | convolution fusion | flops 34467840 | bytes 2679044 | tf_op jit(solution)/shard_map/while/body/eval_jaxpr/gts,gcs->gct/dot_general | solution.py:66
  146.3 8.0 %reshape.141 = bf16[32,128,255]{2,1,0:T(8,128)(2,1)S(1)} reshape(bf16[32,32640]{1,0:T(8,128)(2,1)} %slice.11) | data formatting | bytes 4177920 | tf_op jit(solution)/shard_map/while/body/eval_jaxpr/reshape | solution.py:64
  161.6 8.0 %reshape.141 = bf16[32,128,255]{2,1,0:T(8,128)(2,1)S(1)} reshape(bf16[32,32640]{1,0:T(8,128)(2,1)} %slice.11) | data formatting | bytes 4177920 | tf_op jit(solution)/shard_map/while/body/eval_jaxpr/reshape | solution.py:64
  169.7 2.3 %fusion.38 = f32[8,32,16,128]{3,2,1,0:T(8,128)} fusion(f32[8,32,16,128]{3,2,1,0:T(8,128)} %get-tuple-element.130, s32[]{:T(128)} %get-tuple-element.129, bf16[32,128,255]{2,1,0:T(8,128)(2,1)S(1)} %reshape.141, bf16[128,255]{1,0:T(8,128)(2,1)S(1)} %compare_convert_fusion.2, bf16[256,16,255]{2,1,0:T(8,128)(2,1)} %get-tuple-element.144, s32[]{:T(128)S(6)} %select_n.32), kind=kOutput, calls=%fused_computation.4.clone.1 | convolution fusion | flops 34467840 | bytes 2679044 | tf_op jit(solution)/shard_map/while/body/eval_jaxpr/gts,gcs->gct/dot_general | solution.py:66
  176.9 8.0 %reshape.141 = bf16[32,128,255]{2,1,0:T(8,128)(2,1)S(1)} reshape(bf16[32,32640]{1,0:T(8,128)(2,1)} %slice.11) | data formatting | bytes 4177920 | tf_op jit(solution)/shard_map/while/body/eval_jaxpr/reshape | solution.py:64
  185.0 2.3 %fusion.38 = f32[8,32,16,128]{3,2,1,0:T(8,128)} fusion(f32[8,32,16,128]{3,2,1,0:T(8,128)} %get-tuple-element.130, s32[]{:T(128)} %get-tuple-element.129, bf16[32,128,255]{2,1,0:T(8,128)(2,1)S(1)} %reshape.141, bf16[128,255]{1,0:T(8,128)(2,1)S(1)} %compare_convert_fusion.2, bf16[256,16,255]{2,1,0:T(8,128)(2,1)} %get-tuple-element.144, s32[]{:T(128)S(6)} %select_n.32), kind=kOutput, calls=%fused_computation.4.clone.1 | convolution fusion | flops 34467840 | bytes 2679044 | tf_op jit(solution)/shard_map/while/body/eval_jaxpr/gts,gcs->gct/dot_general | solution.py:66
  192.1 8.0 %reshape.141 = bf16[32,128,255]{2,1,0:T(8,128)(2,1)S(1)} reshape(bf16[32,32640]{1,0:T(8,128)(2,1)} %slice.11) | data formatting | bytes 4177920 | tf_op jit(solution)/shard_map/while/body/eval_jaxpr/reshape | solution.py:64
  200.3 2.3 %fusion.38 = f32[8,32,16,128]{3,2,1,0:T(8,128)} fusion(f32[8,32,16,128]{3,2,1,0:T(8,128)} %get-tuple-element.130, s32[]{:T(128)} %get-tuple-element.129, bf16[32,128,255]{2,1,0:T(8,128)(2,1)S(1)} %reshape.141, bf16[128,255]{1,0:T(8,128)(2,1)S(1)} %compare_convert_fusion.2, bf16[256,16,255]{2,1,0:T(8,128)(2,1)} %get-tuple-element.144, s32[]{:T(128)S(6)} %select_n.32), kind=kOutput, calls=%fused_computation.4.clone.1 | convolution fusion | flops 34467840 | bytes 2679044 | tf_op jit(solution)/shard_map/while/body/eval_jaxpr/gts,gcs->gct/dot_general | solution.py:66
  202.6 2.8 %fusion.19 = bf16[128,4096]{0,1:T(8,128)(2,1)S(1)} fusion(f32[8,32,16,128]{3,2,1,0:T(8,128)} %get-tuple-element.37, f32[4096]{0:T(1024)S(1)} %copy-done.4, f32[4096]{0:T(1024)S(1)} %copy-done.3, f32[128]{0:T(128)S(1)} %add_rsqrt_fusion, f32[32,128,128]{2,1,0:T(8,128)} %copy-done.1), kind=kLoop, calls=%fused_computation.23 | loop fusion | flops 3670016 | bytes 5276160 | tf_op jit(solution)/shard_map/convert_element_type | solution.py:89
  (98 shorter events, 62.6 us)
Async XLA Ops:
  0.0 52.8 %copy-start = (bf16[128,4096]{1,0:T(8,128)(2,1)S(1)}, bf16[128,4096]{1,0:T(8,128)(2,1)}, u32[]{:S(2)}) copy-start(bf16[128,4096]{1,0:T(8,128)(2,1)} %param.9) | copy-start | bytes 3145732
  0.0 17.5 %collective-permute-start = (bf16[128,4096]{1,0:T(8,128)(2,1)}, bf16[128,4096]{1,0:T(8,128)(2,1)}, u32[]{:S(2)}, u32[]{:S(2)}) collective-permute-start(bf16[128,4096]{1,0:T(8,128)(2,1)} %param.11), channel_id=1, source_target_pairs={{0,2},{2,4},{4,6},{6,8},{8,10},{10,12},{12,14},{14,16},{16,18},{18... | collective-permute-start | bytes 3145736 | tf_op jit(solution)/shard_map/ppermute | solution.py:14
  3.7 24.9 %collective-permute-start.2 = (bf16[128,4096]{0,1:T(8,128)(2,1)S(1)}, bf16[128,4096]{0,1:T(8,128)(2,1)S(1)}, u32[]{:S(2)}, u32[]{:S(2)}) collective-permute-start(bf16[128,4096]{0,1:T(8,128)(2,1)S(1)} %copy.22), channel_id=1, source_target_pairs={{0,2},{2,4},{4,6},{6,8},{8,10},{10,12},{12,14},{14,16},{16,18},{18... | collective-permute-start | bytes 3145736 | tf_op jit(solution)/shard_map/ppermute | solution.py:14
  17.5 22.5 %collective-permute-start.1 = (bf16[128,4096]{1,0:T(8,128)(2,1)}, bf16[128,4096]{1,0:T(8,128)(2,1)}, u32[]{:S(2)}, u32[]{:S(2)}) collective-permute-start(bf16[128,4096]{1,0:T(8,128)(2,1)} %collective-permute-done), channel_id=1, source_target_pairs={{0,2},{2,4},{4,6},{6,8},{8,10},{10,12},{12,14},{14,16},{16,18},{18... | collective-permute-start | bytes 3145736 | tf_op jit(solution)/shard_map/ppermute | solution.py:14
  28.6 22.6 %collective-permute-start.3 = (bf16[128,4096]{0,1:T(8,128)(2,1)S(1)}, bf16[128,4096]{0,1:T(8,128)(2,1)}, u32[]{:S(2)}, u32[]{:S(2)}) collective-permute-start(bf16[128,4096]{0,1:T(8,128)(2,1)S(1)} %collective-permute-done.2), channel_id=1, source_target_pairs={{0,2},{2,4},{4,6},{6,8},{8,10},{10,12},{12,14},{14,16},{16,18},{18... | collective-permute-start | bytes 3145736 | tf_op jit(solution)/shard_map/ppermute | solution.py:14
  53.9 2.4 %copy-start.2 = (bf16[384,4096]{0,1:T(8,128)(2,1)S(1)}, bf16[384,4096]{0,1:T(8,128)(2,1)}, u32[]{:S(2)}) copy-start(bf16[384,4096]{0,1:T(8,128)(2,1)} %copy.21) | copy-start | bytes 9437188
  56.3 2.4 %copy-start.3 = (f32[4096]{0:T(1024)S(1)}, f32[4096]{0:T(1024)}, u32[]{:S(2)}) copy-start(f32[4096]{0:T(1024)} %param.13) | copy-start | bytes 49156
  57.3 1.4 copy-start.1
  59.9 17.1 %collective-permute-start.4 = (bf16[127,4096]{0,1:T(8,128)(2,1)S(1)}, bf16[127,4096]{0,1:T(8,128)(2,1)}, u32[]{:S(2)}, u32[]{:S(2)}) collective-permute-start(bf16[127,4096]{0,1:T(8,128)(2,1)S(1)} %slice.9), channel_id=1, source_target_pairs={{0,2},{2,4},{4,6},{6,8},{8,10},{10,12},{12,14},{14,16},{16,18},{18... | collective-permute-start | bytes 3121160 | tf_op jit(solution)/shard_map/ppermute | solution.py:14
  80.4 122.2 %copy-start.4 = (f32[4096]{0:T(1024)S(1)}, f32[4096]{0:T(1024)}, u32[]{:S(2)}) copy-start(f32[4096]{0:T(1024)} %param.15) | copy-start | bytes 49156
where the time goes:
time: 208 us; the launch traced here: 207 us
  local copies, waits for them, and re-layouts  107 us (51%)
  waiting for transfers between devices  45.5 us (22%)
  matrix products  20.7 us (10%)
  other arithmetic  16.6 us (8%)
  starting transfers between devices  11.5 us (6%)
  loops' own time  4.88 us (2%)
    reshape x8, local copies, waits for them, and re-layouts, one_block(): jnp.tile(padded, (1, count))[:, :count * span]  64.3 us
    ppermute x5, waiting for transfers between devices, passed_along(): return lax.ppermute(x, axis, pairs)  45.5 us
    dot_general x8, matrix products, one_block(): jnp.einsum('gts,gcs->gct', matrix, data_block, preferred_element_type=jnp...  18.7 us
    slice x8, local copies, waits for them, and re-layouts, one_block(): jnp.tile(padded, (1, count))[:, :count * span]  11.8 us
    ppermute x5, starting transfers between devices, passed_along(): return lax.ppermute(x, axis, pairs)  11.5 us
    while x8, local copies, waits for them, and re-layouts  9.64 us
    dynamic_slice x8, local copies, waits for them, and re-layouts, one_block(): filter_block = lax.dynamic_slice_in_dim(filters, begin, block_size, 0)  5.63 us
    another operation x1, loops' own time, banded_conv(): lax.map(one_block, jnp.arange(groups // block_size, dtype=jnp.int32))  4.88 us
  transfers between devices with their start and end apart: 5, of which 5 were waited for; matrix products, arithmetic and copies ran while one was open for 5% of the time, Pallas kernels for 0%

commit v1 on v0

v1 whole, which is shorter than its diff:
```python
import math

import jax
import jax.numpy as jnp
from jax import lax
from jax.experimental import pallas as pl
from jax.experimental.pallas import tpu as pltpu
from jax.sharding import PartitionSpec as P

HEAD_DIM = 128
LANES = 128
NEG = -1e30


def permuted(x, pairs):
    return lax.ppermute(x, "ctx", pairs)


def local_starts(lengths, first_row, count):
    ends = jnp.cumsum(lengths)
    position = first_row + jnp.arange(count, dtype=jnp.int32)
    passed = ends[None, :] <= position[:, None]
    return jnp.sum(jnp.where(passed, lengths[None, :], 0), axis=1) - first_row


def weights_kernel(heads, odd_ref, st_ref, qp_ref, q_ref, ka_ref, kb_ref, kn_ref, ko_ref, own_ref, prev_ref, bias_own, bias_prev):
    rows = q_ref.shape[0]

    @pl.when(pl.program_id(0) == 0)
    def _():
        st = st_ref[...]
        row = lax.broadcasted_iota(jnp.int32, (rows, 3 * rows), 0)
        key = lax.broadcasted_iota(jnp.int32, (rows, 3 * rows), 1) - 2 * rows
        bias_own[...] = jnp.where((key >= st) & (key <= row), 0.0, NEG)
        row = lax.broadcasted_iota(jnp.int32, (rows, 2 * rows), 0) - rows
        key = lax.broadcasted_iota(jnp.int32, (rows, 2 * rows), 1) - 2 * rows
        bias_prev[...] = jnp.where((key >= st[0:1, :]) & (key <= row), 0.0, NEG)

    odd = odd_ref[0] == 1
    factor = 1.0 / math.sqrt(HEAD_DIM) * math.log2(math.e)
    dims = (((1,), (1,)), ((), ()))
    for h in range(heads):
        cols = slice(h * HEAD_DIM, (h + 1) * HEAD_DIM)
        kf = jnp.where(odd, kb_ref[:, cols], ka_ref[:, cols])
        kfn = jnp.concatenate([kf, kn_ref[:, cols]], axis=0)
        kfno = jnp.concatenate([kfn, ko_ref[:, cols]], axis=0)
        s = lax.dot_general(q_ref[:, cols], kfno, dims, preferred_element_type=jnp.float32) + bias_own[...]
        s = (s - jnp.max(s, axis=1, keepdims=True)) * factor
        own_ref[h] = jnp.exp2(s).astype(jnp.bfloat16)
        s = lax.dot_general(qp_ref[:, cols], kfn, dims, preferred_element_type=jnp.float32) + bias_prev[...]
        s = (s - jnp.max(s, axis=1, keepdims=True)) * factor
        prev_ref[h] = jnp.exp2(s).astype(jnp.bfloat16)


def finish_kernel(heads, a_steps, odd_ref, st_ref, own_ref, prev_ref, va_ref, vb_ref, vn_ref, vo_ref, taps_ref, gain_ref, bypass_ref, out_ref, att, squares, scale, keep, lhs):
    rows = st_ref.shape[0]
    step = pl.program_id(0)
    all_heads = att.shape[0]
    width = all_heads * LANES

    @pl.when(step == 0)
    def _():
        squares[...] = jnp.zeros_like(squares)
        st = st_ref[...]
        row = lax.broadcasted_iota(jnp.int32, (rows, 2 * rows), 0)
        key = lax.broadcasted_iota(jnp.int32, (rows, 2 * rows), 1) - rows
        keep[...] = jnp.where((key >= st) & (key <= row) & (key > row - rows), 1.0, 0.0).astype(jnp.bfloat16)

    @pl.when(step < a_steps)
    def _():
        odd = odd_ref[0] == 1
        ones = jnp.ones((3 * rows, LANES), jnp.bfloat16)
        for h in range(heads):
            cols = slice(h * HEAD_DIM, (h + 1) * HEAD_DIM)
            vf = jnp.where(odd, vb_ref[:, cols], va_ref[:, cols])
            values = jnp.concatenate([vf, vn_ref[:, cols], vo_ref[:, cols]], axis=0)
            values = jnp.concatenate([values, ones], axis=1)
            o = jnp.dot(prev_ref[h], values[: 2 * rows], preferred_element_type=jnp.float32)
            a = (o[:, :LANES] / o[:, LANES:]).astype(jnp.bfloat16)
            att[step * heads + h, :rows] = a
            a = a.astype(jnp.float32)
            squares[:rows] += a * a
            o = jnp.dot(own_ref[h], values, preferred_element_type=jnp.float32)
            a = (o[:, :LANES] / o[:, LANES:]).astype(jnp.bfloat16)
            att[step * heads + h, rows:] = a
            a = a.astype(jnp.float32)
            squares[rows:] += a * a

    @pl.when(step == a_steps)
    def _():
        total = jnp.sum(squares[...], axis=1, keepdims=True)
        scale[...] = jnp.broadcast_to(lax.rsqrt(total * (1.0 / width) + 1e-06), scale.shape)

    @pl.when(step >= a_steps)
    def _():
        tiles = out_ref.shape[1] // LANES
        groups = taps_ref.shape[0] // tiles
        size = LANES // groups
        lane_group = lax.broadcasted_iota(jnp.int32, (rows, LANES), 1) // size
        first = (step - a_steps) * tiles
        for c in range(tiles):
            cols = slice(c * LANES, (c + 1) * LANES)
            x = att[first + c].astype(jnp.float32) * scale[...] * gain_ref[:, cols]
            x = x.astype(jnp.bfloat16)
            for g in range(groups):
                line = jnp.broadcast_to(taps_ref[c * groups + g : c * groups + g + 1, :], (rows, LANES))
                ring = pltpu.roll(line, 0, 1, stride=1, stride_axis=0).astype(jnp.bfloat16)
                lhs[c % 2, g * rows : (g + 1) * rows, :LANES] = ring * keep[:, :LANES]
                lhs[c % 2, g * rows : (g + 1) * rows, LANES:] = ring * keep[:, LANES:]
            y = jnp.dot(lhs[c % 2], x, preferred_element_type=jnp.float32)
            total = bypass_ref[:, cols] * x[rows:].astype(jnp.float32)
            picked = y[:rows]
            for g in range(1, groups):
                picked = jnp.where(lane_group == g, y[g * rows : (g + 1) * rows], picked)
            out_ref[:, cols] = (total + picked).astype(jnp.bfloat16)


def shards(queries, key_rows, value_rows, lengths, norm_gain, filters, bypass):
    rows, width = queries.shape
    heads = width // HEAD_DIM
    groups, taps = filters.shape
    n = lax.axis_size("ctx")
    me = lax.axis_index("ctx")
    odd = (me % 2).astype(jnp.int32).reshape(1)
    st = local_starts(lengths, me * rows, rows).astype(jnp.int32).reshape(rows, 1)

    ahead = [(i, i + 1) for i in range(n - 1)]
    skip = [(i, i + 2) for i in range(0, n - 2, 2)]
    within = [(i, i + 1) for i in range(0, n - 1, 2)]

    key_near = permuted(key_rows, ahead)
    key_skip = permuted(key_rows, skip)
    query_near = permuted(queries, ahead)
    key_within = permuted(key_near, within)
    value_near = permuted(value_rows, ahead)
    value_skip = permuted(value_rows, skip)
    value_within = permuted(value_near, within)

    hb = 4
    cols = hb * HEAD_DIM
    rowspec = pl.BlockSpec((rows, cols), lambda i: (0, i))
    smem = pl.BlockSpec(memory_space=pltpu.SMEM)
    stspec = pl.BlockSpec((rows, 1), lambda i: (0, 0))
    own, prev = pl.pallas_call(
        lambda *refs: weights_kernel(hb, *refs),
        grid=(heads // hb,),
        out_shape=(
            jax.ShapeDtypeStruct((heads, rows, 3 * rows), jnp.bfloat16),
            jax.ShapeDtypeStruct((heads, rows, 2 * rows), jnp.bfloat16),
        ),
        in_specs=[smem, stspec] + [rowspec] * 6,
        out_specs=(
            pl.BlockSpec((hb, rows, 3 * rows), lambda i: (i, 0, 0)),
            pl.BlockSpec((hb, rows, 2 * rows), lambda i: (i, 0, 0)),
        ),
        scratch_shapes=[pltpu.VMEM((rows, 3 * rows), jnp.float32), pltpu.VMEM((rows, 2 * rows), jnp.float32)],
        compiler_params=pltpu.CompilerParams(vmem_limit_bytes=40 * 2**20),
        cost_estimate=pl.CostEstimate(flops=2 * 5 * rows * rows * width, bytes_accessed=16 * 2**20, transcendentals=0),
        name="weights",
    )(odd, st, query_near, queries, key_skip, key_within, key_near, key_rows)

    mirrored = jnp.roll(filters[:, ::-1], 1, axis=1).astype(jnp.float32)
    ab = 8
    a_steps = heads // ab
    bt = 4
    b_steps = width // (bt * LANES)
    per_tile = groups // (width // LANES)
    clamp_a = lambda i: jnp.minimum(i, a_steps - 1)
    clamp_b = lambda i: jnp.maximum(i - a_steps, 0)
    vspec = pl.BlockSpec((rows, ab * HEAD_DIM), lambda i: (0, clamp_a(i)))
    lane = pl.BlockSpec((1, bt * LANES), lambda i: (0, clamp_b(i)))
    return pl.pallas_call(
        lambda *refs: finish_kernel(ab, a_steps, *refs),
        grid=(a_steps + b_steps,),
        out_shape=jax.ShapeDtypeStruct((rows, width), jnp.bfloat16),
        in_specs=[
            smem,
            stspec,
            pl.BlockSpec((ab, rows, 3 * rows), lambda i: (clamp_a(i), 0, 0)),
            pl.BlockSpec((ab, rows, 2 * rows), lambda i: (clamp_a(i), 0, 0)),
            vspec,
            vspec,
            vspec,
            vspec,
            pl.BlockSpec((bt * per_tile, taps), lambda i: (clamp_b(i), 0)),
            lane,
            lane,
        ],
        out_specs=pl.BlockSpec((rows, bt * LANES), lambda i: (0, clamp_b(i))),
        scratch_shapes=[
            pltpu.VMEM((width // LANES, 2 * rows, LANES), jnp.bfloat16),
            pltpu.VMEM((2 * rows, LANES), jnp.float32),
            pltpu.VMEM((2 * rows, LANES), jnp.float32),
            pltpu.VMEM((rows, 2 * rows), jnp.bfloat16),
            pltpu.VMEM((2, per_tile * rows, 2 * rows), jnp.bfloat16),
        ],
        compiler_params=pltpu.CompilerParams(vmem_limit_bytes=40 * 2**20),
        cost_estimate=pl.CostEstimate(flops=2 * 5 * rows * rows * width, bytes_accessed=16 * 2**20, transcendentals=0),
        name="finish",
    )(odd, st, own, prev, value_skip, value_within, value_near, value_rows, mirrored, norm_gain.reshape(1, width), bypass.reshape(1, width))


def solution(mesh):
    rows = P(("dp", "ctx"), None)
    in_specs = (rows, rows, rows, P("dp"), P(), P(), P())
    return jax.shard_map(shards, mesh=mesh, in_specs=in_specs, out_specs=rows, check_vma=False)
```

time: 208 us -> 83.7 us (0.40)
  local copies, waits for them, and re-layouts: 107 us -> 3.72 us
  matrix products: 20.7 us -> 0 us
  Pallas kernels: 0 us -> 18.4 us
  other arithmetic: 16.6 us -> 2.51 us
  starting transfers between devices: 11.5 us -> 18.1 us
  waiting for transfers between devices: 45.5 us -> 40.2 us
  loops' own time: 4.88 us -> 0 us
    reshape x8 -> x0, local copies, waits for them, and re-layouts: 64.3 us -> none  [one_block(): jnp.tile(padded, (1, count))[:, :count * span]]
    dot_general x10 -> x0, matrix products: 20.7 us -> none  [the longest x8 18.7 us: one_block(): jnp.einsum('gts,gcs->gct', matrix, data_block, preferred_element_type=jnp...]
    pallas_call x0 -> x2, Pallas kernels: none -> 18.4 us  [the longest x1 11.9 us: shards(): pl.pallas_call(lambda *refs: finish_kernel(ab, a_steps, *refs), grid=(a_s...]
    slice x9 -> x2, local copies, waits for them, and re-layouts: 12.2 us -> 1.14 us  [shards(): mirrored = jnp.roll(filters[:, ::-1], 1, axis=1).astype(jnp.float32)]
    dynamic_slice x16 -> x0, local copies, waits for them, and re-layouts: 10.3 us -> none  [the longest x8 5.63 us: one_block(): filter_block = lax.dynamic_slice_in_dim(filters, begin, block_size, 0)]
    while x8 -> x0, local copies, waits for them, and re-layouts: 9.64 us -> none
    concatenate x3 -> x0, other arithmetic: 8.2 us -> none  [the longest x1 3.38 us: shards(): window = jnp.concatenate([received, normed], axis=0)]
    ppermute x5 -> x7, starting transfers between devices: 11.5 us -> 18.1 us  [permuted(): return lax.ppermute(x, 'ctx', pairs)]
  transfers between devices with their start and end apart: 5 -> 7, of which waited for: 5 -> 3; matrix products, arithmetic and copies ran while one was open for 5% -> 5% of each run, Pallas kernels for 0% -> 8%
where the time goes in v1:
time: 83.7 us; the launch traced here: 83.1 us
  waiting for transfers between devices  40.2 us (48%)
  Pallas kernels  18.4 us (22%)
  starting transfers between devices  18.1 us (22%)
  local copies, waits for them, and re-layouts  3.72 us (4%)
  other arithmetic  2.51 us (3%)
    ppermute x7, waiting for transfers between devices, permuted(): return lax.ppermute(x, 'ctx', pairs)  40.2 us
    ppermute x7, starting transfers between devices, permuted(): return lax.ppermute(x, 'ctx', pairs)  18.1 us
    pallas_call x1, Pallas kernels, shards(): pl.pallas_call(lambda *refs: finish_kernel(ab, a_steps, *refs), grid=(a_s...  11.9 us
    pallas_call x1, Pallas kernels, shards(): pl.pallas_call(lambda *refs: weights_kernel(hb, *refs), grid=(heads // hb...  6.53 us
    unnamed x10, local copies, waits for them, and re-layouts  2.46 us
  transfers between devices with their start and end apart: 7, of which 3 were waited for; matrix products, arithmetic and copies ran while one was open for 5% of the time, Pallas kernels for 8%

profile of v1, /device:TPU:28, one launch (start us, length us, event | category | flops | bytes accessed | tf_op | source)
XLA Modules:
  0.0 83.1 jit_solution(7484402337303299208)
XLA Ops:
  0.0 1.9 %collective-permute-start.2 = (bf16[128,4096]{1,0:T(8,128)(2,1)}, bf16[128,4096]{1,0:T(8,128)(2,1)S(1)}, u32[]{:S(2)}, u32[]{:S(2)}) collective-permute-start(bf16[128,4096]{1,0:T(8,128)(2,1)} %refs_7_.2), channel_id=1, source_target_pairs={{0,2},{2,4},{4,6},{6,8},{8,10},{10,12},{12,14},{14,16},{16,18},{18... | collective-permute-start | bytes 3145736 | tf_op jit(solution)/shard_map/ppermute | solution.py:16
  1.9 3.5 %collective-permute-start.5 = (bf16[128,4096]{1,0:T(8,128)(2,1)}, bf16[128,4096]{1,0:T(8,128)(2,1)}, u32[]{:S(2)}, u32[]{:S(2)}) collective-permute-start(bf16[128,4096]{1,0:T(8,128)(2,1)} %refs_7_.3), channel_id=1, source_target_pairs={{0,2},{2,4},{4,6},{6,8},{8,10},{10,12},{12,14},{14,16},{16,18},{18... | collective-permute-start | bytes 3145736 | tf_op jit(solution)/shard_map/ppermute | solution.py:16
  5.4 1.9 %collective-permute-start.1 = (bf16[128,4096]{1,0:T(8,128)(2,1)}, bf16[128,4096]{1,0:T(8,128)(2,1)S(1)}, u32[]{:S(2)}, u32[]{:S(2)}) collective-permute-start(bf16[128,4096]{1,0:T(8,128)(2,1)} %refs_7_.2), channel_id=1, source_target_pairs={{0,4},{4,8},{8,12},{12,16},{16,20},{20,24},{24,28},{1,5},{5,9},{9,... | collective-permute-start | bytes 3145736 | tf_op jit(solution)/shard_map/ppermute | solution.py:16
  7.4 1.9 %collective-permute-start = (bf16[128,4096]{1,0:T(8,128)(2,1)}, bf16[128,4096]{1,0:T(8,128)(2,1)S(1)}, u32[]{:S(2)}, u32[]{:S(2)}) collective-permute-start(bf16[128,4096]{1,0:T(8,128)(2,1)} %refs_3_.1), channel_id=1, source_target_pairs={{0,2},{2,4},{4,6},{6,8},{8,10},{10,12},{12,14},{14,16},{16,18},{18... | collective-permute-start | bytes 3145736 | tf_op jit(solution)/shard_map/ppermute | solution.py:16
  9.3 13.1 %collective-permute-done.2.refs_6_ = bf16[128,4096]{1,0:T(8,128)(2,1)S(1)} collective-permute-done((bf16[128,4096]{1,0:T(8,128)(2,1)}, bf16[128,4096]{1,0:T(8,128)(2,1)S(1)}, u32[]{:S(2)}, u32[]{:S(2)}) %collective-permute-start.2) | collective-permute-done | bytes 1048608 | tf_op jit(solution)/shard_map/ppermute | solution.py:16
  22.4 2.7 %collective-permute-start.3 = (bf16[128,4096]{1,0:T(8,128)(2,1)S(1)}, bf16[128,4096]{1,0:T(8,128)(2,1)}, u32[]{:S(2)}, u32[]{:S(2)}) collective-permute-start(bf16[128,4096]{1,0:T(8,128)(2,1)S(1)} %collective-permute-done.2.refs_6_), channel_id=1, source_target_pairs={{0,2},{4,6},{8,10},{12,14},{16,18},{20,22},{24,26},{28,30},{1,3},{... | collective-permute-start | bytes 3145736 | tf_op jit(solution)/shard_map/ppermute | solution.py:16
  25.1 3.5 %collective-permute-start.4 = (bf16[128,4096]{1,0:T(8,128)(2,1)}, bf16[128,4096]{1,0:T(8,128)(2,1)}, u32[]{:S(2)}, u32[]{:S(2)}) collective-permute-start(bf16[128,4096]{1,0:T(8,128)(2,1)} %refs_7_.3), channel_id=1, source_target_pairs={{0,4},{4,8},{8,12},{12,16},{16,20},{20,24},{24,28},{1,5},{5,9},{9,... | collective-permute-start | bytes 3145736 | tf_op jit(solution)/shard_map/ppermute | solution.py:16
  28.6 16.3 %collective-permute-done.5.refs_6_ = bf16[128,4096]{1,0:T(8,128)(2,1)} collective-permute-done((bf16[128,4096]{1,0:T(8,128)(2,1)}, bf16[128,4096]{1,0:T(8,128)(2,1)}, u32[]{:S(2)}, u32[]{:S(2)}) %collective-permute-start.5) | collective-permute-done | bytes 1048608 | tf_op jit(solution)/shard_map/ppermute | solution.py:16
  44.9 2.6 %collective-permute-start.6 = (bf16[128,4096]{1,0:T(8,128)(2,1)}, bf16[128,4096]{1,0:T(8,128)(2,1)}, u32[]{:S(2)}, u32[]{:S(2)}) collective-permute-start(bf16[128,4096]{1,0:T(8,128)(2,1)} %collective-permute-done.5.refs_6_), channel_id=1, source_target_pairs={{0,2},{4,6},{8,10},{12,14},{16,18},{20,22},{24,26},{28,30},{1,3},{... | collective-permute-start | bytes 3145736 | tf_op jit(solution)/shard_map/ppermute | solution.py:16
  47.5 0.8 reduce-window.8
  48.4 0.7 select_reduce_fusion
  49.1 0.1 copy.11.refs_1_
  49.2 0.9 %slice.13 = bf16[256,127]{1,0:T(8,128)(2,1)S(1)} slice(bf16[256,128]{1,0:T(8,128)(2,1)} %param.12), slice={[0:256], [1:128]} | slice | bytes 130048 | tf_op jit(solution)/shard_map/jit(_roll_static)/slice | solution.py:162
  50.2 0.2 slice.14
  50.4 0.9 %maximum_convert_fusion.refs_8_ = f32[256,128]{1,0:T(8,128)S(1)} fusion(bf16[256,127]{1,0:T(8,128)(2,1)S(1)} %slice.14, bf16[256,1]{1,0:T(8,128)(2,1)} %bitcast.10), kind=kLoop, calls=%fused_computation | loop fusion | flops 131072 | bytes 196608 | tf_op jit(solution)/shard_map/convert_element_type | solution.py:162
  51.3 10.8 %collective-permute-done.refs_2_ = bf16[128,4096]{1,0:T(8,128)(2,1)S(1)} collective-permute-done((bf16[128,4096]{1,0:T(8,128)(2,1)}, bf16[128,4096]{1,0:T(8,128)(2,1)S(1)}, u32[]{:S(2)}, u32[]{:S(2)}) %collective-permute-start) | collective-permute-done | bytes 1048608 | tf_op jit(solution)/shard_map/ppermute | solution.py:16
  62.2 0.0 collective-permute-done.1.refs_4_
  62.2 0.0 collective-permute-done.3.refs_5_
  62.2 1.2 %copy-done = bf16[128,4096]{1,0:T(8,128)(2,1)S(1)} copy-done((bf16[128,4096]{1,0:T(8,128)(2,1)S(1)}, bf16[128,4096]{1,0:T(8,128)(2,1)}, u32[]{:S(2)}) %copy-start) | copy-done | bytes 1048600
  63.4 1.2 %copy-done.1 = bf16[128,4096]{1,0:T(8,128)(2,1)S(1)} copy-done((bf16[128,4096]{1,0:T(8,128)(2,1)S(1)}, bf16[128,4096]{1,0:T(8,128)(2,1)}, u32[]{:S(2)}) %copy-start.1) | copy-done | bytes 1048600
  64.6 6.5 %weights.1 = (bf16[32,128,384]{2,1,0:T(8,128)(2,1)S(1)}, bf16[32,128,256]{2,1,0:T(8,128)(2,1)S(1)}) custom-call(s32[1]{0:T(128)} %bitcast.refs_0_, s32[128,1]{1,0:T(8,128)S(1)} %copy.11.refs_1_, bf16[128,4096]{1,0:T(8,128)(2,1)S(1)} %collective-permute-done.refs_2_, bf16[128,4096]{1,0:T(8,128)(2,1)S(1)} %copy-done, ...), custom_call_target="tpu_custom_call" | custom-call | flops 671088640 | bytes 16777216 | tf_op jit(solution)/shard_map/weights/pallas_call | solution.py:144
  71.2 0.0 collective-permute-done.4.refs_4_
  71.2 0.0 collective-permute-done.6.refs_5_
  71.2 11.9 %finish.1 = bf16[128,4096]{1,0:T(8,128)(2,1)} custom-call(s32[1]{0:T(128)} %bitcast.refs_0_, s32[128,1]{1,0:T(8,128)S(1)} %copy.11.refs_1_, bf16[32,128,384]{2,1,0:T(8,128)(2,1)S(1)} %get-tuple-element.7.refs_2_, bf16[32,128,256]{2,1,0:T(8,128)(2,1)S(1)} %get-tuple-element.8.refs_3_, bf16[128,4096]{1,0:T(8,128)(2,1)} %collective-permute-done.4.refs_4_, ...), custom_call_target="tpu_custom_call" | custom-call | flops 671088640 | bytes 16777216 | tf_op jit(solution)/shard_map/finish/pallas_call | solution.py:172
  (10 shorter events, 0.0 us)
Async XLA Ops:
  0.0 22.4 %collective-permute-start.2 = (bf16[128,4096]{1,0:T(8,128)(2,1)}, bf16[128,4096]{1,0:T(8,128)(2,1)S(1)}, u32[]{:S(2)}, u32[]{:S(2)}) collective-permute-start(bf16[128,4096]{1,0:T(8,128)(2,1)} %refs_7_.2), channel_id=1, source_target_pairs={{0,2},{2,4},{4,6},{6,8},{8,10},{10,12},{12,14},{14,16},{16,18},{18... | collective-permute-start | bytes 3145736 | tf_op jit(solution)/shard_map/ppermute | solution.py:16
  1.9 43.0 %collective-permute-start.5 = (bf16[128,4096]{1,0:T(8,128)(2,1)}, bf16[128,4096]{1,0:T(8,128)(2,1)}, u32[]{:S(2)}, u32[]{:S(2)}) collective-permute-start(bf16[128,4096]{1,0:T(8,128)(2,1)} %refs_7_.3), channel_id=1, source_target_pairs={{0,2},{2,4},{4,6},{6,8},{8,10},{10,12},{12,14},{14,16},{16,18},{18... | collective-permute-start | bytes 3145736 | tf_op jit(solution)/shard_map/ppermute | solution.py:16
  5.4 56.7 %collective-permute-start.1 = (bf16[128,4096]{1,0:T(8,128)(2,1)}, bf16[128,4096]{1,0:T(8,128)(2,1)S(1)}, u32[]{:S(2)}, u32[]{:S(2)}) collective-permute-start(bf16[128,4096]{1,0:T(8,128)(2,1)} %refs_7_.2), channel_id=1, source_target_pairs={{0,4},{4,8},{8,12},{12,16},{16,20},{20,24},{24,28},{1,5},{5,9},{9,... | collective-permute-start | bytes 3145736 | tf_op jit(solution)/shard_map/ppermute | solution.py:16
  7.4 54.8 %collective-permute-start = (bf16[128,4096]{1,0:T(8,128)(2,1)}, bf16[128,4096]{1,0:T(8,128)(2,1)S(1)}, u32[]{:S(2)}, u32[]{:S(2)}) collective-permute-start(bf16[128,4096]{1,0:T(8,128)(2,1)} %refs_3_.1), channel_id=1, source_target_pairs={{0,2},{2,4},{4,6},{6,8},{8,10},{10,12},{12,14},{14,16},{16,18},{18... | collective-permute-start | bytes 3145736 | tf_op jit(solution)/shard_map/ppermute | solution.py:16
  22.4 39.8 %collective-permute-start.3 = (bf16[128,4096]{1,0:T(8,128)(2,1)S(1)}, bf16[128,4096]{1,0:T(8,128)(2,1)}, u32[]{:S(2)}, u32[]{:S(2)}) collective-permute-start(bf16[128,4096]{1,0:T(8,128)(2,1)S(1)} %collective-permute-done.2.refs_6_), channel_id=1, source_target_pairs={{0,2},{4,6},{8,10},{12,14},{16,18},{20,22},{24,26},{28,30},{1,3},{... | collective-permute-start | bytes 3145736 | tf_op jit(solution)/shard_map/ppermute | solution.py:16
  25.1 46.1 %collective-permute-start.4 = (bf16[128,4096]{1,0:T(8,128)(2,1)}, bf16[128,4096]{1,0:T(8,128)(2,1)}, u32[]{:S(2)}, u32[]{:S(2)}) collective-permute-start(bf16[128,4096]{1,0:T(8,128)(2,1)} %refs_7_.3), channel_id=1, source_target_pairs={{0,4},{4,8},{8,12},{12,16},{16,20},{20,24},{24,28},{1,5},{5,9},{9,... | collective-permute-start | bytes 3145736 | tf_op jit(solution)/shard_map/ppermute | solution.py:16
  44.9 26.2 %collective-permute-start.6 = (bf16[128,4096]{1,0:T(8,128)(2,1)}, bf16[128,4096]{1,0:T(8,128)(2,1)}, u32[]{:S(2)}, u32[]{:S(2)}) collective-permute-start(bf16[128,4096]{1,0:T(8,128)(2,1)} %collective-permute-done.5.refs_6_), channel_id=1, source_target_pairs={{0,2},{4,6},{8,10},{12,14},{16,18},{20,22},{24,26},{28,30},{1,3},{... | collective-permute-start | bytes 3145736 | tf_op jit(solution)/shard_map/ppermute | solution.py:16
  62.2 1.2 %copy-start = (bf16[128,4096]{1,0:T(8,128)(2,1)S(1)}, bf16[128,4096]{1,0:T(8,128)(2,1)}, u32[]{:S(2)}) copy-start(bf16[128,4096]{1,0:T(8,128)(2,1)} %refs_3_.1) | copy-start | bytes 3145732
  63.4 1.2 %copy-start.1 = (bf16[128,4096]{1,0:T(8,128)(2,1)S(1)}, bf16[128,4096]{1,0:T(8,128)(2,1)}, u32[]{:S(2)}) copy-start(bf16[128,4096]{1,0:T(8,128)(2,1)} %refs_7_.2) | copy-start | bytes 3145732
  64.6 6.6 %copy-start.2 = (bf16[128,4096]{1,0:T(8,128)(2,1)S(1)}, bf16[128,4096]{1,0:T(8,128)(2,1)}, u32[]{:S(2)}) copy-start(bf16[128,4096]{1,0:T(8,128)(2,1)} %refs_7_.3) | copy-start | bytes 3145732
  64.6 6.6 %copy-start.3 = (f32[4096]{0:T(1024)S(1)}, f32[4096]{0:T(1024)}, u32[]{:S(2)}) copy-start(f32[4096]{0:T(1024)} %param.11) | copy-start | bytes 49156
  64.6 6.6 %copy-start.4 = (f32[4096]{0:T(1024)S(1)}, f32[4096]{0:T(1024)}, u32[]{:S(2)}) copy-start(f32[4096]{0:T(1024)} %param.13) | copy-start | bytes 49156

commit v2 on v1

v2 whole, which is shorter than its diff:
```python
import math

import jax
import jax.numpy as jnp
from jax import lax
from jax.experimental import pallas as pl
from jax.experimental.pallas import tpu as pltpu
from jax.sharding import PartitionSpec as P

HEAD_DIM = 128
LANES = 128
NEG = -1e30
FACTOR = 1.0 / math.sqrt(HEAD_DIM) * math.log2(math.e)
CONTRACT_LAST = (((1,), (1,)), ((), ()))
VMEM_BYTES = 40 * 2**20

ODD, BEFORE, NEXT_BEFORE, NEXT_AFTER = range(4)


def permuted(x, pairs):
    return lax.ppermute(x, "ctx", pairs)


def after(x, *others):
    return lax.optimization_barrier((x, *others))[0]


def places(lengths, first_row, count):
    ends = jnp.cumsum(lengths)
    position = first_row + jnp.arange(count + 1, dtype=jnp.int32)
    passed = ends[None, :] <= position[:, None]
    starts = jnp.sum(jnp.where(passed, lengths[None, :], 0), axis=1) - first_row
    past = jnp.min(jnp.where(passed[count], jnp.int32(2**30), ends)) - first_row - count
    odd = (first_row // count) % 2
    facts = jnp.stack([odd, -starts[0], count - starts[count], past]).astype(jnp.int32)
    return starts[:count].astype(jnp.int32).reshape(count, 1), facts


def bias_of(rows, columns, row_first, key_first, start):
    row = lax.broadcasted_iota(jnp.int32, (rows, columns), 0) + row_first
    key = lax.broadcasted_iota(jnp.int32, (rows, columns), 1) + key_first
    return jnp.where((key >= start) & (key <= row), 0.0, NEG)


def scored(query, key, bias):
    s = lax.dot_general(query, key, CONTRACT_LAST, preferred_element_type=jnp.float32) + bias
    top = jnp.max(s, axis=1, keepdims=True)
    return jnp.exp2((s - top) * FACTOR).astype(jnp.bfloat16), top


def summed(weights, value):
    ones = jnp.ones(value.shape, jnp.bfloat16)
    o = jnp.dot(weights, jnp.concatenate([value, ones], axis=1), preferred_element_type=jnp.float32)
    return o[:, :LANES], o[:, LANES:]


def share_kernel(heads, facts_ref, qb_ref, q_ref, kn_ref, ko_ref, vn_ref, vo_ref, b_ref, stat_ref, c_ref, bias):
    rows = q_ref.shape[0]
    step = pl.program_id(0)
    before = facts_ref[NEXT_BEFORE]
    past = facts_ref[NEXT_AFTER]
    odd = facts_ref[ODD] == 1

    @pl.when(odd & (before <= rows))
    def _():
        b_ref[...] = vo_ref[...]
        c_ref[...] = q_ref[...]

    @pl.when(odd & (before > rows))
    def _():
        @pl.when(step == 0)
        def _():
            bias[:rows] = bias_of(rows, 2 * rows, rows, -rows, rows - before)
            bias[rows:] = bias_of(rows, 2 * rows, 0, -rows, rows - before)

        lane = lax.broadcasted_iota(jnp.int32, (rows, LANES), 1)
        ours = lax.broadcasted_iota(jnp.int32, (rows, LANES), 0) < past
        stat = stat_ref[...]
        for h in range(heads):
            cols = slice(h * HEAD_DIM, (h + 1) * HEAD_DIM)
            key = jnp.concatenate([kn_ref[:, cols], ko_ref[:, cols]], axis=0)
            value = jnp.concatenate([vn_ref[:, cols], vo_ref[:, cols]], axis=0)
            query = jnp.concatenate([qb_ref[:, cols], q_ref[:, cols]], axis=0)
            weights, top = scored(query, key, bias[...])
            o, l = summed(weights, value)
            o = (o / l).astype(jnp.bfloat16)
            b_ref[:, cols] = o[:rows]
            c_ref[:, cols] = o[rows:]
            lse = jnp.where(ours, top[:rows] * FACTOR + jnp.log2(l[:rows]), NEG)
            stat = jnp.where(lane == step * heads + h, lse, stat)
        stat_ref[...] = stat


def weights_kernel(heads, facts_ref, st_ref, q_ref, ko_ref, kp_ref, kf_ref, kn_ref, qn_ref, own_ref, prev_ref, top_ref, bias_own, bias_prev):
    rows = q_ref.shape[0]
    step = pl.program_id(0)
    odd = facts_ref[ODD] == 1

    @pl.when(step == 0)
    def _():
        low = jnp.where((facts_ref[ODD] == 0) & (facts_ref[BEFORE] > rows), 0, -(2**20))
        st = jnp.maximum(st_ref[...], low)
        bias_own[...] = bias_of(rows, 3 * rows, 0, -2 * rows, st)
        bias_prev[...] = bias_of(rows, 2 * rows, -rows, -2 * rows, st_ref[0:1, :])

    @pl.when(odd)
    def _():
        for h in range(heads):
            cols = slice(h * HEAD_DIM, (h + 1) * HEAD_DIM)
            key = jnp.concatenate([kf_ref[:, cols], kn_ref[:, cols], ko_ref[:, cols]], axis=0)
            own_ref[h] = scored(q_ref[:, cols], key, bias_own[...])[0]
            prev_ref[h] = scored(qn_ref[:, cols], key[: 2 * rows], bias_prev[...])[0]

    @pl.when(jnp.logical_not(odd))
    def _():
        lane = lax.broadcasted_iota(jnp.int32, (rows, LANES), 1)
        tops = top_ref[...]
        for h in range(heads):
            cols = slice(h * HEAD_DIM, (h + 1) * HEAD_DIM)
            key = jnp.concatenate([kp_ref[:, cols], ko_ref[:, cols]], axis=0)
            weights, top = scored(q_ref[:, cols], key, bias_own[:, rows:])
            own_ref[h, :, rows:] = weights
            tops = jnp.where(lane == step * heads + h, top * FACTOR, tops)
        top_ref[...] = tops


def values_kernel(heads, facts_ref, own_ref, prev_ref, top_ref, stat_ref, vp_ref, vf_ref, vn_ref, vo_ref, att_ref, near_ref, sq_ref, sq_near_ref):
    rows = vo_ref.shape[0]
    step = pl.program_id(0)
    odd = facts_ref[ODD] == 1

    @pl.when(step == 0)
    def _():
        sq_ref[...] = jnp.zeros_like(sq_ref)
        sq_near_ref[...] = jnp.zeros_like(sq_near_ref)

    @pl.when(odd)
    def _():
        for h in range(heads):
            cols = slice(h * HEAD_DIM, (h + 1) * HEAD_DIM)
            value = jnp.concatenate([vf_ref[:, cols], vn_ref[:, cols], vo_ref[:, cols]], axis=0)
            o, l = summed(own_ref[h], value)
            a = (o / l).astype(jnp.bfloat16)
            att_ref[h] = a
            a = a.astype(jnp.float32)
            sq_ref[...] += a * a
            o, l = summed(prev_ref[h], value[: 2 * rows])
            a = (o / l).astype(jnp.bfloat16)
            near_ref[h] = a
            a = a.astype(jnp.float32)
            sq_near_ref[...] += a * a

    @pl.when(jnp.logical_not(odd))
    def _():
        lane = lax.broadcasted_iota(jnp.int32, (rows, LANES), 1)
        shared = facts_ref[BEFORE] > rows
        for h in range(heads):
            cols = slice(h * HEAD_DIM, (h + 1) * HEAD_DIM)
            value = jnp.concatenate([vp_ref[:, cols], vo_ref[:, cols]], axis=0)
            o, l = summed(own_ref[h, :, rows:], value)
            mine = lane == step * heads + h
            top = jnp.sum(jnp.where(mine, top_ref[...], 0.0), axis=1, keepdims=True)
            lse = jnp.sum(jnp.where(mine, stat_ref[...], 0.0), axis=1, keepdims=True)
            lse = jnp.where(shared, lse, NEG)
            high = jnp.maximum(top, lse)
            here = jnp.exp2(top - high)
            there = jnp.exp2(lse - high)
            o = o * here + vp_ref[:, cols].astype(jnp.float32) * there
            a = (o / (l * here + there)).astype(jnp.bfloat16)
            att_ref[h] = a
            a = a.astype(jnp.float32)
            sq_ref[...] += a * a


def finish_kernel(heads, a_steps, facts_ref, st_ref, kp_ref, vp_ref, c_ref, near_ref, sq_ref, sq_near_ref, att_ref, taps_ref, gain_ref, bypass_ref, out_ref, prev, squares, scale, keep, lhs, bias):
    rows = st_ref.shape[0]
    step = pl.program_id(0)
    width = prev.shape[0] * LANES
    odd = facts_ref[ODD] == 1
    shared = facts_ref[BEFORE] > rows

    @pl.when(step == 0)
    def _():
        squares[...] = sq_near_ref[...]
        st = st_ref[...]
        row = lax.broadcasted_iota(jnp.int32, (rows, 2 * rows), 0)
        key = lax.broadcasted_iota(jnp.int32, (rows, 2 * rows), 1) - rows
        keep[...] = jnp.where((key >= st) & (key <= row) & (key > row - rows), 1.0, 0.0).astype(jnp.bfloat16)
        bias[...] = bias_of(rows, rows, -rows, -rows, st[0:1, :])

    @pl.when((step < a_steps) & odd)
    def _():
        for h in range(heads):
            prev[step * heads + h] = near_ref[h]

    @pl.when((step < a_steps) & jnp.logical_not(odd) & shared)
    def _():
        for h in range(heads):
            a = c_ref[:, h * HEAD_DIM : (h + 1) * HEAD_DIM]
            prev[step * heads + h] = a
            a = a.astype(jnp.float32)
            squares[...] += a * a

    @pl.when((step < a_steps) & jnp.logical_not(odd) & jnp.logical_not(shared))
    def _():
        for h in range(heads):
            cols = slice(h * HEAD_DIM, (h + 1) * HEAD_DIM)
            weights, _ = scored(c_ref[:, cols], kp_ref[:, cols], bias[...])
            o, l = summed(weights, vp_ref[:, cols])
            a = (o / l).astype(jnp.bfloat16)
            prev[step * heads + h] = a
            a = a.astype(jnp.float32)
            squares[...] += a * a

    @pl.when(step == a_steps)
    def _():
        total = jnp.sum(squares[...], axis=1, keepdims=True)
        scale[:rows] = jnp.broadcast_to(lax.rsqrt(total * (1.0 / width) + 1e-06), squares.shape)
        total = jnp.sum(sq_ref[...], axis=1, keepdims=True)
        scale[rows:] = jnp.broadcast_to(lax.rsqrt(total * (1.0 / width) + 1e-06), squares.shape)

    @pl.when(step >= a_steps)
    def _():
        tiles = out_ref.shape[1] // LANES
        groups = taps_ref.shape[0] // tiles
        size = LANES // groups
        lane_group = lax.broadcasted_iota(jnp.int32, (rows, LANES), 1) // size
        first = (step - a_steps) * tiles
        for c in range(tiles):
            cols = slice(c * LANES, (c + 1) * LANES)
            x = jnp.concatenate([prev[first + c], att_ref[c]], axis=0)
            x = (x.astype(jnp.float32) * scale[...] * gain_ref[:, cols]).astype(jnp.bfloat16)
            for g in range(groups):
                line = jnp.broadcast_to(taps_ref[c * groups + g : c * groups + g + 1, :], (rows, LANES))
                ring = pltpu.roll(line, 0, 1, stride=1, stride_axis=0).astype(jnp.bfloat16)
                lhs[c % 2, g * rows : (g + 1) * rows, :LANES] = ring * keep[:, :LANES]
                lhs[c % 2, g * rows : (g + 1) * rows, LANES:] = ring * keep[:, LANES:]
            y = jnp.dot(lhs[c % 2], x, preferred_element_type=jnp.float32)
            total = bypass_ref[:, cols] * x[rows:].astype(jnp.float32)
            picked = y[:rows]
            for g in range(1, groups):
                picked = jnp.where(lane_group == g, y[g * rows : (g + 1) * rows], picked)
            out_ref[:, cols] = (total + picked).astype(jnp.bfloat16)


def params():
    return pltpu.CompilerParams(vmem_limit_bytes=VMEM_BYTES)


def shards(queries, key_rows, value_rows, lengths, norm_gain, filters, bypass):
    rows, width = queries.shape
    heads = width // HEAD_DIM
    groups, taps = filters.shape
    n = lax.axis_size("ctx")
    st, facts = places(lengths, lax.axis_index("ctx") * rows, rows)

    back = [(i, i - 1) for i in range(2, n, 2)]
    within = [(i, i + 1) for i in range(0, n - 1, 2)]
    across = [(i, i + 1) for i in range(1, n - 1, 2)]

    smem = pl.BlockSpec(memory_space=pltpu.SMEM)
    wide = jax.ShapeDtypeStruct((rows, width), jnp.bfloat16)
    stats = jax.ShapeDtypeStruct((rows, LANES), jnp.float32)
    whole = lambda shape: pl.BlockSpec(shape, lambda i: (0,) * len(shape))
    starts = whole((rows, 1))
    square = whole((rows, LANES))
    wide_bytes = rows * width * 2
    tile_flops = 4 * rows * rows * width

    query_back = permuted(queries, back)
    key_near = permuted(key_rows, within)
    value_near = permuted(value_rows, within)
    query_near = permuted(queries, within)
    key_across = permuted(after(key_rows, query_back), across)

    hb = 4
    block = pl.BlockSpec((rows, hb * HEAD_DIM), lambda i: (0, i))
    slot_b, stat, slot_c = pl.pallas_call(
        lambda *refs: share_kernel(hb, *refs),
        grid=(heads // hb,),
        out_shape=(wide, stats, wide),
        in_specs=[smem] + [block] * 6,
        out_specs=(block, square, block),
        scratch_shapes=[pltpu.VMEM((2 * rows, 2 * rows), jnp.float32)],
        compiler_params=params(),
        cost_estimate=pl.CostEstimate(flops=4 * tile_flops, bytes_accessed=8 * wide_bytes, transcendentals=0),
        name="share",
    )(facts, query_back, queries, key_near, key_rows, value_near, value_rows)

    stat_across = permuted(stat, across)
    b_across = permuted(slot_b, across)
    c_across = permuted(after(slot_c, key_across), across)
    key_far = permuted(key_across, within)

    own_spec = lambda size: pl.BlockSpec((size, rows, 3 * rows), lambda i: (i, 0, 0))
    prev_spec = lambda size: pl.BlockSpec((size, rows, 2 * rows), lambda i: (i, 0, 0))
    own, prev, tops = pl.pallas_call(
        lambda *refs: weights_kernel(hb, *refs),
        grid=(heads // hb,),
        out_shape=(
            jax.ShapeDtypeStruct((heads, rows, 3 * rows), jnp.bfloat16),
            jax.ShapeDtypeStruct((heads, rows, 2 * rows), jnp.bfloat16),
            stats,
        ),
        in_specs=[smem, starts] + [block] * 6,
        out_specs=(own_spec(hb), prev_spec(hb), square),
        scratch_shapes=[pltpu.VMEM((rows, 3 * rows), jnp.float32), pltpu.VMEM((rows, 2 * rows), jnp.float32)],
        compiler_params=params(),
        cost_estimate=pl.CostEstimate(flops=5 * tile_flops, bytes_accessed=11 * wide_bytes, transcendentals=0),
        name="weights",
    )(facts, st, queries, key_rows, key_across, key_far, key_near, query_near)

    value_far = permuted(after(b_across, own), within)

    att_shape = jax.ShapeDtypeStruct((heads, rows, HEAD_DIM), jnp.bfloat16)
    att_block = pl.BlockSpec((hb, rows, HEAD_DIM), lambda i: (i, 0, 0))
    att, near, squares, near_squares = pl.pallas_call(
        lambda *refs: values_kernel(hb, *refs),
        grid=(heads // hb,),
        out_shape=(att_shape, att_shape, stats, stats),
        in_specs=[smem, own_spec(hb), prev_spec(hb), square, square] + [block] * 4,
        out_specs=(att_block, att_block, square, square),
        compiler_params=params(),
        cost_estimate=pl.CostEstimate(flops=5 * tile_flops, bytes_accessed=11 * wide_bytes, transcendentals=0),
        name="values",
    )(facts, own, prev, tops, stat_across, b_across, value_far, value_near, value_rows)

    mirrored = jnp.roll(filters[:, ::-1], 1, axis=1).astype(jnp.float32)
    ab = 8
    a_steps = heads // ab
    bt = 4
    b_steps = width // (bt * LANES)
    per_tile = groups // (width // LANES)
    clamp_a = lambda i: jnp.minimum(i, a_steps - 1)
    clamp_b = lambda i: jnp.maximum(i - a_steps, 0)
    early = pl.BlockSpec((rows, ab * HEAD_DIM), lambda i: (0, clamp_a(i)))
    lane = pl.BlockSpec((1, bt * LANES), lambda i: (0, clamp_b(i)))
    return pl.pallas_call(
        lambda *refs: finish_kernel(ab, a_steps, *refs),
        grid=(a_steps + b_steps,),
        out_shape=wide,
        in_specs=[
            smem,
            starts,
            early,
            early,
            early,
            pl.BlockSpec((ab, rows, HEAD_DIM), lambda i: (clamp_a(i), 0, 0)),
            square,
            square,
            pl.BlockSpec((bt, rows, HEAD_DIM), lambda i: (clamp_b(i), 0, 0)),
            pl.BlockSpec((bt * per_tile, taps), lambda i: (clamp_b(i), 0)),
            lane,
            lane,
        ],
        out_specs=pl.BlockSpec((rows, bt * LANES), lambda i: (0, clamp_b(i))),
        scratch_shapes=[
            pltpu.VMEM((width // LANES, rows, LANES), jnp.bfloat16),
            pltpu.VMEM((rows, LANES), jnp.float32),
            pltpu.VMEM((2 * rows, LANES), jnp.float32),
            pltpu.VMEM((rows, 2 * rows), jnp.bfloat16),
            pltpu.VMEM((2, per_tile * rows, 2 * rows), jnp.bfloat16),
            pltpu.VMEM((rows, rows), jnp.float32),
        ],
        compiler_params=params(),
        cost_estimate=pl.CostEstimate(flops=4 * tile_flops, bytes_accessed=6 * wide_bytes, transcendentals=0),
        name="finish",
    )(
        facts,
        st,
        key_across,
        b_across,
        c_across,
        near,
        squares,
        near_squares,
        att,
        mirrored,
        norm_gain.reshape(1, width),
        bypass.reshape(1, width),
    )


def solution(mesh):
    rows = P(("dp", "ctx"), None)
    in_specs = (rows, rows, rows, P("dp"), P(), P(), P())
    return jax.shard_map(shards, mesh=mesh, in_specs=in_specs, out_specs=rows, check_vma=False)
```

time: 83.7 us -> 112 us (1.34)
  Pallas kernels: 18.4 us -> 33 us
  local copies, waits for them, and re-layouts: 3.72 us -> 18.1 us
  waiting for transfers between devices: 40.2 us -> 35.9 us
  between operations: 0.12 us -> 2.12 us
  starting transfers between devices: 18.1 us -> 19.5 us
    unnamed x10 -> x40, local copies, waits for them, and re-layouts: 2.46 us -> 17.1 us
    pallas_call x0 -> x2, Pallas kernels: none -> 9.37 us  [the longest x1 5.45 us: shards(): pl.pallas_call(lambda *refs: values_kernel(hb, *refs), grid=(heads // hb,...]
    pallas_call x1, Pallas kernels: 11.9 us -> 17.4 us  [shards(): pl.pallas_call(lambda *refs: finish_kernel(ab, a_steps, *refs), grid=(a_s...]
    ppermute x7 -> x10, waiting for transfers between devices: 40.2 us -> 35.9 us  [permuted(): return lax.ppermute(x, 'ctx', pairs)]
    ppermute x7 -> x10, starting transfers between devices: 18.1 us -> 19.5 us  [permuted(): return lax.ppermute(x, 'ctx', pairs)]
  transfers between devices with their start and end apart: 7 -> 10, of which waited for: 3 -> 4; matrix products, arithmetic and copies ran while one was open for 5% -> 3% of each run, Pallas kernels for 8% -> 14%
where the time goes in v2:
time: 112 us; the launch traced here: 111 us
  waiting for transfers between devices  35.9 us (32%)
  Pallas kernels  33 us (29%)
  starting transfers between devices  19.5 us (17%)
  local copies, waits for them, and re-layouts  18.1 us (16%)
  other arithmetic  2.59 us (2%)
  between operations  2.12 us (2%)
    ppermute x10, waiting for transfers between devices, permuted(): return lax.ppermute(x, 'ctx', pairs)  35.9 us
    ppermute x10, starting transfers between devices, permuted(): return lax.ppermute(x, 'ctx', pairs)  19.5 us
    pallas_call x1, Pallas kernels, shards(): pl.pallas_call(lambda *refs: finish_kernel(ab, a_steps, *refs), grid=(a_s...  17.4 us
    unnamed x40, local copies, waits for them, and re-layouts  17.1 us
    pallas_call x1, Pallas kernels, shards(): pl.pallas_call(lambda *refs: weights_kernel(hb, *refs), grid=(heads // hb...  6.23 us
    pallas_call x1, Pallas kernels, shards(): pl.pallas_call(lambda *refs: values_kernel(hb, *refs), grid=(heads // hb,...  5.45 us
    pallas_call x1, Pallas kernels, shards(): pl.pallas_call(lambda *refs: share_kernel(hb, *refs), grid=(heads // hb,)...  3.92 us
  transfers between devices with their start and end apart: 10, of which 4 were waited for; matrix products, arithmetic and copies ran while one was open for 3% of the time, Pallas kernels for 14%

profile of v2, /device:TPU:28, one launch (start us, length us, event | category | flops | bytes accessed | tf_op | source)
XLA Modules:
  0.0 111.2 jit_solution(17921276120074185936)
XLA Ops:
  0.0 2.8 %collective-permute-start = (bf16[128,4096]{1,0:T(8,128)(2,1)}, bf16[128,4096]{1,0:T(8,128)(2,1)S(1)}, u32[]{:S(2)}, u32[]{:S(2)}) collective-permute-start(bf16[128,4096]{1,0:T(8,128)(2,1)} %refs_2_.3), channel_id=1, source_target_pairs={{4,2},{8,6},{12,10},{16,14},{20,18},{24,22},{28,26},{5,3},{9,7},{1... | collective-permute-start | bytes 3145736 | tf_op jit(solution)/shard_map/ppermute | solution.py:21
  2.8 12.5 %collective-permute-done.refs_1_ = bf16[128,4096]{1,0:T(8,128)(2,1)S(1)} collective-permute-done((bf16[128,4096]{1,0:T(8,128)(2,1)}, bf16[128,4096]{1,0:T(8,128)(2,1)S(1)}, u32[]{:S(2)}, u32[]{:S(2)}) %collective-permute-start) | collective-permute-done | bytes 1048608 | tf_op jit(solution)/shard_map/ppermute | solution.py:21
  16.3 1.3 %collective-permute-start.1 = (bf16[128,4096]{1,0:T(8,128)(2,1)}, bf16[128,4096]{1,0:T(8,128)(2,1)}, u32[]{:S(2)}, u32[]{:S(2)}) collective-permute-start(bf16[128,4096]{1,0:T(8,128)(2,1)} %refs_3_.1), channel_id=1, source_target_pairs={{2,4},{6,8},{10,12},{14,16},{18,20},{22,24},{26,28},{3,5},{7,9},{1... | collective-permute-start | bytes 3145736 | tf_op jit(solution)/shard_map/ppermute | solution.py:21
  17.6 4.3 %collective-permute-start.2 = (bf16[128,4096]{1,0:T(8,128)(2,1)}, bf16[128,4096]{1,0:T(8,128)(2,1)S(1)}, u32[]{:S(2)}, u32[]{:S(2)}) collective-permute-start(bf16[128,4096]{1,0:T(8,128)(2,1)} %refs_3_.1), channel_id=1, source_target_pairs={{0,2},{4,6},{8,10},{12,14},{16,18},{20,22},{24,26},{28,30},{1,3},{... | collective-permute-start | bytes 3145736 | tf_op jit(solution)/shard_map/ppermute | solution.py:21
  21.9 1.4 %collective-permute-start.3 = (bf16[128,4096]{1,0:T(8,128)(2,1)}, bf16[128,4096]{1,0:T(8,128)(2,1)S(1)}, u32[]{:S(2)}, u32[]{:S(2)}) collective-permute-start(bf16[128,4096]{1,0:T(8,128)(2,1)} %refs_8_.1), channel_id=1, source_target_pairs={{0,2},{4,6},{8,10},{12,14},{16,18},{20,22},{24,26},{28,30},{1,3},{... | collective-permute-start | bytes 3145736 | tf_op jit(solution)/shard_map/ppermute | solution.py:21
  23.3 2.3 %collective-permute-start.7 = (bf16[128,4096]{1,0:T(8,128)(2,1)}, bf16[128,4096]{1,0:T(8,128)(2,1)}, u32[]{:S(2)}, u32[]{:S(2)}) collective-permute-start(bf16[128,4096]{1,0:T(8,128)(2,1)} %refs_2_.3), channel_id=1, source_target_pairs={{0,2},{4,6},{8,10},{12,14},{16,18},{20,22},{24,26},{28,30},{1,3},{... | collective-permute-start | bytes 3145736 | tf_op jit(solution)/shard_map/ppermute | solution.py:21
  30.5 3.1 %collective-permute-done.1.refs_4_.refs_2_ = bf16[128,4096]{1,0:T(8,128)(2,1)} collective-permute-done((bf16[128,4096]{1,0:T(8,128)(2,1)}, bf16[128,4096]{1,0:T(8,128)(2,1)}, u32[]{:S(2)}, u32[]{:S(2)}) %collective-permute-start.1) | collective-permute-done | bytes 1048608 | tf_op jit(solution)/shard_map/ppermute | solution.py:21
  33.6 2.3 %collective-permute-start.6 = (bf16[128,4096]{1,0:T(8,128)(2,1)}, bf16[128,4096]{1,0:T(8,128)(2,1)}, u32[]{:S(2)}, u32[]{:S(2)}) collective-permute-start(bf16[128,4096]{1,0:T(8,128)(2,1)} %collective-permute-done.1.refs_4_.refs_2_), channel_id=1, source_target_pairs={{0,2},{4,6},{8,10},{12,14},{16,18},{20,22},{24,26},{28,30},{1,3},{... | collective-permute-start | bytes 3145736 | tf_op jit(solution)/shard_map/ppermute | solution.py:21
  37.0 1.2 %copy-done = bf16[128,4096]{1,0:T(8,128)(2,1)S(1)} copy-done((bf16[128,4096]{1,0:T(8,128)(2,1)S(1)}, bf16[128,4096]{1,0:T(8,128)(2,1)}, u32[]{:S(2)}) %copy-start) | copy-done | bytes 1048600
  43.1 3.9 %share.1 = (bf16[128,4096]{1,0:T(8,128)(2,1)}, f32[128,128]{1,0:T(8,128)S(1)}, bf16[128,4096]{1,0:T(8,128)(2,1)}) custom-call(s32[4]{0:T(128)S(1)} %pad_add_fusion.refs_0_, bf16[128,4096]{1,0:T(8,128)(2,1)S(1)} %copy-done.16, bf16[128,4096]{1,0:T(8,128)(2,1)S(1)} %copy-done.2, bf16[128,4096]{1,0:T(8,128)(2,1)S(1)} %copy-done.9, ...), custom_call_target="tpu_custom_call" | custom-call | flops 1073741824 | bytes 8388608 | tf_op jit(solution)/shard_map/share/pallas_call | solution.py:278
  47.0 1.3 %collective-permute-start.4 = (bf16[128,4096]{1,0:T(8,128)(2,1)}, bf16[128,4096]{1,0:T(8,128)(2,1)}, u32[]{:S(2)}, u32[]{:S(2)}) collective-permute-start(bf16[128,4096]{1,0:T(8,128)(2,1)} %get-tuple-element.19), channel_id=1, source_target_pairs={{2,4},{6,8},{10,12},{14,16},{18,20},{22,24},{26,28},{3,5},{7,9},{1... | collective-permute-start | bytes 3145736 | tf_op jit(solution)/shard_map/ppermute | solution.py:21
  48.5 1.3 %copy-done.10 = bf16[128,4096]{1,0:T(8,128)(2,1)S(1)} copy-done((bf16[128,4096]{1,0:T(8,128)(2,1)S(1)}, bf16[128,4096]{1,0:T(8,128)(2,1)}, u32[]{:S(2)}) %copy-start.10) | copy-done | bytes 1048600
  49.8 6.2 %weights.1 = (bf16[32,128,384]{2,1,0:T(8,128)(2,1)S(1)}, bf16[32,128,256]{2,1,0:T(8,128)(2,1)S(1)}, f32[128,128]{1,0:T(8,128)S(1)}) custom-call(s32[4]{0:T(128)S(1)} %pad_add_fusion.refs_0_, s32[128,1]{1,0:T(8,128)S(1)} %copy.9.refs_1_, bf16[128,4096]{1,0:T(8,128)(2,1)S(1)} %copy-done.3, bf16[128,4096]{1,0:T(8,128)(2,1)S(1)} %copy-done.1, ...), custom_call_target="tpu_custom_call" | custom-call | flops 1342177280 | bytes 11534336 | tf_op jit(solution)/shard_map/weights/pallas_call | solution.py:297
  56.0 1.6 %copy-done.11 = bf16[32,128,384]{2,1,0:T(8,128)(2,1)} copy-done((bf16[32,128,384]{2,1,0:T(8,128)(2,1)}, bf16[32,128,384]{2,1,0:T(8,128)(2,1)S(1)}, u32[]{:S(2)}) %copy-start.11) | copy-done | bytes 3145752
  57.7 1.4 %copy-done.13 = bf16[32,128,256]{2,1,0:T(8,128)(2,1)} copy-done((bf16[32,128,256]{2,1,0:T(8,128)(2,1)}, bf16[32,128,256]{2,1,0:T(8,128)(2,1)S(1)}, u32[]{:S(2)}) %copy-start.13) | copy-done | bytes 2097176
  59.0 5.3 %collective-permute-done.4.refs_5_.refs_3_ = bf16[128,4096]{1,0:T(8,128)(2,1)} collective-permute-done((bf16[128,4096]{1,0:T(8,128)(2,1)}, bf16[128,4096]{1,0:T(8,128)(2,1)}, u32[]{:S(2)}, u32[]{:S(2)}) %collective-permute-start.4) | collective-permute-done | bytes 1048608 | tf_op jit(solution)/shard_map/ppermute | solution.py:21
  64.3 1.3 %collective-permute-start.9 = (bf16[128,4096]{1,0:T(8,128)(2,1)}, bf16[128,4096]{1,0:T(8,128)(2,1)S(1)}, u32[]{:S(2)}, u32[]{:S(2)}) collective-permute-start(bf16[128,4096]{1,0:T(8,128)(2,1)} %collective-permute-done.4.refs_5_.refs_3_), channel_id=1, source_target_pairs={{0,2},{4,6},{8,10},{12,14},{16,18},{20,22},{24,26},{28,30},{1,3},{... | collective-permute-start | bytes 3145736 | tf_op jit(solution)/shard_map/ppermute | solution.py:21
  65.7 1.3 %collective-permute-start.5 = (bf16[128,4096]{1,0:T(8,128)(2,1)}, bf16[128,4096]{1,0:T(8,128)(2,1)S(1)}, u32[]{:S(2)}, u32[]{:S(2)}) collective-permute-start(bf16[128,4096]{1,0:T(8,128)(2,1)} %get-tuple-element.21), channel_id=1, source_target_pairs={{2,4},{6,8},{10,12},{14,16},{18,20},{22,24},{26,28},{3,5},{7,9},{1... | collective-permute-start | bytes 3145736 | tf_op jit(solution)/shard_map/ppermute | solution.py:21
  67.3 1.3 %collective-permute-start.8 = (f32[128,128]{1,0:T(8,128)S(1)}, f32[128,128]{1,0:T(8,128)S(1)}, u32[]{:S(2)}, u32[]{:S(2)}) collective-permute-start(f32[128,128]{1,0:T(8,128)S(1)} %get-tuple-element.25), channel_id=1, source_target_pairs={{2,4},{6,8},{10,12},{14,16},{18,20},{22,24},{26,28},{3,5},{7,9},{1... | collective-permute-start | bytes 196616 | tf_op jit(solution)/shard_map/ppermute | solution.py:21
  68.7 14.9 %collective-permute-done.8.refs_4_ = f32[128,128]{1,0:T(8,128)S(1)} collective-permute-done((f32[128,128]{1,0:T(8,128)S(1)}, f32[128,128]{1,0:T(8,128)S(1)}, u32[]{:S(2)}, u32[]{:S(2)}) %collective-permute-start.8) | collective-permute-done | bytes 65568 | tf_op jit(solution)/shard_map/ppermute | solution.py:21
  84.9 1.9 %copy-done.12 = bf16[32,128,384]{2,1,0:T(8,128)(2,1)S(1)} copy-done((bf16[32,128,384]{2,1,0:T(8,128)(2,1)S(1)}, bf16[32,128,384]{2,1,0:T(8,128)(2,1)}, u32[]{:S(2)}) %copy-start.12) | copy-done | bytes 3145752
  86.7 1.6 %copy-done.14 = bf16[32,128,256]{2,1,0:T(8,128)(2,1)S(1)} copy-done((bf16[32,128,256]{2,1,0:T(8,128)(2,1)S(1)}, bf16[32,128,256]{2,1,0:T(8,128)(2,1)}, u32[]{:S(2)}) %copy-start.14) | copy-done | bytes 2097176
  88.3 5.5 %values.1 = (bf16[32,128,128]{2,1,0:T(8,128)(2,1)S(1)}, bf16[32,128,128]{2,1,0:T(8,128)(2,1)S(1)}, f32[128,128]{1,0:T(8,128)S(1)}, f32[128,128]{1,0:T(8,128)S(1)}) custom-call(s32[4]{0:T(128)S(1)} %pad_add_fusion.refs_0_, bf16[32,128,384]{2,1,0:T(8,128)(2,1)S(1)} %copy-done.12, bf16[32,128,256]{2,1,0:T(8,128)(2,1)S(1)} %copy-done.14, ...), custom_call_target="tpu_custom_call" | custom-call | flops 1342177280 | bytes 11534336 | tf_op jit(solution)/shard_map/values/pallas_call | solution.py:317
  93.8 17.4 %finish.1 = bf16[128,4096]{1,0:T(8,128)(2,1)} custom-call(s32[4]{0:T(128)S(1)} %pad_add_fusion.refs_0_, s32[128,1]{1,0:T(8,128)S(1)} %copy.9.refs_1_, bf16[128,4096]{1,0:T(8,128)(2,1)} %collective-permute-done.1.refs_4_.refs_2_, bf16[128,4096]{1,0:T(8,128)(2,1)} %collective-permute-done.4.refs_5_.refs_3_, ...), custom_call_target="tpu_custom_call" | custom-call | flops 1073741824 | bytes 6291456 | tf_op jit(solution)/shard_map/finish/pallas_call | solution.py:338
  (53 shorter events, 11.7 us)
Async XLA Ops:
  0.0 15.3 %collective-permute-start = (bf16[128,4096]{1,0:T(8,128)(2,1)}, bf16[128,4096]{1,0:T(8,128)(2,1)S(1)}, u32[]{:S(2)}, u32[]{:S(2)}) collective-permute-start(bf16[128,4096]{1,0:T(8,128)(2,1)} %refs_2_.3), channel_id=1, source_target_pairs={{4,2},{8,6},{12,10},{16,14},{20,18},{24,22},{28,26},{5,3},{9,7},{1... | collective-permute-start | bytes 3145736 | tf_op jit(solution)/shard_map/ppermute | solution.py:21
  16.3 17.3 %collective-permute-start.1 = (bf16[128,4096]{1,0:T(8,128)(2,1)}, bf16[128,4096]{1,0:T(8,128)(2,1)}, u32[]{:S(2)}, u32[]{:S(2)}) collective-permute-start(bf16[128,4096]{1,0:T(8,128)(2,1)} %refs_3_.1), channel_id=1, source_target_pairs={{2,4},{6,8},{10,12},{14,16},{18,20},{22,24},{26,28},{3,5},{7,9},{1... | collective-permute-start | bytes 3145736 | tf_op jit(solution)/shard_map/ppermute | solution.py:21
  17.6 18.4 %collective-permute-start.2 = (bf16[128,4096]{1,0:T(8,128)(2,1)}, bf16[128,4096]{1,0:T(8,128)(2,1)S(1)}, u32[]{:S(2)}, u32[]{:S(2)}) collective-permute-start(bf16[128,4096]{1,0:T(8,128)(2,1)} %refs_3_.1), channel_id=1, source_target_pairs={{0,2},{4,6},{8,10},{12,14},{16,18},{20,22},{24,26},{28,30},{1,3},{... | collective-permute-start | bytes 3145736 | tf_op jit(solution)/shard_map/ppermute | solution.py:21
  21.9 15.0 %collective-permute-start.3 = (bf16[128,4096]{1,0:T(8,128)(2,1)}, bf16[128,4096]{1,0:T(8,128)(2,1)S(1)}, u32[]{:S(2)}, u32[]{:S(2)}) collective-permute-start(bf16[128,4096]{1,0:T(8,128)(2,1)} %refs_8_.1), channel_id=1, source_target_pairs={{0,2},{4,6},{8,10},{12,14},{16,18},{20,22},{24,26},{28,30},{1,3},{... | collective-permute-start | bytes 3145736 | tf_op jit(solution)/shard_map/ppermute | solution.py:21
  23.3 25.2 %collective-permute-start.7 = (bf16[128,4096]{1,0:T(8,128)(2,1)}, bf16[128,4096]{1,0:T(8,128)(2,1)}, u32[]{:S(2)}, u32[]{:S(2)}) collective-permute-start(bf16[128,4096]{1,0:T(8,128)(2,1)} %refs_2_.3), channel_id=1, source_target_pairs={{0,2},{4,6},{8,10},{12,14},{16,18},{20,22},{24,26},{28,30},{1,3},{... | collective-permute-start | bytes 3145736 | tf_op jit(solution)/shard_map/ppermute | solution.py:21
  33.6 14.8 %collective-permute-start.6 = (bf16[128,4096]{1,0:T(8,128)(2,1)}, bf16[128,4096]{1,0:T(8,128)(2,1)}, u32[]{:S(2)}, u32[]{:S(2)}) collective-permute-start(bf16[128,4096]{1,0:T(8,128)(2,1)} %collective-permute-done.1.refs_4_.refs_2_), channel_id=1, source_target_pairs={{0,2},{4,6},{8,10},{12,14},{16,18},{20,22},{24,26},{28,30},{1,3},{... | collective-permute-start | bytes 3145736 | tf_op jit(solution)/shard_map/ppermute | solution.py:21
  37.0 1.2 %copy-start = (bf16[128,4096]{1,0:T(8,128)(2,1)S(1)}, bf16[128,4096]{1,0:T(8,128)(2,1)}, u32[]{:S(2)}) copy-start(bf16[128,4096]{1,0:T(8,128)(2,1)} %refs_3_.1) | copy-start | bytes 3145732
  43.1 3.9 %copy-start.6 = (bf16[128,4096]{1,0:T(8,128)(2,1)}, bf16[128,4096]{1,0:T(8,128)(2,1)S(1)}, u32[]{:S(2)}) copy-start(bf16[128,4096]{1,0:T(8,128)(2,1)S(1)} %collective-permute-done.3.refs_5_.refs_7_) | copy-start | bytes 3145732
  43.1 5.4 %copy-start.1 = (bf16[128,4096]{1,0:T(8,128)(2,1)S(1)}, bf16[128,4096]{1,0:T(8,128)(2,1)}, u32[]{:S(2)}) copy-start(bf16[128,4096]{1,0:T(8,128)(2,1)} %refs_3_.1) | copy-start | bytes 3145732
  43.1 5.4 %copy-start.3 = (bf16[128,4096]{1,0:T(8,128)(2,1)S(1)}, bf16[128,4096]{1,0:T(8,128)(2,1)}, u32[]{:S(2)}) copy-start(bf16[128,4096]{1,0:T(8,128)(2,1)} %refs_2_.3) | copy-start | bytes 3145732
  47.0 17.3 %collective-permute-start.4 = (bf16[128,4096]{1,0:T(8,128)(2,1)}, bf16[128,4096]{1,0:T(8,128)(2,1)}, u32[]{:S(2)}, u32[]{:S(2)}) collective-permute-start(bf16[128,4096]{1,0:T(8,128)(2,1)} %get-tuple-element.19), channel_id=1, source_target_pairs={{2,4},{6,8},{10,12},{14,16},{18,20},{22,24},{26,28},{3,5},{7,9},{1... | collective-permute-start | bytes 3145736 | tf_op jit(solution)/shard_map/ppermute | solution.py:21
  48.3 18.7 %copy-start.19 = (bf16[256,128]{1,0:T(8,128)(2,1)S(1)}, bf16[256,128]{1,0:T(8,128)(2,1)}, u32[]{:S(2)}) copy-start(bf16[256,128]{1,0:T(8,128)(2,1)} %param.12) | copy-start | bytes 196612
  48.4 35.2 %copy-start.5 = (bf16[128,4096]{1,0:T(8,128)(2,1)S(1)}, bf16[128,4096]{1,0:T(8,128)(2,1)}, u32[]{:S(2)}) copy-start(bf16[128,4096]{1,0:T(8,128)(2,1)} %refs_8_.1) | copy-start | bytes 3145732
  48.5 1.3 %copy-start.10 = (bf16[128,4096]{1,0:T(8,128)(2,1)S(1)}, bf16[128,4096]{1,0:T(8,128)(2,1)}, u32[]{:S(2)}) copy-start(bf16[128,4096]{1,0:T(8,128)(2,1)} %copy-done.8) | copy-start | bytes 3145732
  56.0 1.6 %copy-start.11 = (bf16[32,128,384]{2,1,0:T(8,128)(2,1)}, bf16[32,128,384]{2,1,0:T(8,128)(2,1)S(1)}, u32[]{:S(2)}) copy-start(bf16[32,128,384]{2,1,0:T(8,128)(2,1)S(1)} %get-tuple-element.22.refs_1_) | copy-start | bytes 9437188
  57.7 1.4 %copy-start.13 = (bf16[32,128,256]{2,1,0:T(8,128)(2,1)}, bf16[32,128,256]{2,1,0:T(8,128)(2,1)S(1)}, u32[]{:S(2)}) copy-start(bf16[32,128,256]{2,1,0:T(8,128)(2,1)S(1)} %get-tuple-element.23.refs_2_) | copy-start | bytes 6291460
  64.3 19.3 %collective-permute-start.9 = (bf16[128,4096]{1,0:T(8,128)(2,1)}, bf16[128,4096]{1,0:T(8,128)(2,1)S(1)}, u32[]{:S(2)}, u32[]{:S(2)}) collective-permute-start(bf16[128,4096]{1,0:T(8,128)(2,1)} %collective-permute-done.4.refs_5_.refs_3_), channel_id=1, source_target_pairs={{0,2},{4,6},{8,10},{12,14},{16,18},{20,22},{24,26},{28,30},{1,3},{... | collective-permute-start | bytes 3145736 | tf_op jit(solution)/shard_map/ppermute | solution.py:21
  65.7 28.1 %collective-permute-start.5 = (bf16[128,4096]{1,0:T(8,128)(2,1)}, bf16[128,4096]{1,0:T(8,128)(2,1)S(1)}, u32[]{:S(2)}, u32[]{:S(2)}) collective-permute-start(bf16[128,4096]{1,0:T(8,128)(2,1)} %get-tuple-element.21), channel_id=1, source_target_pairs={{2,4},{6,8},{10,12},{14,16},{18,20},{22,24},{26,28},{3,5},{7,9},{1... | collective-permute-start | bytes 3145736 | tf_op jit(solution)/shard_map/ppermute | solution.py:21
  67.3 16.3 %collective-permute-start.8 = (f32[128,128]{1,0:T(8,128)S(1)}, f32[128,128]{1,0:T(8,128)S(1)}, u32[]{:S(2)}, u32[]{:S(2)}) collective-permute-start(f32[128,128]{1,0:T(8,128)S(1)} %get-tuple-element.25), channel_id=1, source_target_pairs={{2,4},{6,8},{10,12},{14,16},{18,20},{22,24},{26,28},{3,5},{7,9},{1... | collective-permute-start | bytes 196616 | tf_op jit(solution)/shard_map/ppermute | solution.py:21
  83.6 1.2 %copy-start.7 = (bf16[128,4096]{1,0:T(8,128)(2,1)S(1)}, bf16[128,4096]{1,0:T(8,128)(2,1)}, u32[]{:S(2)}) copy-start(bf16[128,4096]{1,0:T(8,128)(2,1)} %copy-done.6) | copy-start | bytes 3145732
  84.9 1.9 %copy-start.12 = (bf16[32,128,384]{2,1,0:T(8,128)(2,1)S(1)}, bf16[32,128,384]{2,1,0:T(8,128)(2,1)}, u32[]{:S(2)}) copy-start(bf16[32,128,384]{2,1,0:T(8,128)(2,1)} %copy-done.11) | copy-start | bytes 9437188
  86.7 1.6 %copy-start.14 = (bf16[32,128,256]{2,1,0:T(8,128)(2,1)S(1)}, bf16[32,128,256]{2,1,0:T(8,128)(2,1)}, u32[]{:S(2)}) copy-start(bf16[32,128,256]{2,1,0:T(8,128)(2,1)} %copy-done.13) | copy-start | bytes 6291460
  88.3 5.5 %copy-start.17 = (f32[4096]{0:T(1024)S(1)}, f32[4096]{0:T(1024)}, u32[]{:S(2)}) copy-start(f32[4096]{0:T(1024)} %param.11) | copy-start | bytes 49156
  88.3 5.5 %copy-start.18 = (f32[4096]{0:T(1024)S(1)}, f32[4096]{0:T(1024)}, u32[]{:S(2)}) copy-start(f32[4096]{0:T(1024)} %param.13) | copy-start | bytes 49156
  (6 other events, 6.9 us)

commit v3 on v2

v3 whole, which is shorter than its diff:
```python
import math

import jax
import jax.numpy as jnp
from jax import lax
from jax.experimental import pallas as pl
from jax.experimental.pallas import tpu as pltpu
from jax.sharding import PartitionSpec as P

HEAD_DIM = 128
LANES = 128
NEG = -1e30
FACTOR = 1.0 / math.sqrt(HEAD_DIM) * math.log2(math.e)
CONTRACT_LAST = (((1,), (1,)), ((), ()))
VMEM_BYTES = 20 * 2**20

ODD, BEFORE, NEXT_BEFORE, NEXT_AFTER = range(4)


def permuted(x, pairs):
    return lax.ppermute(x, "ctx", pairs)


def after(x, *others):
    return lax.optimization_barrier((x, *others))[0]


def places(lengths, first_row, count):
    ends = jnp.cumsum(lengths)
    position = first_row + jnp.arange(count + 1, dtype=jnp.int32)
    passed = ends[None, :] <= position[:, None]
    starts = jnp.sum(jnp.where(passed, lengths[None, :], 0), axis=1) - first_row
    past = jnp.min(jnp.where(passed[count], jnp.int32(2**30), ends)) - first_row - count
    odd = (first_row // count) % 2
    facts = jnp.stack([odd, -starts[0], count - starts[count], past]).astype(jnp.int32)
    return starts[:count].astype(jnp.int32).reshape(count, 1), facts


def bias_of(rows, columns, row_first, key_first, start):
    row = lax.broadcasted_iota(jnp.int32, (rows, columns), 0) + row_first
    key = lax.broadcasted_iota(jnp.int32, (rows, columns), 1) + key_first
    return jnp.where((key >= start) & (key <= row), 0.0, NEG)


def scores_of(query, key):
    return lax.dot_general(query, key, CONTRACT_LAST, preferred_element_type=jnp.float32)


def raised(scores, bias):
    s = scores + bias
    top = jnp.max(s, axis=1, keepdims=True)
    return jnp.exp2((s - top) * FACTOR).astype(jnp.bfloat16), top


def summed(weights, value):
    ones = jnp.ones(value.shape, jnp.bfloat16)
    o = jnp.dot(weights, jnp.concatenate([value, ones], axis=1), preferred_element_type=jnp.float32)
    return o[:, :LANES], o[:, LANES:]


def columns(head):
    return slice(head * HEAD_DIM, (head + 1) * HEAD_DIM)


def attend(heads, query, key, value, bias, use):
    ahead = scores_of(query(0), key(0))
    held = None
    for h in range(heads):
        now = ahead
        if h + 1 < heads:
            ahead = scores_of(query(h + 1), key(h + 1))
        weights, top = raised(now, bias)
        if held is not None:
            use(h - 1, *summed(held[0], value(h - 1)), held[1])
        held = weights, top
    use(heads - 1, *summed(held[0], value(heads - 1)), held[1])


def taps_kernel(facts_ref, st_ref, filters_ref, far_ref, near_ref, keep):
    rows = st_ref.shape[0]

    @pl.when(pl.program_id(0) == 0)
    def _():
        st = st_ref[...]
        row = lax.broadcasted_iota(jnp.int32, (rows, 2 * rows), 0)
        key = lax.broadcasted_iota(jnp.int32, (rows, 2 * rows), 1) - rows
        keep[...] = jnp.where((key >= st) & (key <= row) & (key > row - rows), 1.0, 0.0).astype(jnp.bfloat16)

    tap = lax.broadcasted_iota(jnp.int32, (rows, rows), 0)
    place = lax.broadcasted_iota(jnp.int32, (rows, rows), 1)
    turn = jnp.where((tap + place == 0) | (tap + place == rows), 1.0, 0.0).astype(jnp.bfloat16)
    lines = jnp.dot(filters_ref[...], turn, preferred_element_type=jnp.float32)
    tiles = far_ref.shape[0]
    groups = filters_ref.shape[0] // tiles
    for c in range(tiles):
        for g in range(groups):
            line = jnp.broadcast_to(lines[c * groups + g : c * groups + g + 1], (rows, rows))
            ring = pltpu.roll(line, 0, 1, stride=1, stride_axis=0).astype(jnp.bfloat16)
            cols = slice(g * rows, (g + 1) * rows)
            far_ref[c, :, cols] = ring * keep[:, :rows]
            near_ref[c, :, cols] = ring * keep[:, rows:]


def share_kernel(heads, facts_ref, qb_ref, q_ref, kn_ref, ko_ref, vn_ref, vo_ref, b_ref, stat_ref, c_ref, bias):
    rows = q_ref.shape[0]
    step = pl.program_id(0)
    before = facts_ref[NEXT_BEFORE]
    past = facts_ref[NEXT_AFTER]
    odd = facts_ref[ODD] == 1

    @pl.when(odd & (before <= rows))
    def _():
        b_ref[...] = vo_ref[...]
        c_ref[...] = q_ref[...]

    @pl.when(odd & (before > rows))
    def _():
        @pl.when(step == 0)
        def _():
            bias[:rows] = bias_of(rows, 2 * rows, rows, -rows, rows - before)
            bias[rows:] = bias_of(rows, 2 * rows, 0, -rows, rows - before)

        lane = lax.broadcasted_iota(jnp.int32, (rows, LANES), 1)
        ours = lax.broadcasted_iota(jnp.int32, (rows, LANES), 0) < past
        stat = [stat_ref[...]]

        def use(h, o, l, top):
            o = (o / l).astype(jnp.bfloat16)
            b_ref[:, columns(h)] = o[:rows]
            c_ref[:, columns(h)] = o[rows:]
            lse = jnp.where(ours, top[:rows] * FACTOR + jnp.log2(l[:rows]), NEG)
            stat[0] = jnp.where(lane == step * heads + h, lse, stat[0])

        attend(
            heads,
            lambda h: jnp.concatenate([qb_ref[:, columns(h)], q_ref[:, columns(h)]], axis=0),
            lambda h: jnp.concatenate([kn_ref[:, columns(h)], ko_ref[:, columns(h)]], axis=0),
            lambda h: jnp.concatenate([vn_ref[:, columns(h)], vo_ref[:, columns(h)]], axis=0),
            bias[...],
            use,
        )
        stat_ref[...] = stat[0]


def weights_kernel(heads, facts_ref, st_ref, q_ref, ko_ref, kp_ref, kf_ref, kn_ref, qn_ref, three_ref, two_ref, top_ref, bias_own, bias_prev):
    rows = q_ref.shape[0]
    step = pl.program_id(0)
    odd = facts_ref[ODD] == 1

    @pl.when(step == 0)
    def _():
        low = jnp.where((facts_ref[ODD] == 0) & (facts_ref[BEFORE] > rows), 0, -(2**20))
        st = jnp.maximum(st_ref[...], low)
        bias_own[...] = bias_of(rows, 3 * rows, 0, -2 * rows, st)
        bias_prev[...] = bias_of(rows, 2 * rows, -rows, -2 * rows, st_ref[0:1, :])

    @pl.when(odd)
    def _():
        def scores(h):
            key = jnp.concatenate([kf_ref[:, columns(h)], kn_ref[:, columns(h)], ko_ref[:, columns(h)]], axis=0)
            return scores_of(q_ref[:, columns(h)], key), scores_of(qn_ref[:, columns(h)], key[: 2 * rows])

        ahead = scores(0)
        for h in range(heads):
            now = ahead
            if h + 1 < heads:
                ahead = scores(h + 1)
            three_ref[h] = raised(now[0], bias_own[...])[0]
            two_ref[h] = raised(now[1], bias_prev[...])[0]

    @pl.when(jnp.logical_not(odd))
    def _():
        lane = lax.broadcasted_iota(jnp.int32, (rows, LANES), 1)
        tops = top_ref[...]

        def scores(h):
            key = jnp.concatenate([kp_ref[:, columns(h)], ko_ref[:, columns(h)]], axis=0)
            return scores_of(q_ref[:, columns(h)], key)

        ahead = scores(0)
        for h in range(heads):
            now = ahead
            if h + 1 < heads:
                ahead = scores(h + 1)
            weights, top = raised(now, bias_own[:, rows:])
            two_ref[h] = weights
            tops = jnp.where(lane == step * heads + h, top * FACTOR, tops)
        top_ref[...] = tops


def values_kernel(heads, facts_ref, three_ref, two_ref, top_ref, stat_ref, vp_ref, vf_ref, vn_ref, vo_ref, att_ref, near_ref, sq_ref, sq_near_ref):
    rows = vo_ref.shape[0]
    step = pl.program_id(0)
    odd = facts_ref[ODD] == 1

    @pl.when(step == 0)
    def _():
        sq_ref[...] = jnp.zeros_like(sq_ref)
        sq_near_ref[...] = jnp.zeros_like(sq_near_ref)

    @pl.when(odd)
    def _():
        squares = sq_ref[...]
        squares_near = sq_near_ref[...]
        for h in range(heads):
            value = jnp.concatenate([vf_ref[:, columns(h)], vn_ref[:, columns(h)], vo_ref[:, columns(h)]], axis=0)
            o, l = summed(three_ref[h], value)
            a = (o / l).astype(jnp.bfloat16)
            att_ref[h] = a
            a = a.astype(jnp.float32)
            squares += a * a
            o, l = summed(two_ref[h], value[: 2 * rows])
            a = (o / l).astype(jnp.bfloat16)
            near_ref[h] = a
            a = a.astype(jnp.float32)
            squares_near += a * a
        sq_ref[...] = squares
        sq_near_ref[...] = squares_near

    @pl.when(jnp.logical_not(odd))
    def _():
        lane = lax.broadcasted_iota(jnp.int32, (rows, LANES), 1)
        shared = facts_ref[BEFORE] > rows
        stat = jnp.where(shared, stat_ref[...], NEG)
        tops = top_ref[...]
        squares = sq_ref[...]
        high = jnp.maximum(tops, stat)
        here_all = jnp.exp2(tops - high)
        there_all = jnp.exp2(stat - high)
        for h in range(heads):
            value = jnp.concatenate([vp_ref[:, columns(h)], vo_ref[:, columns(h)]], axis=0)
            o, l = summed(two_ref[h], value)
            mine = lane == step * heads + h
            here = jnp.sum(jnp.where(mine, here_all, 0.0), axis=1, keepdims=True)
            there = jnp.sum(jnp.where(mine, there_all, 0.0), axis=1, keepdims=True)
            o = o * here + vp_ref[:, columns(h)].astype(jnp.float32) * there
            a = (o / (l * here + there)).astype(jnp.bfloat16)
            att_ref[h] = a
            a = a.astype(jnp.float32)
            squares += a * a
        sq_ref[...] = squares


def scale_of(squares, width):
    total = jnp.sum(squares, axis=1, keepdims=True)
    return jnp.broadcast_to(lax.rsqrt(total * (1.0 / width) + 1e-06), squares.shape)


def spread(x, groups):
    size = LANES // groups
    lane_group = lax.broadcasted_iota(jnp.int32, x.shape, 1) // size
    return jnp.concatenate([jnp.where(lane_group == g, x, jnp.zeros_like(x)) for g in range(groups)], axis=0)


def own_kernel(width, facts_ref, att_ref, sq_ref, taps_ref, gain_ref, bypass_ref, out_ref, scale):
    tiles, rows, _ = att_ref.shape

    @pl.when(pl.program_id(0) == 0)
    def _():
        scale[...] = scale_of(sq_ref[...], width)

    for c in range(tiles):
        cols = columns(c)
        x = (att_ref[c].astype(jnp.float32) * scale[...] * gain_ref[:, cols]).astype(jnp.bfloat16)
        y = jnp.dot(taps_ref[c], spread(x, taps_ref.shape[2] // rows), preferred_element_type=jnp.float32)
        out_ref[:, cols] = y + bypass_ref[:, cols] * x.astype(jnp.float32)


def finish_kernel(heads, a_steps, facts_ref, st_ref, kp_ref, vp_ref, c_ref, near_ref, sq_near_ref, part_ref, taps_ref, gain_ref, out_ref, prev, squares, scale, bias):
    rows = st_ref.shape[0]
    step = pl.program_id(0)
    width = prev.shape[0] * LANES
    odd = facts_ref[ODD] == 1
    shared = facts_ref[BEFORE] > rows

    @pl.when(step == 0)
    def _():
        squares[...] = jnp.where(odd, sq_near_ref[...], 0.0)
        bias[...] = bias_of(rows, rows, -rows, -rows, st_ref[0:1, :])

    @pl.when((step < a_steps) & odd)
    def _():
        for h in range(heads):
            prev[step * heads + h] = near_ref[h]

    @pl.when((step < a_steps) & jnp.logical_not(odd) & shared)
    def _():
        total = squares[...]
        for h in range(heads):
            a = c_ref[:, columns(h)]
            prev[step * heads + h] = a
            a = a.astype(jnp.float32)
            total += a * a
        squares[...] = total

    @pl.when((step < a_steps) & jnp.logical_not(odd) & jnp.logical_not(shared))
    def _():
        total = [squares[...]]

        def use(h, o, l, top):
            a = (o / l).astype(jnp.bfloat16)
            prev[step * heads + h] = a
            a = a.astype(jnp.float32)
            total[0] += a * a

        attend(heads, lambda h: c_ref[:, columns(h)], lambda h: kp_ref[:, columns(h)], lambda h: vp_ref[:, columns(h)], bias[...], use)
        squares[...] = total[0]

    @pl.when(step == a_steps)
    def _():
        scale[...] = scale_of(squares[...], width)

    @pl.when(step >= a_steps)
    def _():
        tiles = taps_ref.shape[0]
        first = (step - a_steps) * tiles
        for c in range(tiles):
            cols = columns(c)
            x = (prev[first + c].astype(jnp.float32) * scale[...] * gain_ref[:, cols]).astype(jnp.bfloat16)
            y = jnp.dot(taps_ref[c], spread(x, taps_ref.shape[2] // rows), preferred_element_type=jnp.float32)
            out_ref[:, cols] = (y + part_ref[:, cols]).astype(jnp.bfloat16)


def run(kernel, name, steps, facts, out_shape, in_specs, out_specs, scratch, args):
    return pl.pallas_call(
        kernel,
        out_shape=out_shape,
        grid_spec=pltpu.PrefetchScalarGridSpec(
            num_scalar_prefetch=1, grid=(steps,), in_specs=in_specs, out_specs=out_specs, scratch_shapes=scratch
        ),
        compiler_params=pltpu.CompilerParams(vmem_limit_bytes=VMEM_BYTES),
        cost_estimate=pl.CostEstimate(flops=2**20, bytes_accessed=2**16, transcendentals=0),
        name=name,
    )(facts, *args)


def shards(queries, key_rows, value_rows, lengths, norm_gain, filters, bypass):
    rows, width = queries.shape
    heads = width // HEAD_DIM
    groups, taps = filters.shape
    n = lax.axis_size("ctx")
    st, facts = places(lengths, lax.axis_index("ctx") * rows, rows)

    back = [(i, i - 1) for i in range(2, n, 2)]
    within = [(i, i + 1) for i in range(0, n - 1, 2)]
    across = [(i, i + 1) for i in range(1, n - 1, 2)]

    wide = jax.ShapeDtypeStruct((rows, width), jnp.bfloat16)
    stats = jax.ShapeDtypeStruct((rows, LANES), jnp.float32)
    always = lambda i, facts: i
    if_odd = lambda i, facts: jnp.where(facts[ODD] == 1, i, 0)
    if_even = lambda i, facts: jnp.where(facts[ODD] == 0, i, 0)
    whole = lambda shape: pl.BlockSpec(shape, lambda i, facts: (0,) * len(shape))
    starts = whole((rows, 1))
    square = whole((rows, LANES))

    def strip(size, when=always):
        return pl.BlockSpec((rows, size * LANES), lambda i, facts: (0, when(i, facts)))

    def stack(size, depth, when=always):
        return pl.BlockSpec((size, rows, depth), lambda i, facts: (when(i, facts), 0, 0))

    query_back = permuted(queries, back)
    key_near = permuted(key_rows, within)
    value_near = permuted(value_rows, within)
    query_near = permuted(queries, within)

    tiles = width // LANES
    per_tile = groups // tiles
    tb = 4
    taps_shape = jax.ShapeDtypeStruct((tiles, rows, per_tile * rows), jnp.bfloat16)
    taps_far, taps_near = run(
        taps_kernel,
        "taps",
        tiles // tb,
        facts,
        (taps_shape, taps_shape),
        [starts, pl.BlockSpec((tb * per_tile, taps), lambda i, facts: (i, 0))],
        (stack(tb, per_tile * rows), stack(tb, per_tile * rows)),
        [pltpu.VMEM((rows, 2 * rows), jnp.bfloat16)],
        (st, filters),
    )

    key_across = permuted(after(key_rows, query_back, taps_far), across)

    hb = 8
    both = lambda i, facts: jnp.where((facts[ODD] == 1) & (facts[NEXT_BEFORE] > rows), i, 0)
    slot_b, stat, slot_c = run(
        lambda *refs: share_kernel(hb, *refs),
        "share",
        heads // hb,
        facts,
        (wide, stats, wide),
        [strip(hb, both), strip(hb, if_odd), strip(hb, both), strip(hb, both), strip(hb, both), strip(hb, if_odd)],
        (strip(hb, if_odd), square, strip(hb, if_odd)),
        [pltpu.VMEM((2 * rows, 2 * rows), jnp.float32)],
        (query_back, queries, key_near, key_rows, value_near, value_rows),
    )
    b_across = permuted(slot_b, across)
    stat_across = permuted(stat, across)
    c_across = permuted(slot_c, across)
    key_far = permuted(after(key_across, slot_b), within)

    three = jax.ShapeDtypeStruct((heads, rows, 3 * rows), jnp.bfloat16)
    two = jax.ShapeDtypeStruct((heads, rows, 2 * rows), jnp.bfloat16)
    weights_three, weights_two, tops = run(
        lambda *refs: weights_kernel(hb, *refs),
        "weights",
        heads // hb,
        facts,
        (three, two, stats),
        [starts, strip(hb), strip(hb), strip(hb, if_even)] + [strip(hb, if_odd)] * 3,
        (stack(hb, 3 * rows, if_odd), stack(hb, 2 * rows), square),
        [pltpu.VMEM((rows, 3 * rows), jnp.float32), pltpu.VMEM((rows, 2 * rows), jnp.float32)],
        (st, queries, key_rows, key_across, key_far, key_near, query_near),
    )
    value_far = permuted(after(b_across, weights_two), within)

    att_shape = jax.ShapeDtypeStruct((heads, rows, HEAD_DIM), jnp.bfloat16)
    att, near, squares, near_squares = run(
        lambda *refs: values_kernel(hb, *refs),
        "values",
        heads // hb,
        facts,
        (att_shape, att_shape, stats, stats),
        [stack(hb, 3 * rows, if_odd), stack(hb, 2 * rows), square, square, strip(hb, if_even), strip(hb, if_odd), strip(hb, if_odd), strip(hb)],
        (stack(hb, HEAD_DIM), stack(hb, HEAD_DIM, if_odd), square, square),
        [],
        (weights_three, weights_two, tops, stat_across, b_across, value_far, value_near, value_rows),
    )

    gain = norm_gain.reshape(1, width)
    lane = pl.BlockSpec((1, tb * LANES), lambda i, facts: (0, i))
    part = run(
        lambda *refs: own_kernel(width, *refs),
        "own",
        tiles // tb,
        facts,
        jax.ShapeDtypeStruct((rows, width), jnp.float32),
        [stack(tb, HEAD_DIM), square, stack(tb, per_tile * rows), lane, lane],
        strip(tb),
        [pltpu.VMEM((rows, LANES), jnp.float32)],
        (att, squares, taps_near, gain, bypass.reshape(1, width)),
    )

    a_steps = heads // hb
    early = lambda when: lambda i, facts: jnp.where(when(facts), jnp.minimum(i, a_steps - 1), 0)
    late = lambda i, facts: jnp.maximum(i - a_steps, 0)
    alone = early(lambda facts: (facts[ODD] == 0) & (facts[BEFORE] <= rows))
    return run(
        lambda *refs: finish_kernel(hb, a_steps, *refs),
        "finish",
        a_steps + tiles // tb,
        facts,
        wide,
        [
            starts,
            strip(hb, alone),
            strip(hb, alone),
            strip(hb, early(lambda facts: facts[ODD] == 0)),
            stack(hb, HEAD_DIM, early(lambda facts: facts[ODD] == 1)),
            square,
            strip(tb, late),
            stack(tb, per_tile * rows, late),
            pl.BlockSpec((1, tb * LANES), lambda i, facts: (0, late(i, facts))),
        ],
        strip(tb, late),
        [
            pltpu.VMEM((tiles, rows, LANES), jnp.bfloat16),
            pltpu.VMEM((rows, LANES), jnp.float32),
            pltpu.VMEM((rows, LANES), jnp.float32),
            pltpu.VMEM((rows, rows), jnp.float32),
        ],
        (st, key_across, b_across, after(c_across, part), near, near_squares, part, taps_far, gain),
    )


def solution(mesh):
    rows = P(("dp", "ctx"), None)
    in_specs = (rows, rows, rows, P("dp"), P(), P(), P())
    return jax.shard_map(shards, mesh=mesh, in_specs=in_specs, out_specs=rows, check_vma=False)
```

time: 112 us -> 88.2 us (0.79)
  local copies, waits for them, and re-layouts: 18.1 us -> 5.23 us
  Pallas kernels: 33 us -> 25.4 us
  starting transfers between devices: 19.5 us -> 16.8 us
    unnamed x40 -> x18, local copies, waits for them, and re-layouts: 17.1 us -> 4.53 us
    pallas_call x4 -> x6, Pallas kernels: 33 us -> 25.4 us  [run(): pl.pallas_call(kernel, out_shape=out_shape, grid_spec=pltpu.PrefetchScala...]
    ppermute x10, starting transfers between devices: 19.5 us -> 16.8 us  [permuted(): return lax.ppermute(x, 'ctx', pairs)]
  transfers between devices with their start and end apart: 10 -> 10, of which waited for: 4 -> 4; matrix products, arithmetic and copies ran while one was open for 3% -> 4% of each run, Pallas kernels for 14% -> 19%
where the time goes in v3:
time: 88.2 us; the launch traced here: 87.7 us
  waiting for transfers between devices  35.5 us (40%)
  Pallas kernels  25.4 us (29%)
  starting transfers between devices  16.8 us (19%)
  local copies, waits for them, and re-layouts  5.23 us (6%)
  other arithmetic  2.49 us (3%)
  between operations  2.2 us (2%)
    ppermute x10, waiting for transfers between devices, permuted(): return lax.ppermute(x, 'ctx', pairs)  35.5 us
    pallas_call x6, Pallas kernels, run(): pl.pallas_call(kernel, out_shape=out_shape, grid_spec=pltpu.PrefetchScala...  25.4 us
    ppermute x10, starting transfers between devices, permuted(): return lax.ppermute(x, 'ctx', pairs)  16.8 us
    unnamed x18, local copies, waits for them, and re-layouts  4.53 us
  transfers between devices with their start and end apart: 10, of which 4 were waited for; matrix products, arithmetic and copies ran while one was open for 4% of the time, Pallas kernels for 19%

profile of v3, /device:TPU:28, one launch (start us, length us, event | category | flops | bytes accessed | tf_op | source)
XLA Modules:
  0.0 87.7 jit_solution(4742174107300850458)
XLA Ops:
  0.0 1.8 %collective-permute-start.3 = (bf16[128,4096]{1,0:T(8,128)(2,1)}, bf16[128,4096]{1,0:T(8,128)(2,1)S(1)}, u32[]{:S(2)}, u32[]{:S(2)}) collective-permute-start(bf16[128,4096]{1,0:T(8,128)(2,1)} %refs_8_.1), channel_id=1, source_target_pairs={{0,2},{4,6},{8,10},{12,14},{16,18},{20,22},{24,26},{28,30},{1,3},{... | collective-permute-start | bytes 3145736 | tf_op jit(solution)/shard_map/ppermute | solution.py:21
  1.8 2.3 %collective-permute-start = (bf16[128,4096]{1,0:T(8,128)(2,1)}, bf16[128,4096]{1,0:T(8,128)(2,1)S(1)}, u32[]{:S(2)}, u32[]{:S(2)}) collective-permute-start(bf16[128,4096]{1,0:T(8,128)(2,1)} %refs_2_.3), channel_id=1, source_target_pairs={{4,2},{8,6},{12,10},{16,14},{20,18},{24,22},{28,26},{5,3},{9,7},{1... | collective-permute-start | bytes 3145736 | tf_op jit(solution)/shard_map/ppermute | solution.py:21
  4.1 1.4 %collective-permute-start.2 = (bf16[128,4096]{1,0:T(8,128)(2,1)}, bf16[128,4096]{1,0:T(8,128)(2,1)S(1)}, u32[]{:S(2)}, u32[]{:S(2)}) collective-permute-start(bf16[128,4096]{1,0:T(8,128)(2,1)} %refs_3_.1), channel_id=1, source_target_pairs={{0,2},{4,6},{8,10},{12,14},{16,18},{20,22},{24,26},{28,30},{1,3},{... | collective-permute-start | bytes 3145736 | tf_op jit(solution)/shard_map/ppermute | solution.py:21
  6.3 0.8 select_reduce_fusion
  11.5 5.2 %taps.1 = (bf16[32,128,1024]{2,1,0:T(8,128)(2,1)S(1)}, bf16[32,128,1024]{2,1,0:T(8,128)(2,1)S(1)}) custom-call(s32[4]{0:T(128)S(1)} %pad_add_fusion.facts_ref.refs_0_, s32[128,1]{1,0:T(8,128)S(1)} %copy.10.st_ref.refs_1_, bf16[256,128]{1,0:T(8,128)(2,1)S(1)} %copy-done.6), custom_call_target="tpu_custom_call" | custom-call | flops 1048576 | bytes 65536 | tf_op jit(solution)/shard_map/taps/pallas_call | solution.py:325
  16.7 1.3 %collective-permute-start.1 = (bf16[128,4096]{1,0:T(8,128)(2,1)}, bf16[128,4096]{1,0:T(8,128)(2,1)S(1)}, u32[]{:S(2)}, u32[]{:S(2)}) collective-permute-start(bf16[128,4096]{1,0:T(8,128)(2,1)} %refs_3_.1), channel_id=1, source_target_pairs={{2,4},{6,8},{10,12},{14,16},{18,20},{22,24},{26,28},{3,5},{7,9},{1... | collective-permute-start | bytes 3145736 | tf_op jit(solution)/shard_map/ppermute | solution.py:21
  18.0 3.4 %collective-permute-start.7 = (bf16[128,4096]{1,0:T(8,128)(2,1)}, bf16[128,4096]{1,0:T(8,128)(2,1)S(1)}, u32[]{:S(2)}, u32[]{:S(2)}) collective-permute-start(bf16[128,4096]{1,0:T(8,128)(2,1)} %refs_2_.3), channel_id=1, source_target_pairs={{0,2},{4,6},{8,10},{12,14},{16,18},{20,22},{24,26},{28,30},{1,3},{... | collective-permute-start | bytes 3145736 | tf_op jit(solution)/shard_map/ppermute | solution.py:21
  21.4 1.2 %copy-done = bf16[128,4096]{1,0:T(8,128)(2,1)S(1)} copy-done((bf16[128,4096]{1,0:T(8,128)(2,1)S(1)}, bf16[128,4096]{1,0:T(8,128)(2,1)}, u32[]{:S(2)}) %copy-start) | copy-done | bytes 1048600
  22.6 1.2 %copy-done.2 = bf16[128,4096]{1,0:T(8,128)(2,1)S(1)} copy-done((bf16[128,4096]{1,0:T(8,128)(2,1)S(1)}, bf16[128,4096]{1,0:T(8,128)(2,1)}, u32[]{:S(2)}) %copy-start.2) | copy-done | bytes 1048600
  23.9 1.2 %copy-done.4 = bf16[128,4096]{1,0:T(8,128)(2,1)S(1)} copy-done((bf16[128,4096]{1,0:T(8,128)(2,1)S(1)}, bf16[128,4096]{1,0:T(8,128)(2,1)}, u32[]{:S(2)}) %copy-start.4) | copy-done | bytes 1048600
  25.1 1.1 %share.1 = (bf16[128,4096]{1,0:T(8,128)(2,1)S(1)}, f32[128,128]{1,0:T(8,128)S(1)}, bf16[128,4096]{1,0:T(8,128)(2,1)S(1)}) custom-call(s32[4]{0:T(128)S(1)} %pad_add_fusion.facts_ref.refs_0_, bf16[128,4096]{1,0:T(8,128)(2,1)S(1)} %collective-permute-done.refs_1_, bf16[128,4096]{1,0:T(8,128)(2,1)S(1)} %copy-done.2, ...), custom_call_target="tpu_custom_call" | custom-call | flops 1048576 | bytes 65536 | tf_op jit(solution)/shard_map/share/pallas_call | solution.py:325
  26.2 7.7 %collective-permute-done.1.refs_4_.refs_2_ = bf16[128,4096]{1,0:T(8,128)(2,1)S(1)} collective-permute-done((bf16[128,4096]{1,0:T(8,128)(2,1)}, bf16[128,4096]{1,0:T(8,128)(2,1)S(1)}, u32[]{:S(2)}, u32[]{:S(2)}) %collective-permute-start.1) | collective-permute-done | bytes 1048608 | tf_op jit(solution)/shard_map/ppermute | solution.py:21
  33.9 1.5 %collective-permute-start.6 = (bf16[128,4096]{1,0:T(8,128)(2,1)S(1)}, bf16[128,4096]{1,0:T(8,128)(2,1)S(1)}, u32[]{:S(2)}, u32[]{:S(2)}) collective-permute-start(bf16[128,4096]{1,0:T(8,128)(2,1)S(1)} %collective-permute-done.1.refs_4_.refs_2_), channel_id=1, source_target_pairs={{0,2},{4,6},{8,10},{12,14},{16,18},{20,22},{24,26},{28,30},{1,3},{... | collective-permute-start | bytes 3145736 | tf_op jit(solution)/shard_map/ppermute | solution.py:21
  35.4 1.3 %collective-permute-start.4 = (bf16[128,4096]{1,0:T(8,128)(2,1)S(1)}, bf16[128,4096]{1,0:T(8,128)(2,1)S(1)}, u32[]{:S(2)}, u32[]{:S(2)}) collective-permute-start(bf16[128,4096]{1,0:T(8,128)(2,1)S(1)} %get-tuple-element.23), channel_id=1, source_target_pairs={{2,4},{6,8},{10,12},{14,16},{18,20},{22,24},{26,28},{3,5},{7,9},{1... | collective-permute-start | bytes 3145736 | tf_op jit(solution)/shard_map/ppermute | solution.py:21
  36.7 0.9 %collective-permute-done.6.refs_5_ = bf16[128,4096]{1,0:T(8,128)(2,1)S(1)} collective-permute-done((bf16[128,4096]{1,0:T(8,128)(2,1)S(1)}, bf16[128,4096]{1,0:T(8,128)(2,1)S(1)}, u32[]{:S(2)}, u32[]{:S(2)}) %collective-permute-start.6) | collective-permute-done | bytes 1048608 | tf_op jit(solution)/shard_map/ppermute | solution.py:21
  37.6 3.0 %weights.1 = (bf16[32,128,384]{2,1,0:T(8,128)(2,1)S(1)}, bf16[32,128,256]{2,1,0:T(8,128)(2,1)S(1)}, f32[128,128]{1,0:T(8,128)S(1)}) custom-call(s32[4]{0:T(128)S(1)} %pad_add_fusion.facts_ref.refs_0_, s32[128,1]{1,0:T(8,128)S(1)} %copy.10.st_ref.refs_1_, bf16[128,4096]{1,0:T(8,128)(2,1)S(1)} %copy-done.3, bf16[128,4096]{1,0:T(8,128)(2,1)S(1)} %copy-done.1, ...), custom_call_target="tpu_custom_call" | custom-call | flops 1048576 | bytes 65536 | tf_op jit(solution)/shard_map/weights/pallas_call | solution.py:325
  40.6 11.8 %collective-permute-done.4.refs_5_.refs_3_ = bf16[128,4096]{1,0:T(8,128)(2,1)S(1)} collective-permute-done((bf16[128,4096]{1,0:T(8,128)(2,1)S(1)}, bf16[128,4096]{1,0:T(8,128)(2,1)S(1)}, u32[]{:S(2)}, u32[]{:S(2)}) %collective-permute-start.4) | collective-permute-done | bytes 1048608 | tf_op jit(solution)/shard_map/ppermute | solution.py:21
  52.4 1.3 %collective-permute-start.9 = (bf16[128,4096]{1,0:T(8,128)(2,1)S(1)}, bf16[128,4096]{1,0:T(8,128)(2,1)S(1)}, u32[]{:S(2)}, u32[]{:S(2)}) collective-permute-start(bf16[128,4096]{1,0:T(8,128)(2,1)S(1)} %collective-permute-done.4.refs_5_.refs_3_), channel_id=1, source_target_pairs={{0,2},{4,6},{8,10},{12,14},{16,18},{20,22},{24,26},{28,30},{1,3},{... | collective-permute-start | bytes 3145736 | tf_op jit(solution)/shard_map/ppermute | solution.py:21
  53.8 1.3 %collective-permute-start.5 = (bf16[128,4096]{1,0:T(8,128)(2,1)S(1)}, bf16[128,4096]{1,0:T(8,128)(2,1)S(1)}, u32[]{:S(2)}, u32[]{:S(2)}) collective-permute-start(bf16[128,4096]{1,0:T(8,128)(2,1)S(1)} %get-tuple-element.24), channel_id=1, source_target_pairs={{2,4},{6,8},{10,12},{14,16},{18,20},{22,24},{26,28},{3,5},{7,9},{1... | collective-permute-start | bytes 3145736 | tf_op jit(solution)/shard_map/ppermute | solution.py:21
  55.1 1.3 %collective-permute-start.8 = (f32[128,128]{1,0:T(8,128)S(1)}, f32[128,128]{1,0:T(8,128)S(1)}, u32[]{:S(2)}, u32[]{:S(2)}) collective-permute-start(f32[128,128]{1,0:T(8,128)S(1)} %get-tuple-element.29), channel_id=1, source_target_pairs={{2,4},{6,8},{10,12},{14,16},{18,20},{22,24},{26,28},{3,5},{7,9},{1... | collective-permute-start | bytes 196616 | tf_op jit(solution)/shard_map/ppermute | solution.py:21
  56.4 15.1 %collective-permute-done.8.refs_4_ = f32[128,128]{1,0:T(8,128)S(1)} collective-permute-done((f32[128,128]{1,0:T(8,128)S(1)}, f32[128,128]{1,0:T(8,128)S(1)}, u32[]{:S(2)}, u32[]{:S(2)}) %collective-permute-start.8) | collective-permute-done | bytes 65568 | tf_op jit(solution)/shard_map/ppermute | solution.py:21
  71.5 2.8 %values.1 = (bf16[32,128,128]{2,1,0:T(8,128)(2,1)S(1)}, bf16[32,128,128]{2,1,0:T(8,128)(2,1)S(1)}, f32[128,128]{1,0:T(8,128)S(1)}, f32[128,128]{1,0:T(8,128)S(1)}) custom-call(s32[4]{0:T(128)S(1)} %pad_add_fusion.facts_ref.refs_0_, bf16[32,128,384]{2,1,0:T(8,128)(2,1)S(1)} %get-tuple-element.26.refs_1_, bf16[32,128,256]{2,1,0:T(8,128)(2,1)S(1)} %get-tuple-element.27.refs_2_, ...), custom_call_target="tpu_custom_call" | custom-call | flops 1048576 | bytes 65536 | tf_op jit(solution)/shard_map/values/pallas_call | solution.py:325
  74.3 4.3 %own.1.refs_7_ = f32[128,4096]{1,0:T(8,128)S(1)} custom-call(s32[4]{0:T(128)S(1)} %pad_add_fusion.facts_ref.refs_0_, bf16[32,128,128]{2,1,0:T(8,128)(2,1)S(1)} %get-tuple-element.31.refs_1_, f32[128,128]{1,0:T(8,128)S(1)} %get-tuple-element.32.refs_2_, bf16[32,128,1024]{2,1,0:T(8,128)(2,1)S(1)} %get-tuple-element.33.refs_3_, f32[1,4096]{1,0:T(1,128)S(1)} %bitcast.15, ...), custom_call_target="tpu_custom_call" | custom-call | flops 1048576 | bytes 65536 | tf_op jit(solution)/shard_map/own/pallas_call | solution.py:325
  78.6 9.1 %finish.1 = bf16[128,4096]{1,0:T(8,128)(2,1)} custom-call(s32[4]{0:T(128)S(1)} %pad_add_fusion.facts_ref.refs_0_, s32[128,1]{1,0:T(8,128)S(1)} %copy.10.st_ref.refs_1_, bf16[128,4096]{1,0:T(8,128)(2,1)S(1)} %collective-permute-done.1.refs_4_.refs_2_, bf16[128,4096]{1,0:T(8,128)(2,1)S(1)} %collective-permute-done.4.refs_5_.refs_3_, ...), custom_call_target="tpu_custom_call" | custom-call | flops 1048576 | bytes 65536 | tf_op jit(solution)/shard_map/finish/pallas_call | solution.py:325
  (30 shorter events, 3.2 us)
Async XLA Ops:
  0.0 21.4 %collective-permute-start.3 = (bf16[128,4096]{1,0:T(8,128)(2,1)}, bf16[128,4096]{1,0:T(8,128)(2,1)S(1)}, u32[]{:S(2)}, u32[]{:S(2)}) collective-permute-start(bf16[128,4096]{1,0:T(8,128)(2,1)} %refs_8_.1), channel_id=1, source_target_pairs={{0,2},{4,6},{8,10},{12,14},{16,18},{20,22},{24,26},{28,30},{1,3},{... | collective-permute-start | bytes 3145736 | tf_op jit(solution)/shard_map/ppermute | solution.py:21
  1.8 14.9 %collective-permute-start = (bf16[128,4096]{1,0:T(8,128)(2,1)}, bf16[128,4096]{1,0:T(8,128)(2,1)S(1)}, u32[]{:S(2)}, u32[]{:S(2)}) collective-permute-start(bf16[128,4096]{1,0:T(8,128)(2,1)} %refs_2_.3), channel_id=1, source_target_pairs={{4,2},{8,6},{12,10},{16,14},{20,18},{24,22},{28,26},{5,3},{9,7},{1... | collective-permute-start | bytes 3145736 | tf_op jit(solution)/shard_map/ppermute | solution.py:21
  4.1 17.3 %collective-permute-start.2 = (bf16[128,4096]{1,0:T(8,128)(2,1)}, bf16[128,4096]{1,0:T(8,128)(2,1)S(1)}, u32[]{:S(2)}, u32[]{:S(2)}) collective-permute-start(bf16[128,4096]{1,0:T(8,128)(2,1)} %refs_3_.1), channel_id=1, source_target_pairs={{0,2},{4,6},{8,10},{12,14},{16,18},{20,22},{24,26},{28,30},{1,3},{... | collective-permute-start | bytes 3145736 | tf_op jit(solution)/shard_map/ppermute | solution.py:21
  10.6 0.8 copy-start.6
  16.7 17.2 %collective-permute-start.1 = (bf16[128,4096]{1,0:T(8,128)(2,1)}, bf16[128,4096]{1,0:T(8,128)(2,1)S(1)}, u32[]{:S(2)}, u32[]{:S(2)}) collective-permute-start(bf16[128,4096]{1,0:T(8,128)(2,1)} %refs_3_.1), channel_id=1, source_target_pairs={{2,4},{6,8},{10,12},{14,16},{18,20},{22,24},{26,28},{3,5},{7,9},{1... | collective-permute-start | bytes 3145736 | tf_op jit(solution)/shard_map/ppermute | solution.py:21
  18.0 18.7 %collective-permute-start.7 = (bf16[128,4096]{1,0:T(8,128)(2,1)}, bf16[128,4096]{1,0:T(8,128)(2,1)S(1)}, u32[]{:S(2)}, u32[]{:S(2)}) collective-permute-start(bf16[128,4096]{1,0:T(8,128)(2,1)} %refs_2_.3), channel_id=1, source_target_pairs={{0,2},{4,6},{8,10},{12,14},{16,18},{20,22},{24,26},{28,30},{1,3},{... | collective-permute-start | bytes 3145736 | tf_op jit(solution)/shard_map/ppermute | solution.py:21
  21.4 1.2 %copy-start = (bf16[128,4096]{1,0:T(8,128)(2,1)S(1)}, bf16[128,4096]{1,0:T(8,128)(2,1)}, u32[]{:S(2)}) copy-start(bf16[128,4096]{1,0:T(8,128)(2,1)} %refs_3_.1) | copy-start | bytes 3145732
  22.6 1.2 %copy-start.2 = (bf16[128,4096]{1,0:T(8,128)(2,1)S(1)}, bf16[128,4096]{1,0:T(8,128)(2,1)}, u32[]{:S(2)}) copy-start(bf16[128,4096]{1,0:T(8,128)(2,1)} %refs_2_.3) | copy-start | bytes 3145732
  23.9 1.2 %copy-start.4 = (bf16[128,4096]{1,0:T(8,128)(2,1)S(1)}, bf16[128,4096]{1,0:T(8,128)(2,1)}, u32[]{:S(2)}) copy-start(bf16[128,4096]{1,0:T(8,128)(2,1)} %refs_8_.1) | copy-start | bytes 3145732
  25.1 12.5 %copy-start.1 = (bf16[128,4096]{1,0:T(8,128)(2,1)S(1)}, bf16[128,4096]{1,0:T(8,128)(2,1)}, u32[]{:S(2)}) copy-start(bf16[128,4096]{1,0:T(8,128)(2,1)} %refs_3_.1) | copy-start | bytes 3145732
  25.1 12.5 %copy-start.3 = (bf16[128,4096]{1,0:T(8,128)(2,1)S(1)}, bf16[128,4096]{1,0:T(8,128)(2,1)}, u32[]{:S(2)}) copy-start(bf16[128,4096]{1,0:T(8,128)(2,1)} %refs_2_.3) | copy-start | bytes 3145732
  33.9 37.6 %copy-start.5 = (bf16[128,4096]{1,0:T(8,128)(2,1)S(1)}, bf16[128,4096]{1,0:T(8,128)(2,1)}, u32[]{:S(2)}) copy-start(bf16[128,4096]{1,0:T(8,128)(2,1)} %refs_8_.1) | copy-start | bytes 3145732
  33.9 3.7 %collective-permute-start.6 = (bf16[128,4096]{1,0:T(8,128)(2,1)S(1)}, bf16[128,4096]{1,0:T(8,128)(2,1)S(1)}, u32[]{:S(2)}, u32[]{:S(2)}) collective-permute-start(bf16[128,4096]{1,0:T(8,128)(2,1)S(1)} %collective-permute-done.1.refs_4_.refs_2_), channel_id=1, source_target_pairs={{0,2},{4,6},{8,10},{12,14},{16,18},{20,22},{24,26},{28,30},{1,3},{... | collective-permute-start | bytes 3145736 | tf_op jit(solution)/shard_map/ppermute | solution.py:21
  35.4 17.0 %collective-permute-start.4 = (bf16[128,4096]{1,0:T(8,128)(2,1)S(1)}, bf16[128,4096]{1,0:T(8,128)(2,1)S(1)}, u32[]{:S(2)}, u32[]{:S(2)}) collective-permute-start(bf16[128,4096]{1,0:T(8,128)(2,1)S(1)} %get-tuple-element.23), channel_id=1, source_target_pairs={{2,4},{6,8},{10,12},{14,16},{18,20},{22,24},{26,28},{3,5},{7,9},{1... | collective-permute-start | bytes 3145736 | tf_op jit(solution)/shard_map/ppermute | solution.py:21
  52.4 19.1 %collective-permute-start.9 = (bf16[128,4096]{1,0:T(8,128)(2,1)S(1)}, bf16[128,4096]{1,0:T(8,128)(2,1)S(1)}, u32[]{:S(2)}, u32[]{:S(2)}) collective-permute-start(bf16[128,4096]{1,0:T(8,128)(2,1)S(1)} %collective-permute-done.4.refs_5_.refs_3_), channel_id=1, source_target_pairs={{0,2},{4,6},{8,10},{12,14},{16,18},{20,22},{24,26},{28,30},{1,3},{... | collective-permute-start | bytes 3145736 | tf_op jit(solution)/shard_map/ppermute | solution.py:21
  53.8 24.9 %collective-permute-start.5 = (bf16[128,4096]{1,0:T(8,128)(2,1)S(1)}, bf16[128,4096]{1,0:T(8,128)(2,1)S(1)}, u32[]{:S(2)}, u32[]{:S(2)}) collective-permute-start(bf16[128,4096]{1,0:T(8,128)(2,1)S(1)} %get-tuple-element.24), channel_id=1, source_target_pairs={{2,4},{6,8},{10,12},{14,16},{18,20},{22,24},{26,28},{3,5},{7,9},{1... | collective-permute-start | bytes 3145736 | tf_op jit(solution)/shard_map/ppermute | solution.py:21
  55.1 16.4 %collective-permute-start.8 = (f32[128,128]{1,0:T(8,128)S(1)}, f32[128,128]{1,0:T(8,128)S(1)}, u32[]{:S(2)}, u32[]{:S(2)}) collective-permute-start(f32[128,128]{1,0:T(8,128)S(1)} %get-tuple-element.29), channel_id=1, source_target_pairs={{2,4},{6,8},{10,12},{14,16},{18,20},{22,24},{26,28},{3,5},{7,9},{1... | collective-permute-start | bytes 196616 | tf_op jit(solution)/shard_map/ppermute | solution.py:21
  71.5 2.8 %copy-start.7 = (f32[4096]{0:T(1024)S(1)}, f32[4096]{0:T(1024)}, u32[]{:S(2)}) copy-start(f32[4096]{0:T(1024)} %param.11) | copy-start | bytes 49156
  71.5 2.8 %copy-start.8 = (f32[4096]{0:T(1024)S(1)}, f32[4096]{0:T(1024)}, u32[]{:S(2)}) copy-start(f32[4096]{0:T(1024)} %param.13) | copy-start | bytes 49156

commit v4 on v3

--- a/solution.py
+++ b/solution.py
@@ -101,16 +101,19 @@
             near_ref[c, :, cols] = ring * keep[:, rows:]
 
 
-def share_kernel(heads, facts_ref, qb_ref, q_ref, kn_ref, ko_ref, vn_ref, vo_ref, b_ref, stat_ref, c_ref, bias):
+def share_kernel(heads, facts_ref, qb_ref, q_ref, kn_ref, ko_ref, vn_ref, vo_ref, *rest):
+    b_ref, c_ref, bias, stat_ref = rest[-4:]
     rows = q_ref.shape[0]
     step = pl.program_id(0)
     before = facts_ref[NEXT_BEFORE]
     past = facts_ref[NEXT_AFTER]
     odd = facts_ref[ODD] == 1
+    last = b_ref.shape[0] - 1
 
     @pl.when(odd & (before <= rows))
     def _():
-        b_ref[...] = vo_ref[...]
+        for h in range(heads):
+            b_ref[step * heads + h] = vo_ref[:, columns(h)]
         c_ref[...] = q_ref[...]
 
     @pl.when(odd & (before > rows))
@@ -119,6 +122,7 @@
         def _():
             bias[:rows] = bias_of(rows, 2 * rows, rows, -rows, rows - before)
             bias[rows:] = bias_of(rows, 2 * rows, 0, -rows, rows - before)
+            stat_ref[...] = jnp.zeros_like(stat_ref)
 
         lane = lax.broadcasted_iota(jnp.int32, (rows, LANES), 1)
         ours = lax.broadcasted_iota(jnp.int32, (rows, LANES), 0) < past
@@ -126,7 +130,7 @@
 
         def use(h, o, l, top):
             o = (o / l).astype(jnp.bfloat16)
-            b_ref[:, columns(h)] = o[:rows]
+            b_ref[step * heads + h] = o[:rows]
             c_ref[:, columns(h)] = o[rows:]
             lse = jnp.where(ours, top[:rows] * FACTOR + jnp.log2(l[:rows]), NEG)
             stat[0] = jnp.where(lane == step * heads + h, lse, stat[0])
@@ -141,11 +145,23 @@
         )
         stat_ref[...] = stat[0]
 
-
-def weights_kernel(heads, facts_ref, st_ref, q_ref, ko_ref, kp_ref, kf_ref, kn_ref, qn_ref, three_ref, two_ref, top_ref, bias_own, bias_prev):
+        @pl.when(step == pl.num_programs(0) - 1)
+        def _():
+            total = stat[0]
+            high = total.astype(jnp.bfloat16).astype(jnp.float32)
+            middle = (total - high).astype(jnp.bfloat16).astype(jnp.float32)
+            low = total - high - middle
+            packed = high + pltpu.roll(middle, last, 1) + pltpu.roll(low, 2 * last, 1)
+            b_ref[last] = packed.astype(jnp.bfloat16)
+
+
+def attention_kernel(heads, facts_ref, st_ref, q_ref, ko_ref, vo_ref, kp_ref, vp0_ref, vp1_ref, stat0_ref, stat1_ref, qn_ref, kn_ref, vn_ref, kf_ref, vf0_ref, vf1_ref, att_ref, near_ref, sq_ref, sq_near_ref, bias_own, bias_prev):
     rows = q_ref.shape[0]
     step = pl.program_id(0)
     odd = facts_ref[ODD] == 1
+    half = pl.num_programs(0) // 2
+    vp = lambda h: jnp.where(step < half, vp0_ref[h], vp1_ref[h])
+    vf = lambda h: jnp.where(step < half, vf0_ref[h], vf1_ref[h])
 
     @pl.when(step == 0)
     def _():
@@ -153,92 +169,75 @@
         st = jnp.maximum(st_ref[...], low)
         bias_own[...] = bias_of(rows, 3 * rows, 0, -2 * rows, st)
         bias_prev[...] = bias_of(rows, 2 * rows, -rows, -2 * rows, st_ref[0:1, :])
-
-    @pl.when(odd)
-    def _():
-        def scores(h):
-            key = jnp.concatenate([kf_ref[:, columns(h)], kn_ref[:, columns(h)], ko_ref[:, columns(h)]], axis=0)
-            return scores_of(q_ref[:, columns(h)], key), scores_of(qn_ref[:, columns(h)], key[: 2 * rows])
-
-        ahead = scores(0)
-        for h in range(heads):
-            now = ahead
-            if h + 1 < heads:
-                ahead = scores(h + 1)
-            three_ref[h] = raised(now[0], bias_own[...])[0]
-            two_ref[h] = raised(now[1], bias_prev[...])[0]
-
-    @pl.when(jnp.logical_not(odd))
-    def _():
-        lane = lax.broadcasted_iota(jnp.int32, (rows, LANES), 1)
-        tops = top_ref[...]
-
-        def scores(h):
-            key = jnp.concatenate([kp_ref[:, columns(h)], ko_ref[:, columns(h)]], axis=0)
-            return scores_of(q_ref[:, columns(h)], key)
-
-        ahead = scores(0)
-        for h in range(heads):
-            now = ahead
-            if h + 1 < heads:
-                ahead = scores(h + 1)
-            weights, top = raised(now, bias_own[:, rows:])
-            two_ref[h] = weights
-            tops = jnp.where(lane == step * heads + h, top * FACTOR, tops)
-        top_ref[...] = tops
-
-
-def values_kernel(heads, facts_ref, three_ref, two_ref, top_ref, stat_ref, vp_ref, vf_ref, vn_ref, vo_ref, att_ref, near_ref, sq_ref, sq_near_ref):
-    rows = vo_ref.shape[0]
-    step = pl.program_id(0)
-    odd = facts_ref[ODD] == 1
-
-    @pl.when(step == 0)
-    def _():
         sq_ref[...] = jnp.zeros_like(sq_ref)
         sq_near_ref[...] = jnp.zeros_like(sq_near_ref)
 
     @pl.when(odd)
     def _():
-        squares = sq_ref[...]
-        squares_near = sq_near_ref[...]
-        for h in range(heads):
-            value = jnp.concatenate([vf_ref[:, columns(h)], vn_ref[:, columns(h)], vo_ref[:, columns(h)]], axis=0)
-            o, l = summed(three_ref[h], value)
+        squares = [sq_ref[...], sq_near_ref[...]]
+
+        def use_own(h, o, l, top):
             a = (o / l).astype(jnp.bfloat16)
             att_ref[h] = a
             a = a.astype(jnp.float32)
-            squares += a * a
-            o, l = summed(two_ref[h], value[: 2 * rows])
+            squares[0] += a * a
+
+        def use_near(h, o, l, top):
             a = (o / l).astype(jnp.bfloat16)
             near_ref[h] = a
             a = a.astype(jnp.float32)
-            squares_near += a * a
-        sq_ref[...] = squares
-        sq_near_ref[...] = squares_near
+            squares[1] += a * a
+
+        attend(
+            heads,
+            lambda h: q_ref[:, columns(h)],
+            lambda h: jnp.concatenate([kf_ref[:, columns(h)], kn_ref[:, columns(h)], ko_ref[:, columns(h)]], axis=0),
+            lambda h: jnp.concatenate([vf(h), vn_ref[:, columns(h)], vo_ref[:, columns(h)]], axis=0),
+            bias_own[...],
+            use_own,
+        )
+        attend(
+            heads,
+            lambda h: qn_ref[:, columns(h)],
+            lambda h: jnp.concatenate([kf_ref[:, columns(h)], kn_ref[:, columns(h)]], axis=0),
+            lambda h: jnp.concatenate([vf(h), vn_ref[:, columns(h)]], axis=0),
+            bias_prev[...],
+            use_near,
+        )
+        sq_ref[...] = squares[0]
+        sq_near_ref[...] = squares[1]
 
     @pl.when(jnp.logical_not(odd))
     def _():
         lane = lax.broadcasted_iota(jnp.int32, (rows, LANES), 1)
-        shared = facts_ref[BEFORE] > rows
-        stat = jnp.where(shared, stat_ref[...], NEG)
-        tops = top_ref[...]
-        squares = sq_ref[...]
-        high = jnp.maximum(tops, stat)
-        here_all = jnp.exp2(tops - high)
-        there_all = jnp.exp2(stat - high)
-        for h in range(heads):
-            value = jnp.concatenate([vp_ref[:, columns(h)], vo_ref[:, columns(h)]], axis=0)
-            o, l = summed(two_ref[h], value)
-            mine = lane == step * heads + h
-            here = jnp.sum(jnp.where(mine, here_all, 0.0), axis=1, keepdims=True)
-            there = jnp.sum(jnp.where(mine, there_all, 0.0), axis=1, keepdims=True)
-            o = o * here + vp_ref[:, columns(h)].astype(jnp.float32) * there
+        slot_heads = half * heads
+        first = lax.rem(step, half) * heads
+        packed = jnp.where(step < half, stat0_ref[0], stat1_ref[0]).astype(jnp.float32)
+        stat = packed + pltpu.roll(packed, LANES - slot_heads, 1) + pltpu.roll(packed, LANES - 2 * slot_heads, 1)
+        stat = jnp.where(facts_ref[BEFORE] > rows, stat, NEG)
+        squares = [sq_ref[...]]
+
+        def use(h, o, l, top):
+            lse = jnp.sum(jnp.where(lane == first + h, stat, 0.0), axis=1, keepdims=True)
+            top = top * FACTOR
+            high = jnp.maximum(top, lse)
+            here = jnp.exp2(top - high)
+            there = jnp.exp2(lse - high)
+            o = o * here + vp(h).astype(jnp.float32) * there
             a = (o / (l * here + there)).astype(jnp.bfloat16)
             att_ref[h] = a
             a = a.astype(jnp.float32)
-            squares += a * a
-        sq_ref[...] = squares
+            squares[0] += a * a
+
+        attend(
+            heads,
+            lambda h: q_ref[:, columns(h)],
+            lambda h: jnp.concatenate([kp_ref[:, columns(h)], ko_ref[:, columns(h)]], axis=0),
+            lambda h: jnp.concatenate([vp(h), vo_ref[:, columns(h)]], axis=0),
+            bias_own[:, rows:],
+            use,
+        )
+        sq_ref[...] = squares[0]
 
 
 def scale_of(squares, width):
@@ -266,12 +265,15 @@
         out_ref[:, cols] = y + bypass_ref[:, cols] * x.astype(jnp.float32)
 
 
-def finish_kernel(heads, a_steps, facts_ref, st_ref, kp_ref, vp_ref, c_ref, near_ref, sq_near_ref, part_ref, taps_ref, gain_ref, out_ref, prev, squares, scale, bias):
+def finish_kernel(heads, a_steps, facts_ref, st_ref, kp_ref, vp0_ref, vp1_ref, c_ref, near_ref, sq_near_ref, part_ref, taps_ref, gain_ref, out_ref, prev, squares, scale, bias):
     rows = st_ref.shape[0]
     step = pl.program_id(0)
     width = prev.shape[0] * LANES
     odd = facts_ref[ODD] == 1
     shared = facts_ref[BEFORE] > rows
+    half = a_steps // 2
+    vp = lambda h: jnp.where(step < half, vp0_ref[h], vp1_ref[h])
+    slot = lambda h: c_ref[:, columns(h)]
 
     @pl.when(step == 0)
     def _():
@@ -287,7 +289,7 @@
     def _():
         total = squares[...]
         for h in range(heads):
-            a = c_ref[:, columns(h)]
+            a = slot(h)
             prev[step * heads + h] = a
             a = a.astype(jnp.float32)
             total += a * a
@@ -303,7 +305,7 @@
             a = a.astype(jnp.float32)
             total[0] += a * a
 
-        attend(heads, lambda h: c_ref[:, columns(h)], lambda h: kp_ref[:, columns(h)], lambda h: vp_ref[:, columns(h)], bias[...], use)
+        attend(heads, slot, lambda h: kp_ref[:, columns(h)], vp, bias[...], use)
         squares[...] = total[0]
 
     @pl.when(step == a_steps)
@@ -321,7 +323,7 @@
             out_ref[:, cols] = (y + part_ref[:, cols]).astype(jnp.bfloat16)
 
 
-def run(kernel, name, steps, facts, out_shape, in_specs, out_specs, scratch, args):
+def run(kernel, name, steps, facts, out_shape, in_specs, out_specs, scratch, args, aliases={}):
     return pl.pallas_call(
         kernel,
         out_shape=out_shape,
@@ -330,6 +332,7 @@
         ),
         compiler_params=pltpu.CompilerParams(vmem_limit_bytes=VMEM_BYTES),
         cost_estimate=pl.CostEstimate(flops=2**20, bytes_accessed=2**16, transcendentals=0),
+        input_output_aliases=aliases,
         name=name,
     )(facts, *args)
 
@@ -385,48 +388,63 @@
 
     hb = 8
     both = lambda i, facts: jnp.where((facts[ODD] == 1) & (facts[NEXT_BEFORE] > rows), i, 0)
-    slot_b, stat, slot_c = run(
-        lambda *refs: share_kernel(hb, *refs),
-        "share",
-        heads // hb,
-        facts,
-        (wide, stats, wide),
-        [strip(hb, both), strip(hb, if_odd), strip(hb, both), strip(hb, both), strip(hb, both), strip(hb, if_odd)],
-        (strip(hb, if_odd), square, strip(hb, if_odd)),
-        [pltpu.VMEM((2 * rows, 2 * rows), jnp.float32)],
-        (query_back, queries, key_near, key_rows, value_near, value_rows),
-    )
-    b_across = permuted(slot_b, across)
-    stat_across = permuted(stat, across)
+    half_heads = heads // 2
+    half_steps = half_heads // hb
+    slots = jax.ShapeDtypeStruct((half_heads + 1, rows, HEAD_DIM), jnp.bfloat16)
+
+    def share(part, *filled):
+        offset = part * half_steps
+        on_odd = lambda i, facts: jnp.where(facts[ODD] == 1, i + offset, offset)
+        on_both = lambda i, facts: jnp.where((facts[ODD] == 1) & (facts[NEXT_BEFORE] > rows), i + offset, offset)
+        return run(
+            lambda *refs: share_kernel(hb, *refs),
+            "share",
+            half_steps,
+            facts,
+            (slots, wide),
+            [strip(hb, on_both), strip(hb, on_odd), strip(hb, on_both), strip(hb, on_both), strip(hb, on_both), strip(hb, on_odd)]
+            + [pl.BlockSpec(memory_space=pl.ANY)] * len(filled),
+            (whole((half_heads + 1, rows, HEAD_DIM)), strip(hb, on_odd)),
+            [pltpu.VMEM((2 * rows, 2 * rows), jnp.float32), pltpu.VMEM((rows, LANES), jnp.float32)],
+            (query_back, queries, key_near, key_rows, value_near, value_rows, *filled),
+            {7: 1} if filled else {},
+        )
+
+    slot_b0, slot_c = share(0)
+    slot_b1, slot_c = share(1, slot_c)
+    slots_b = slot_b0, slot_b1
+    b_across = [permuted(x, across) for x in slots_b]
     c_across = permuted(slot_c, across)
-    key_far = permuted(after(key_across, slot_b), within)
-
-    three = jax.ShapeDtypeStruct((heads, rows, 3 * rows), jnp.bfloat16)
-    two = jax.ShapeDtypeStruct((heads, rows, 2 * rows), jnp.bfloat16)
-    weights_three, weights_two, tops = run(
-        lambda *refs: weights_kernel(hb, *refs),
-        "weights",
-        heads // hb,
-        facts,
-        (three, two, stats),
-        [starts, strip(hb), strip(hb), strip(hb, if_even)] + [strip(hb, if_odd)] * 3,
-        (stack(hb, 3 * rows, if_odd), stack(hb, 2 * rows), square),
-        [pltpu.VMEM((rows, 3 * rows), jnp.float32), pltpu.VMEM((rows, 2 * rows), jnp.float32)],
-        (st, queries, key_rows, key_across, key_far, key_near, query_near),
-    )
-    value_far = permuted(after(b_across, weights_two), within)
+    key_far = permuted(after(key_across, *slots_b), within)
+    value_far = [permuted(x, within) for x in b_across]
 
     att_shape = jax.ShapeDtypeStruct((heads, rows, HEAD_DIM), jnp.bfloat16)
     att, near, squares, near_squares = run(
-        lambda *refs: values_kernel(hb, *refs),
-        "values",
+        lambda *refs: attention_kernel(hb, *refs),
+        "attention",
         heads // hb,
         facts,
         (att_shape, att_shape, stats, stats),
-        [stack(hb, 3 * rows, if_odd), stack(hb, 2 * rows), square, square, strip(hb, if_even), strip(hb, if_odd), strip(hb, if_odd), strip(hb)],
+        [
+            starts,
+            strip(hb),
+            strip(hb),
+            strip(hb),
+            strip(hb, if_even),
+            stack(hb, HEAD_DIM, lambda i, facts: if_even(jnp.minimum(i, half_steps - 1), facts)),
+            stack(hb, HEAD_DIM, lambda i, facts: if_even(jnp.maximum(i - half_steps, 0), facts)),
+            stack(1, HEAD_DIM, lambda i, facts: half_heads),
+            stack(1, HEAD_DIM, lambda i, facts: half_heads),
+            strip(hb, if_odd),
+            strip(hb, if_odd),
+            strip(hb, if_odd),
+            strip(hb, if_odd),
+            stack(hb, HEAD_DIM, lambda i, facts: if_odd(jnp.minimum(i, half_steps - 1), facts)),
+            stack(hb, HEAD_DIM, lambda i, facts: if_odd(jnp.maximum(i - half_steps, 0), facts)),
+        ],
         (stack(hb, HEAD_DIM), stack(hb, HEAD_DIM, if_odd), square, square),
-        [],
-        (weights_three, weights_two, tops, stat_across, b_across, value_far, value_near, value_rows),
+        [pltpu.VMEM((rows, 3 * rows), jnp.float32), pltpu.VMEM((rows, 2 * rows), jnp.float32)],
+        (st, queries, key_rows, value_rows, key_across, *b_across, *b_across, query_near, key_near, value_near, key_far, *value_far),
     )
 
     gain = norm_gain.reshape(1, width)
@@ -444,9 +462,13 @@
     )
 
     a_steps = heads // hb
-    early = lambda when: lambda i, facts: jnp.where(when(facts), jnp.minimum(i, a_steps - 1), 0)
+
+    def early(when, low=0, high=a_steps - 1):
+        return lambda i, facts: jnp.where(when(facts), jnp.clip(i - low, 0, high - low), 0)
+
     late = lambda i, facts: jnp.maximum(i - a_steps, 0)
-    alone = early(lambda facts: (facts[ODD] == 0) & (facts[BEFORE] <= rows))
+    even = lambda facts: facts[ODD] == 0
+    alone = lambda facts: even(facts) & (facts[BEFORE] <= rows)
     return run(
         lambda *refs: finish_kernel(hb, a_steps, *refs),
         "finish",
@@ -455,9 +477,10 @@
         wide,
         [
             starts,
-            strip(hb, alone),
-            strip(hb, alone),
-            strip(hb, early(lambda facts: facts[ODD] == 0)),
+            strip(hb, early(alone)),
+            stack(hb, HEAD_DIM, early(alone, 0, half_steps - 1)),
+            stack(hb, HEAD_DIM, early(alone, half_steps)),
+            strip(hb, early(even)),
             stack(hb, HEAD_DIM, early(lambda facts: facts[ODD] == 1)),
             square,
             strip(tb, late),
@@ -471,7 +494,7 @@
             pltpu.VMEM((rows, LANES), jnp.float32),
             pltpu.VMEM((rows, rows), jnp.float32),
         ],
-        (st, key_across, b_across, after(c_across, part), near, near_squares, part, taps_far, gain),
+        (st, key_across, *b_across, c_across, near, near_squares, part, taps_far, gain),
     )
 
 

time: 88.2 us -> 68 us (0.77)
  the two profiles are of different devices: /device:TPU:28 before, /device:TPU:17 now
where the time goes in v4:
time: 68 us; the launch traced here: 67.5 us
  Pallas kernels  29.6 us (44%)
  starting transfers between devices  18.8 us (28%)
  waiting for transfers between devices  9.21 us (14%)
  local copies, waits for them, and re-layouts  5.19 us (8%)
  other arithmetic  2.49 us (4%)
  between operations  2.25 us (3%)
    pallas_call x6, Pallas kernels, run(): pl.pallas_call(kernel, out_shape=out_shape, grid_spec=pltpu.PrefetchScala...  29.6 us
    ppermute x11, starting transfers between devices, permuted(): return lax.ppermute(x, 'ctx', pairs)  18.8 us
    ppermute x11, waiting for transfers between devices, permuted(): return lax.ppermute(x, 'ctx', pairs)  9.21 us
    unnamed x18, local copies, waits for them, and re-layouts  4.53 us
  transfers between devices with their start and end apart: 11, of which 3 were waited for; matrix products, arithmetic and copies ran while one was open for 5% of the time, Pallas kernels for 34%

profile of v4, /device:TPU:17, one launch (start us, length us, event | category | flops | bytes accessed | tf_op | source)
XLA Modules:
  0.0 67.5 jit_solution(11046909573773498261)
XLA Ops:
  0.0 1.3 %collective-permute-start.3 = (bf16[128,4096]{1,0:T(8,128)(2,1)}, bf16[128,4096]{1,0:T(8,128)(2,1)S(1)}, u32[]{:S(2)}, u32[]{:S(2)}) collective-permute-start(bf16[128,4096]{1,0:T(8,128)(2,1)} %refs_4_.5), channel_id=1, source_target_pairs={{0,2},{4,6},{8,10},{12,14},{16,18},{20,22},{24,26},{28,30},{1,3},{... | collective-permute-start | bytes 3145736 | tf_op jit(solution)/shard_map/ppermute | solution.py:21
  1.3 1.3 %collective-permute-start = (bf16[128,4096]{1,0:T(8,128)(2,1)}, bf16[128,4096]{1,0:T(8,128)(2,1)S(1)}, u32[]{:S(2)}, u32[]{:S(2)}) collective-permute-start(bf16[128,4096]{1,0:T(8,128)(2,1)} %refs_2_.5), channel_id=1, source_target_pairs={{4,2},{8,6},{12,10},{16,14},{20,18},{24,22},{28,26},{5,3},{9,7},{1... | collective-permute-start | bytes 3145736 | tf_op jit(solution)/shard_map/ppermute | solution.py:21
  2.6 1.3 %collective-permute-start.2 = (bf16[128,4096]{1,0:T(8,128)(2,1)}, bf16[128,4096]{1,0:T(8,128)(2,1)S(1)}, u32[]{:S(2)}, u32[]{:S(2)}) collective-permute-start(bf16[128,4096]{1,0:T(8,128)(2,1)} %refs_3_.1), channel_id=1, source_target_pairs={{0,2},{4,6},{8,10},{12,14},{16,18},{20,22},{24,26},{28,30},{1,3},{... | collective-permute-start | bytes 3145736 | tf_op jit(solution)/shard_map/ppermute | solution.py:21
  4.7 0.8 %select_reduce_fusion = s32[129]{0:T(256)S(1)} fusion(s32[10]{0:T(128)} %param.10, s32[129]{0:T(256)S(1)} %iota_add_fusion, s32[10]{0:T(128)S(1)} %bitcast.18), kind=kLoop, calls=%fused_computation | loop fusion | flops 3741 | bytes 1112 | tf_op jit(solution)/shard_map/reduce_sum | solution.py:32
  9.9 5.2 %taps.1 = (bf16[32,128,1024]{2,1,0:T(8,128)(2,1)S(1)}, bf16[32,128,1024]{2,1,0:T(8,128)(2,1)S(1)}) custom-call(s32[4]{0:T(128)S(1)} %pad_add_fusion.facts_ref.refs_0_, s32[128,1]{1,0:T(8,128)S(1)} %copy.11.st_ref.refs_1_, bf16[256,128]{1,0:T(8,128)(2,1)S(1)} %copy-done.6), custom_call_target="tpu_custom_call" | custom-call | flops 1048576 | bytes 65536 | tf_op jit(solution)/shard_map/taps/pallas_call | solution.py:327
  15.1 2.5 %collective-permute-done.refs_1_ = bf16[128,4096]{1,0:T(8,128)(2,1)S(1)} collective-permute-done((bf16[128,4096]{1,0:T(8,128)(2,1)}, bf16[128,4096]{1,0:T(8,128)(2,1)S(1)}, u32[]{:S(2)}, u32[]{:S(2)}) %collective-permute-start) | collective-permute-done | bytes 1048608 | tf_op jit(solution)/shard_map/ppermute | solution.py:21
  17.6 1.9 %collective-permute-start.1 = (bf16[128,4096]{1,0:T(8,128)(2,1)}, bf16[128,4096]{1,0:T(8,128)(2,1)S(1)}, u32[]{:S(2)}, u32[]{:S(2)}) collective-permute-start(bf16[128,4096]{1,0:T(8,128)(2,1)} %refs_3_.1), channel_id=1, source_target_pairs={{2,4},{6,8},{10,12},{14,16},{18,20},{22,24},{26,28},{3,5},{7,9},{1... | collective-permute-start | bytes 3145736 | tf_op jit(solution)/shard_map/ppermute | solution.py:21
  19.6 1.2 %copy-done = bf16[128,4096]{1,0:T(8,128)(2,1)S(1)} copy-done((bf16[128,4096]{1,0:T(8,128)(2,1)S(1)}, bf16[128,4096]{1,0:T(8,128)(2,1)}, u32[]{:S(2)}) %copy-start) | copy-done | bytes 1048600
  20.8 1.2 %copy-done.2 = bf16[128,4096]{1,0:T(8,128)(2,1)S(1)} copy-done((bf16[128,4096]{1,0:T(8,128)(2,1)S(1)}, bf16[128,4096]{1,0:T(8,128)(2,1)}, u32[]{:S(2)}) %copy-start.2) | copy-done | bytes 1048600
  22.0 1.2 %copy-done.4 = bf16[128,4096]{1,0:T(8,128)(2,1)S(1)} copy-done((bf16[128,4096]{1,0:T(8,128)(2,1)S(1)}, bf16[128,4096]{1,0:T(8,128)(2,1)}, u32[]{:S(2)}) %copy-start.4) | copy-done | bytes 1048600
  23.3 3.1 %share.2 = (bf16[17,128,128]{2,1,0:T(8,128)(2,1)S(1)}, bf16[128,4096]{1,0:T(8,128)(2,1)S(1)}) custom-call(s32[4]{0:T(128)S(1)} %pad_add_fusion.facts_ref.refs_0_, bf16[128,4096]{1,0:T(8,128)(2,1)S(1)} %collective-permute-done.refs_1_, bf16[128,4096]{1,0:T(8,128)(2,1)S(1)} %copy-done.2, bf16[128,4096]{1,0:T(8,128)(2,1)S(1)} %collective-permute-done.2.refs_3_.refs_11_, ...), custom_call_target="tpu_custom_call" | custom-call | flops 1048576 | bytes 65536 | tf_op jit(solution)/shard_map/share/pallas_call | solution.py:327
  26.4 3.1 %share.3 = (bf16[17,128,128]{2,1,0:T(8,128)(2,1)S(1)}, bf16[128,4096]{1,0:T(8,128)(2,1)S(1)}) custom-call(s32[4]{0:T(128)S(1)} %pad_add_fusion.facts_ref.refs_0_, bf16[128,4096]{1,0:T(8,128)(2,1)S(1)} %collective-permute-done.refs_1_, bf16[128,4096]{1,0:T(8,128)(2,1)S(1)} %copy-done.2, ...), custom_call_target="tpu_custom_call", output_to_operand_aliasing={{1}: (7, {})} | custom-call | flops 1048576 | bytes 65536 | tf_op jit(solution)/shard_map/share/pallas_call | solution.py:327
  29.4 1.3 %collective-permute-start.5 = (bf16[17,128,128]{2,1,0:T(8,128)(2,1)S(1)}, bf16[17,128,128]{2,1,0:T(8,128)(2,1)S(1)}, u32[]{:S(2)}, u32[]{:S(2)}) collective-permute-start(bf16[17,128,128]{2,1,0:T(8,128)(2,1)S(1)} %get-tuple-element.21), channel_id=1, source_target_pairs={{2,4},{6,8},{10,12},{14,16},{18,20},{22,24},{26,28},{3,5},{7,9},{1... | collective-permute-start | bytes 1671176 | tf_op jit(solution)/shard_map/ppermute | solution.py:21
  30.8 1.3 %collective-permute-start.4 = (bf16[17,128,128]{2,1,0:T(8,128)(2,1)S(1)}, bf16[17,128,128]{2,1,0:T(8,128)(2,1)S(1)}, u32[]{:S(2)}, u32[]{:S(2)}) collective-permute-start(bf16[17,128,128]{2,1,0:T(8,128)(2,1)S(1)} %get-tuple-element.19), channel_id=1, source_target_pairs={{2,4},{6,8},{10,12},{14,16},{18,20},{22,24},{26,28},{3,5},{7,9},{1... | collective-permute-start | bytes 1671176 | tf_op jit(solution)/shard_map/ppermute | solution.py:21
  32.1 1.3 %collective-permute-start.7 = (bf16[128,4096]{1,0:T(8,128)(2,1)S(1)}, bf16[128,4096]{1,0:T(8,128)(2,1)S(1)}, u32[]{:S(2)}, u32[]{:S(2)}) collective-permute-start(bf16[128,4096]{1,0:T(8,128)(2,1)S(1)} %copy-done.2), channel_id=1, source_target_pairs={{0,2},{4,6},{8,10},{12,14},{16,18},{20,22},{24,26},{28,30},{1,3},{... | collective-permute-start | bytes 3145736 | tf_op jit(solution)/shard_map/ppermute | solution.py:21
  33.4 1.3 %collective-permute-start.8 = (bf16[128,4096]{1,0:T(8,128)(2,1)S(1)}, bf16[128,4096]{1,0:T(8,128)(2,1)S(1)}, u32[]{:S(2)}, u32[]{:S(2)}) collective-permute-start(bf16[128,4096]{1,0:T(8,128)(2,1)S(1)} %collective-permute-done.1.refs_5_.refs_2_), channel_id=1, source_target_pairs={{0,2},{4,6},{8,10},{12,14},{16,18},{20,22},{24,26},{28,30},{1,3},{... | collective-permute-start | bytes 3145736 | tf_op jit(solution)/shard_map/ppermute | solution.py:21
  34.7 5.2 %collective-permute-start.6 = (bf16[128,4096]{1,0:T(8,128)(2,1)S(1)}, bf16[128,4096]{1,0:T(8,128)(2,1)S(1)}, u32[]{:S(2)}, u32[]{:S(2)}) collective-permute-start(bf16[128,4096]{1,0:T(8,128)(2,1)S(1)} %get-tuple-element.22), channel_id=1, source_target_pairs={{2,4},{6,8},{10,12},{14,16},{18,20},{22,24},{26,28},{3,5},{7,9},{1... | collective-permute-start | bytes 3145736 | tf_op jit(solution)/shard_map/ppermute | solution.py:21
  40.0 1.3 %collective-permute-start.10 = (bf16[17,128,128]{2,1,0:T(8,128)(2,1)S(1)}, bf16[17,128,128]{2,1,0:T(8,128)(2,1)S(1)}, u32[]{:S(2)}, u32[]{:S(2)}) collective-permute-start(bf16[17,128,128]{2,1,0:T(8,128)(2,1)S(1)} %collective-permute-done.5.refs_7_.refs_9_.refs_4_), channel_id=1, source_target_pairs={{0,2},{4,6},{8,10},{12,14},{16,18},{20,22},{24,26},{28,30},{1,3},{... | collective-permute-start | bytes 1671176 | tf_op jit(solution)/shard_map/ppermute | solution.py:21
  41.3 2.1 %collective-permute-done.4.refs_6_.refs_8_.refs_3_ = bf16[17,128,128]{2,1,0:T(8,128)(2,1)S(1)} collective-permute-done((bf16[17,128,128]{2,1,0:T(8,128)(2,1)S(1)}, bf16[17,128,128]{2,1,0:T(8,128)(2,1)S(1)}, u32[]{:S(2)}, u32[]{:S(2)}) %collective-permute-start.4) | collective-permute-done | bytes 557088 | tf_op jit(solution)/shard_map/ppermute | solution.py:21
  43.4 1.3 %collective-permute-start.9 = (bf16[17,128,128]{2,1,0:T(8,128)(2,1)S(1)}, bf16[17,128,128]{2,1,0:T(8,128)(2,1)S(1)}, u32[]{:S(2)}, u32[]{:S(2)}) collective-permute-start(bf16[17,128,128]{2,1,0:T(8,128)(2,1)S(1)} %collective-permute-done.4.refs_6_.refs_8_.refs_3_), channel_id=1, source_target_pairs={{0,2},{4,6},{8,10},{12,14},{16,18},{20,22},{24,26},{28,30},{1,3},{... | collective-permute-start | bytes 1671176 | tf_op jit(solution)/shard_map/ppermute | solution.py:21
  44.7 4.5 %collective-permute-done.9.refs_14_ = bf16[17,128,128]{2,1,0:T(8,128)(2,1)S(1)} collective-permute-done((bf16[17,128,128]{2,1,0:T(8,128)(2,1)S(1)}, bf16[17,128,128]{2,1,0:T(8,128)(2,1)S(1)}, u32[]{:S(2)}, u32[]{:S(2)}) %collective-permute-start.9) | collective-permute-done | bytes 557088 | tf_op jit(solution)/shard_map/ppermute | solution.py:21
  49.2 7.5 %attention.1 = (bf16[32,128,128]{2,1,0:T(8,128)(2,1)S(1)}, bf16[32,128,128]{2,1,0:T(8,128)(2,1)S(1)}, f32[128,128]{1,0:T(8,128)S(1)}, f32[128,128]{1,0:T(8,128)S(1)}) custom-call(s32[4]{0:T(128)S(1)} %pad_add_fusion.facts_ref.refs_0_, s32[128,1]{1,0:T(8,128)S(1)} %copy.11.st_ref.refs_1_, bf16[128,4096]{1,0:T(8,128)(2,1)S(1)} %copy-done.3, ...), custom_call_target="tpu_custom_call" | custom-call | flops 1048576 | bytes 65536 | tf_op jit(solution)/shard_map/attention/pallas_call | solution.py:327
  56.8 4.3 %own.1.refs_8_ = f32[128,4096]{1,0:T(8,128)S(1)} custom-call(s32[4]{0:T(128)S(1)} %pad_add_fusion.facts_ref.refs_0_, bf16[32,128,128]{2,1,0:T(8,128)(2,1)S(1)} %get-tuple-element.26.refs_1_, f32[128,128]{1,0:T(8,128)S(1)} %get-tuple-element.27.refs_2_, bf16[32,128,1024]{2,1,0:T(8,128)(2,1)S(1)} %get-tuple-element.28.refs_3_, f32[1,4096]{1,0:T(1,128)S(1)} %bitcast.15, ...), custom_call_target="tpu_custom_call" | custom-call | flops 1048576 | bytes 65536 | tf_op jit(solution)/shard_map/own/pallas_call | solution.py:327
  61.1 6.4 %finish.1 = bf16[128,4096]{1,0:T(8,128)(2,1)} custom-call(s32[4]{0:T(128)S(1)} %pad_add_fusion.facts_ref.refs_0_, s32[128,1]{1,0:T(8,128)S(1)} %copy.11.st_ref.refs_1_, bf16[128,4096]{1,0:T(8,128)(2,1)S(1)} %collective-permute-done.1.refs_5_.refs_2_, bf16[17,128,128]{2,1,0:T(8,128)(2,1)S(1)} %collective-permute-done.4.refs_6_.refs_8_.refs_3_, ...), custom_call_target="tpu_custom_call" | custom-call | flops 1048576 | bytes 65536 | tf_op jit(solution)/shard_map/finish/pallas_call | solution.py:327
  (32 shorter events, 3.2 us)
Async XLA Ops:
  0.0 19.6 %collective-permute-start.3 = (bf16[128,4096]{1,0:T(8,128)(2,1)}, bf16[128,4096]{1,0:T(8,128)(2,1)S(1)}, u32[]{:S(2)}, u32[]{:S(2)}) collective-permute-start(bf16[128,4096]{1,0:T(8,128)(2,1)} %refs_4_.5), channel_id=1, source_target_pairs={{0,2},{4,6},{8,10},{12,14},{16,18},{20,22},{24,26},{28,30},{1,3},{... | collective-permute-start | bytes 3145736 | tf_op jit(solution)/shard_map/ppermute | solution.py:21
  1.3 16.3 %collective-permute-start = (bf16[128,4096]{1,0:T(8,128)(2,1)}, bf16[128,4096]{1,0:T(8,128)(2,1)S(1)}, u32[]{:S(2)}, u32[]{:S(2)}) collective-permute-start(bf16[128,4096]{1,0:T(8,128)(2,1)} %refs_2_.5), channel_id=1, source_target_pairs={{4,2},{8,6},{12,10},{16,14},{20,18},{24,22},{28,26},{5,3},{9,7},{1... | collective-permute-start | bytes 3145736 | tf_op jit(solution)/shard_map/ppermute | solution.py:21
  2.6 17.0 %collective-permute-start.2 = (bf16[128,4096]{1,0:T(8,128)(2,1)}, bf16[128,4096]{1,0:T(8,128)(2,1)S(1)}, u32[]{:S(2)}, u32[]{:S(2)}) collective-permute-start(bf16[128,4096]{1,0:T(8,128)(2,1)} %refs_3_.1), channel_id=1, source_target_pairs={{0,2},{4,6},{8,10},{12,14},{16,18},{20,22},{24,26},{28,30},{1,3},{... | collective-permute-start | bytes 3145736 | tf_op jit(solution)/shard_map/ppermute | solution.py:21
  9.0 0.8 %copy-start.6 = (bf16[256,128]{1,0:T(8,128)(2,1)S(1)}, bf16[256,128]{1,0:T(8,128)(2,1)}, u32[]{:S(2)}) copy-start(bf16[256,128]{1,0:T(8,128)(2,1)} %filters_ref.1) | copy-start | bytes 196612
  17.6 15.8 %collective-permute-start.1 = (bf16[128,4096]{1,0:T(8,128)(2,1)}, bf16[128,4096]{1,0:T(8,128)(2,1)S(1)}, u32[]{:S(2)}, u32[]{:S(2)}) collective-permute-start(bf16[128,4096]{1,0:T(8,128)(2,1)} %refs_3_.1), channel_id=1, source_target_pairs={{2,4},{6,8},{10,12},{14,16},{18,20},{22,24},{26,28},{3,5},{7,9},{1... | collective-permute-start | bytes 3145736 | tf_op jit(solution)/shard_map/ppermute | solution.py:21
  19.6 1.2 %copy-start = (bf16[128,4096]{1,0:T(8,128)(2,1)S(1)}, bf16[128,4096]{1,0:T(8,128)(2,1)}, u32[]{:S(2)}) copy-start(bf16[128,4096]{1,0:T(8,128)(2,1)} %refs_3_.1) | copy-start | bytes 3145732
  20.8 1.2 %copy-start.2 = (bf16[128,4096]{1,0:T(8,128)(2,1)S(1)}, bf16[128,4096]{1,0:T(8,128)(2,1)}, u32[]{:S(2)}) copy-start(bf16[128,4096]{1,0:T(8,128)(2,1)} %refs_2_.5) | copy-start | bytes 3145732
  22.0 1.2 %copy-start.4 = (bf16[128,4096]{1,0:T(8,128)(2,1)S(1)}, bf16[128,4096]{1,0:T(8,128)(2,1)}, u32[]{:S(2)}) copy-start(bf16[128,4096]{1,0:T(8,128)(2,1)} %refs_4_.5) | copy-start | bytes 3145732
  23.3 26.0 %copy-start.1 = (bf16[128,4096]{1,0:T(8,128)(2,1)S(1)}, bf16[128,4096]{1,0:T(8,128)(2,1)}, u32[]{:S(2)}) copy-start(bf16[128,4096]{1,0:T(8,128)(2,1)} %refs_3_.1) | copy-start | bytes 3145732
  23.3 26.0 %copy-start.3 = (bf16[128,4096]{1,0:T(8,128)(2,1)S(1)}, bf16[128,4096]{1,0:T(8,128)(2,1)}, u32[]{:S(2)}) copy-start(bf16[128,4096]{1,0:T(8,128)(2,1)} %refs_2_.5) | copy-start | bytes 3145732
  23.3 26.0 %copy-start.5 = (bf16[128,4096]{1,0:T(8,128)(2,1)S(1)}, bf16[128,4096]{1,0:T(8,128)(2,1)}, u32[]{:S(2)}) copy-start(bf16[128,4096]{1,0:T(8,128)(2,1)} %refs_4_.5) | copy-start | bytes 3145732
  26.3 30.4 %copy-start.7 = (f32[4096]{0:T(1024)S(1)}, f32[4096]{0:T(1024)}, u32[]{:S(2)}) copy-start(f32[4096]{0:T(1024)} %param.11) | copy-start | bytes 49156
  26.3 30.4 %copy-start.8 = (f32[4096]{0:T(1024)S(1)}, f32[4096]{0:T(1024)}, u32[]{:S(2)}) copy-start(f32[4096]{0:T(1024)} %param.13) | copy-start | bytes 49156
  29.4 10.5 %collective-permute-start.5 = (bf16[17,128,128]{2,1,0:T(8,128)(2,1)S(1)}, bf16[17,128,128]{2,1,0:T(8,128)(2,1)S(1)}, u32[]{:S(2)}, u32[]{:S(2)}) collective-permute-start(bf16[17,128,128]{2,1,0:T(8,128)(2,1)S(1)} %get-tuple-element.21), channel_id=1, source_target_pairs={{2,4},{6,8},{10,12},{14,16},{18,20},{22,24},{26,28},{3,5},{7,9},{1... | collective-permute-start | bytes 1671176 | tf_op jit(solution)/shard_map/ppermute | solution.py:21
  30.8 12.6 %collective-permute-start.4 = (bf16[17,128,128]{2,1,0:T(8,128)(2,1)S(1)}, bf16[17,128,128]{2,1,0:T(8,128)(2,1)S(1)}, u32[]{:S(2)}, u32[]{:S(2)}) collective-permute-start(bf16[17,128,128]{2,1,0:T(8,128)(2,1)S(1)} %get-tuple-element.19), channel_id=1, source_target_pairs={{2,4},{6,8},{10,12},{14,16},{18,20},{22,24},{26,28},{3,5},{7,9},{1... | collective-permute-start | bytes 1671176 | tf_op jit(solution)/shard_map/ppermute | solution.py:21
  32.1 12.5 %collective-permute-start.7 = (bf16[128,4096]{1,0:T(8,128)(2,1)S(1)}, bf16[128,4096]{1,0:T(8,128)(2,1)S(1)}, u32[]{:S(2)}, u32[]{:S(2)}) collective-permute-start(bf16[128,4096]{1,0:T(8,128)(2,1)S(1)} %copy-done.2), channel_id=1, source_target_pairs={{0,2},{4,6},{8,10},{12,14},{16,18},{20,22},{24,26},{28,30},{1,3},{... | collective-permute-start | bytes 3145736 | tf_op jit(solution)/shard_map/ppermute | solution.py:21
  33.4 15.8 %collective-permute-start.8 = (bf16[128,4096]{1,0:T(8,128)(2,1)S(1)}, bf16[128,4096]{1,0:T(8,128)(2,1)S(1)}, u32[]{:S(2)}, u32[]{:S(2)}) collective-permute-start(bf16[128,4096]{1,0:T(8,128)(2,1)S(1)} %collective-permute-done.1.refs_5_.refs_2_), channel_id=1, source_target_pairs={{0,2},{4,6},{8,10},{12,14},{16,18},{20,22},{24,26},{28,30},{1,3},{... | collective-permute-start | bytes 3145736 | tf_op jit(solution)/shard_map/ppermute | solution.py:21
  34.7 26.4 %collective-permute-start.6 = (bf16[128,4096]{1,0:T(8,128)(2,1)S(1)}, bf16[128,4096]{1,0:T(8,128)(2,1)S(1)}, u32[]{:S(2)}, u32[]{:S(2)}) collective-permute-start(bf16[128,4096]{1,0:T(8,128)(2,1)S(1)} %get-tuple-element.22), channel_id=1, source_target_pairs={{2,4},{6,8},{10,12},{14,16},{18,20},{22,24},{26,28},{3,5},{7,9},{1... | collective-permute-start | bytes 3145736 | tf_op jit(solution)/shard_map/ppermute | solution.py:21
  40.0 4.7 %collective-permute-start.10 = (bf16[17,128,128]{2,1,0:T(8,128)(2,1)S(1)}, bf16[17,128,128]{2,1,0:T(8,128)(2,1)S(1)}, u32[]{:S(2)}, u32[]{:S(2)}) collective-permute-start(bf16[17,128,128]{2,1,0:T(8,128)(2,1)S(1)} %collective-permute-done.5.refs_7_.refs_9_.refs_4_), channel_id=1, source_target_pairs={{0,2},{4,6},{8,10},{12,14},{16,18},{20,22},{24,26},{28,30},{1,3},{... | collective-permute-start | bytes 1671176 | tf_op jit(solution)/shard_map/ppermute | solution.py:21
  43.4 5.8 %collective-permute-start.9 = (bf16[17,128,128]{2,1,0:T(8,128)(2,1)S(1)}, bf16[17,128,128]{2,1,0:T(8,128)(2,1)S(1)}, u32[]{:S(2)}, u32[]{:S(2)}) collective-permute-start(bf16[17,128,128]{2,1,0:T(8,128)(2,1)S(1)} %collective-permute-done.4.refs_6_.refs_8_.refs_3_), channel_id=1, source_target_pairs={{0,2},{4,6},{8,10},{12,14},{16,18},{20,22},{24,26},{28,30},{1,3},{... | collective-permute-start | bytes 1671176 | tf_op jit(solution)/shard_map/ppermute | solution.py:21

commit v5 on v0

v5 whole, which is shorter than its diff:
```python
import math

import jax
import jax.numpy as jnp
from jax import lax
from jax.experimental import pallas as pl
from jax.experimental.pallas import tpu as pltpu
from jax.sharding import PartitionSpec as P

HEAD_DIM = 128
LANES = 128
NEG = -1e30
FACTOR = 1.0 / math.sqrt(HEAD_DIM) * math.log2(math.e)
CONTRACT_LAST = (((1,), (1,)), ((), ()))
VMEM_BYTES = 16 * 2**20
UNROLL = 8

ODD, BEFORE, NEXT_BEFORE, NEXT_AFTER = range(4)


def permuted(x, pairs):
    return lax.ppermute(x, "ctx", pairs)


def after(x, *others):
    return lax.optimization_barrier((x, *others))[0]


def places(lengths, first_row, count):
    ends = jnp.cumsum(lengths)
    position = first_row + jnp.arange(count + 1, dtype=jnp.int32)
    passed = ends[None, :] <= position[:, None]
    starts = jnp.sum(jnp.where(passed, lengths[None, :], 0), axis=1) - first_row
    past = jnp.min(jnp.where(passed[count], jnp.int32(2**30), ends)) - first_row - count
    odd = (first_row // count) % 2
    facts = jnp.stack([odd, -starts[0], count - starts[count], past]).astype(jnp.int32)
    return starts[:count].astype(jnp.int32).reshape(count, 1), facts


def bias_of(rows, columns, row_first, key_first, start):
    row = lax.broadcasted_iota(jnp.int32, (rows, columns), 0) + row_first
    key = lax.broadcasted_iota(jnp.int32, (rows, columns), 1) + key_first
    return jnp.where((key >= start) & (key <= row), 0.0, NEG)


def scores_of(query, key):
    return lax.dot_general(query, key, CONTRACT_LAST, preferred_element_type=jnp.float32)


def raised(scores, bias):
    s = scores + bias
    top = jnp.max(s, axis=1, keepdims=True)
    return jnp.exp2((s - top) * FACTOR).astype(jnp.bfloat16), top


def summed(weights, value):
    ones = jnp.ones(value.shape, jnp.bfloat16)
    o = jnp.dot(weights, jnp.concatenate([value, ones], axis=1), preferred_element_type=jnp.float32)
    return o[:, :LANES], o[:, LANES:]


def columns(head):
    if isinstance(head, int):
        return slice(head * HEAD_DIM, (head + 1) * HEAD_DIM)
    return pl.ds(pl.multiple_of(head * HEAD_DIM, HEAD_DIM), HEAD_DIM)


def attend(heads, query, key, value, bias, use):
    ahead = scores_of(query(0), key(0))
    held = None
    for h in range(heads):
        now = ahead
        if h + 1 < heads:
            ahead = scores_of(query(h + 1), key(h + 1))
        weights, top = raised(now, bias)
        if held is not None:
            use(h - 1, *summed(held[0], value(h - 1)), held[1])
        held = weights, top
    use(heads - 1, *summed(held[0], value(heads - 1)), held[1])


def each(count, body):
    @pl.loop(0, count // UNROLL)
    def _(step):
        body(step * UNROLL)


def taps_kernel(facts_ref, st_ref, filters_ref, far_ref, near_ref, keep, lines):
    rows = st_ref.shape[0]
    tiles = far_ref.shape[0]
    groups = filters_ref.shape[0] // tiles
    st = st_ref[...]
    row = lax.broadcasted_iota(jnp.int32, (rows, 2 * rows), 0)
    key = lax.broadcasted_iota(jnp.int32, (rows, 2 * rows), 1) - rows
    keep[...] = jnp.where((key >= st) & (key <= row) & (key > row - rows), 1.0, 0.0).astype(jnp.bfloat16)
    tap = lax.broadcasted_iota(jnp.int32, (rows, rows), 0)
    place = lax.broadcasted_iota(jnp.int32, (rows, rows), 1)
    turn = jnp.where((tap + place == 0) | (tap + place == rows), 1.0, 0.0).astype(jnp.bfloat16)
    lines[...] = jnp.dot(filters_ref[...], turn, preferred_element_type=jnp.float32).reshape(lines.shape)

    @pl.loop(0, tiles)
    def _(c):
        some = lines[c]
        for g in range(groups):
            line = jnp.broadcast_to(some[g : g + 1], (rows, rows))
            ring = pltpu.roll(line, 0, 1, stride=1, stride_axis=0).astype(jnp.bfloat16)
            cols = slice(g * rows, (g + 1) * rows)
            far_ref[c, :, cols] = ring * keep[:, :rows]
            near_ref[c, :, cols] = ring * keep[:, rows:]


def share_kernel(facts_ref, qb_ref, q_ref, kn_ref, ko_ref, vn_ref, vo_ref, b0_ref, b1_ref, c_ref, bias, stat_ref):
    rows = q_ref.shape[0]
    before = facts_ref[NEXT_BEFORE]
    past = facts_ref[NEXT_AFTER]
    odd = facts_ref[ODD] == 1
    half = b0_ref.shape[0] - 1

    @pl.when(odd & (before <= rows))
    def _():
        c_ref[...] = q_ref[...]
        for part, b_ref in enumerate((b0_ref, b1_ref)):

            @pl.loop(0, half)
            def _(h):
                b_ref[h] = vo_ref[:, columns(part * half + h)]

    @pl.when(odd & (before > rows))
    def _():
        bias[:rows] = bias_of(rows, 2 * rows, rows, -rows, rows - before)
        bias[rows:] = bias_of(rows, 2 * rows, 0, -rows, rows - before)
        lane = lax.broadcasted_iota(jnp.int32, (rows, LANES), 1)
        ours = lax.broadcasted_iota(jnp.int32, (rows, LANES), 0) < past
        for part, b_ref in enumerate((b0_ref, b1_ref)):
            stat_ref[...] = jnp.zeros_like(stat_ref)

            def heads(first):
                at = lambda h: columns(part * half + first + h)
                stat = [stat_ref[...]]

                def use(h, o, l, top):
                    o = (o / l).astype(jnp.bfloat16)
                    b_ref[first + h] = o[:rows]
                    c_ref[:, at(h)] = o[rows:]
                    lse = jnp.where(ours, top[:rows] * FACTOR + jnp.log2(l[:rows]), NEG)
                    stat[0] = jnp.where(lane == first + h, lse, stat[0])

                attend(
                    UNROLL,
                    lambda h: jnp.concatenate([qb_ref[:, at(h)], q_ref[:, at(h)]], axis=0),
                    lambda h: jnp.concatenate([kn_ref[:, at(h)], ko_ref[:, at(h)]], axis=0),
                    lambda h: jnp.concatenate([vn_ref[:, at(h)], vo_ref[:, at(h)]], axis=0),
                    bias[...],
                    use,
                )
                stat_ref[...] = stat[0]

            each(half, heads)
            total = stat_ref[...]
            high = total.astype(jnp.bfloat16).astype(jnp.float32)
            middle = (total - high).astype(jnp.bfloat16).astype(jnp.float32)
            low = total - high - middle
            packed = high + pltpu.roll(middle, half, 1) + pltpu.roll(low, 2 * half, 1)
            b_ref[half] = packed.astype(jnp.bfloat16)


def attention_kernel(part, facts_ref, st_ref, q_ref, ko_ref, vo_ref, kp_ref, vp_ref, qn_ref, kn_ref, vn_ref, kf_ref, vf_ref, att_ref, near_ref, sq_ref, sq_near_ref, bias_own, bias_prev):
    rows = q_ref.shape[0]
    odd = facts_ref[ODD] == 1
    half = att_ref.shape[0]
    low = jnp.where((facts_ref[ODD] == 0) & (facts_ref[BEFORE] > rows), 0, -(2**20))
    bias_own[...] = bias_of(rows, 3 * rows, 0, -2 * rows, jnp.maximum(st_ref[...], low))
    sq_ref[...] = jnp.zeros_like(sq_ref)
    sq_near_ref[...] = jnp.zeros_like(sq_near_ref)

    @pl.when(odd)
    def _():
        bias_prev[...] = bias_of(rows, 2 * rows, -rows, -2 * rows, st_ref[0:1, :])

        def heads(first):
            at = lambda h: columns(part * half + first + h)
            squares = [sq_ref[...], sq_near_ref[...]]

            def use_own(h, o, l, top):
                a = (o / l).astype(jnp.bfloat16)
                att_ref[first + h] = a
                a = a.astype(jnp.float32)
                squares[0] += a * a

            def use_near(h, o, l, top):
                a = (o / l).astype(jnp.bfloat16)
                near_ref[first + h] = a
                a = a.astype(jnp.float32)
                squares[1] += a * a

            attend(
                UNROLL,
                lambda h: q_ref[:, at(h)],
                lambda h: jnp.concatenate([kf_ref[:, at(h)], kn_ref[:, at(h)], ko_ref[:, at(h)]], axis=0),
                lambda h: jnp.concatenate([vf_ref[first + h], vn_ref[:, at(h)], vo_ref[:, at(h)]], axis=0),
                bias_own[...],
                use_own,
            )
            attend(
                UNROLL,
                lambda h: qn_ref[:, at(h)],
                lambda h: jnp.concatenate([kf_ref[:, at(h)], kn_ref[:, at(h)]], axis=0),
                lambda h: jnp.concatenate([vf_ref[first + h], vn_ref[:, at(h)]], axis=0),
                bias_prev[...],
                use_near,
            )
            sq_ref[...] = squares[0]
            sq_near_ref[...] = squares[1]

        each(half, heads)

    @pl.when(jnp.logical_not(odd))
    def _():
        lane = lax.broadcasted_iota(jnp.int32, (rows, LANES), 1)

        def heads(first):
            at = lambda h: columns(part * half + first + h)
            packed = vp_ref[half].astype(jnp.float32)
            stat = packed + pltpu.roll(packed, LANES - half, 1) + pltpu.roll(packed, LANES - 2 * half, 1)
            stat = jnp.where(facts_ref[BEFORE] > rows, stat, NEG)
            squares = [sq_ref[...]]

            def use(h, o, l, top):
                lse = jnp.sum(jnp.where(lane == first + h, stat, 0.0), axis=1, keepdims=True)
                top = top * FACTOR
                high = jnp.maximum(top, lse)
                here = jnp.exp2(top - high)
                there = jnp.exp2(lse - high)
                o = o * here + vp_ref[first + h].astype(jnp.float32) * there
                a = (o / (l * here + there)).astype(jnp.bfloat16)
                att_ref[first + h] = a
                a = a.astype(jnp.float32)
                squares[0] += a * a

            attend(
                UNROLL,
                lambda h: q_ref[:, at(h)],
                lambda h: jnp.concatenate([kp_ref[:, at(h)], ko_ref[:, at(h)]], axis=0),
                lambda h: jnp.concatenate([vp_ref[first + h], vo_ref[:, at(h)]], axis=0),
                bias_own[:, rows:],
                use,
            )
            sq_ref[...] = squares[0]

        each(half, heads)


def scale_of(squares, width):
    total = jnp.sum(squares, axis=1, keepdims=True)
    return jnp.broadcast_to(lax.rsqrt(total * (1.0 / width) + 1e-06), squares.shape)


def spread(x, groups):
    size = LANES // groups
    lane_group = lax.broadcasted_iota(jnp.int32, x.shape, 1) // size
    return jnp.concatenate([jnp.where(lane_group == g, x, jnp.zeros_like(x)) for g in range(groups)], axis=0)


def own_kernel(facts_ref, att0_ref, att1_ref, sq0_ref, sq1_ref, taps_ref, gain_ref, bypass_ref, out_ref, scale):
    half, rows, _ = att0_ref.shape
    scale[...] = scale_of(sq0_ref[...] + sq1_ref[...], 2 * half * LANES)
    for part, att_ref in enumerate((att0_ref, att1_ref)):

        def tiles(first):
            for c in range(UNROLL):
                tile = part * half + first + c
                cols = columns(tile)
                x = (att_ref[first + c].astype(jnp.float32) * scale[...] * gain_ref[:, cols]).astype(jnp.bfloat16)
                y = jnp.dot(taps_ref[tile], spread(x, taps_ref.shape[2] // rows), preferred_element_type=jnp.float32)
                out_ref[:, cols] = y + bypass_ref[:, cols] * x.astype(jnp.float32)

        each(half, tiles)


def finish_kernel(facts_ref, st_ref, kp_ref, vp0_ref, vp1_ref, c_ref, near0_ref, near1_ref, sq0_ref, sq1_ref, part_ref, taps_ref, gain_ref, out_ref, prev, squares, scale, bias):
    rows = st_ref.shape[0]
    half = near0_ref.shape[0]
    width = prev.shape[0] * LANES
    odd = facts_ref[ODD] == 1
    shared = facts_ref[BEFORE] > rows

    @pl.when(odd)
    def _():
        squares[...] = sq0_ref[...] + sq1_ref[...]
        for part, near_ref in enumerate((near0_ref, near1_ref)):

            @pl.loop(0, half)
            def _(h):
                prev[part * half + h] = near_ref[h]

    @pl.when(jnp.logical_not(odd) & shared)
    def _():
        squares[...] = jnp.zeros_like(squares)

        def heads(first):
            total = squares[...]
            for h in range(UNROLL):
                a = c_ref[:, columns(first + h)]
                prev[first + h] = a
                a = a.astype(jnp.float32)
                total += a * a
            squares[...] = total

        each(2 * half, heads)

    @pl.when(jnp.logical_not(odd) & jnp.logical_not(shared))
    def _():
        squares[...] = jnp.zeros_like(squares)
        bias[...] = bias_of(rows, rows, -rows, -rows, st_ref[0:1, :])
        for part, vp_ref in enumerate((vp0_ref, vp1_ref)):

            def heads(first):
                at = lambda h: columns(part * half + first + h)
                total = [squares[...]]

                def use(h, o, l, top):
                    a = (o / l).astype(jnp.bfloat16)
                    prev[part * half + first + h] = a
                    a = a.astype(jnp.float32)
                    total[0] += a * a

                attend(UNROLL, lambda h: c_ref[:, at(h)], lambda h: kp_ref[:, at(h)], lambda h: vp_ref[first + h], bias[...], use)
                squares[...] = total[0]

            each(half, heads)

    scale[...] = scale_of(squares[...], width)

    def tiles(first):
        for c in range(UNROLL):
            cols = columns(first + c)
            x = (prev[first + c].astype(jnp.float32) * scale[...] * gain_ref[:, cols]).astype(jnp.bfloat16)
            y = jnp.dot(taps_ref[first + c], spread(x, taps_ref.shape[2] // rows), preferred_element_type=jnp.float32)
            out_ref[:, cols] = (y + part_ref[:, cols]).astype(jnp.bfloat16)

    each(2 * half, tiles)


def run(kernel, name, facts, out_shape, scratch, args):
    many = isinstance(out_shape, tuple)
    vmem = pl.BlockSpec(memory_space=pltpu.VMEM)
    return pl.pallas_call(
        kernel,
        out_shape=out_shape,
        in_specs=[pl.BlockSpec(memory_space=pltpu.SMEM)] + [vmem] * len(args),
        out_specs=(vmem,) * len(out_shape) if many else vmem,
        scratch_shapes=scratch,
        compiler_params=pltpu.CompilerParams(vmem_limit_bytes=VMEM_BYTES),
        cost_estimate=pl.CostEstimate(flops=2**20, bytes_accessed=2**16, transcendentals=0),
        name=name,
    )(facts, *args)


def shards(queries, key_rows, value_rows, lengths, norm_gain, filters, bypass):
    rows, width = queries.shape
    heads = width // HEAD_DIM
    half = heads // 2
    groups, taps = filters.shape
    n = lax.axis_size("ctx")
    st, facts = places(lengths, lax.axis_index("ctx") * rows, rows)

    back = [(i, i - 1) for i in range(2, n, 2)]
    within = [(i, i + 1) for i in range(0, n - 1, 2)]
    across = [(i, i + 1) for i in range(1, n - 1, 2)]

    bf16 = lambda *shape: jax.ShapeDtypeStruct(shape, jnp.bfloat16)
    f32 = lambda *shape: jax.ShapeDtypeStruct(shape, jnp.float32)

    query_back = permuted(queries, back)
    key_near = permuted(key_rows, within)
    value_near = permuted(value_rows, within)
    query_near = permuted(queries, within)

    taps_far, taps_near = run(
        taps_kernel,
        "taps",
        facts,
        (bf16(heads, rows, groups // heads * rows),) * 2,
        [pltpu.VMEM((rows, 2 * rows), jnp.bfloat16), pltpu.VMEM((heads, groups // heads, taps), jnp.float32)],
        (st, filters),
    )
    key_across = permuted(after(key_rows, taps_far), across)

    slot_b0, slot_b1, slot_c = run(
        share_kernel,
        "share",
        facts,
        (bf16(half + 1, rows, HEAD_DIM), bf16(half + 1, rows, HEAD_DIM), bf16(rows, width)),
        [pltpu.VMEM((2 * rows, 2 * rows), jnp.float32), pltpu.VMEM((rows, LANES), jnp.float32)],
        (query_back, queries, key_near, key_rows, value_near, value_rows),
    )
    b_across = [permuted(x, across) for x in (slot_b0, slot_b1)]
    c_across = permuted(slot_c, across)
    key_far = permuted(after(key_across, slot_c), within)
    value_far = [permuted(x, within) for x in b_across]

    att, near, squares, near_squares = zip(
        *[
            run(
                lambda *refs, part=part: attention_kernel(part, *refs),
                "attention",
                facts,
                (bf16(half, rows, HEAD_DIM), bf16(half, rows, HEAD_DIM), f32(rows, LANES), f32(rows, LANES)),
                [pltpu.VMEM((rows, 3 * rows), jnp.float32), pltpu.VMEM((rows, 2 * rows), jnp.float32)],
                (st, queries, key_rows, value_rows, key_across, b_across[part], query_near, key_near, value_near, key_far, value_far[part]),
            )
            for part in range(2)
        ]
    )

    gain = norm_gain.reshape(1, width)
    part = run(
        own_kernel,
        "own",
        facts,
        f32(rows, width),
        [pltpu.VMEM((rows, LANES), jnp.float32)],
        (*att, *squares, taps_near, gain, bypass.reshape(1, width)),
    )
    return run(
        finish_kernel,
        "finish",
        facts,
        bf16(rows, width),
        [
            pltpu.VMEM((heads, rows, LANES), jnp.bfloat16),
            pltpu.VMEM((rows, LANES), jnp.float32),
            pltpu.VMEM((rows, LANES), jnp.float32),
            pltpu.VMEM((rows, rows), jnp.float32),
        ],
        (st, key_across, *b_across, c_across, *near, *near_squares, part, taps_far, gain),
    )


def solution(mesh):
    rows = P(("dp", "ctx"), None)
    in_specs = (rows, rows, rows, P("dp"), P(), P(), P())
    return jax.shard_map(shards, mesh=mesh, in_specs=in_specs, out_specs=rows, check_vma=False)
```

time: 208 us -> 67.4 us (0.32)
  local copies, waits for them, and re-layouts: 107 us -> 8.84 us
  waiting for transfers between devices: 45.5 us -> 13.1 us
  Pallas kernels: 0 us -> 21.7 us
  matrix products: 20.7 us -> 0 us
  other arithmetic: 16.6 us -> 2.49 us
  starting transfers between devices: 11.5 us -> 18.5 us
  loops' own time: 4.88 us -> 0 us
    reshape x8 -> x2, local copies, waits for them, and re-layouts: 64.3 us -> 0.12 us  [places(): return (starts[:count].astype(jnp.int32).reshape(count, 1), facts)]
    ppermute x5 -> x11, waiting for transfers between devices: 45.5 us -> 13.1 us  [permuted(): return lax.ppermute(x, 'ctx', pairs)]
    pallas_call x0 -> x6, Pallas kernels: none -> 21.7 us  [run(): pl.pallas_call(kernel, out_shape=out_shape, in_specs=[pl.BlockSpec(memory...]
    dot_general x10 -> x0, matrix products: 20.7 us -> none  [the longest x8 18.7 us: one_block(): jnp.einsum('gts,gcs->gct', matrix, data_block, preferred_element_type=jnp...]
    slice x9 -> x1, local copies, waits for them, and re-layouts: 12.2 us -> 0.54 us  [places(): starts[0]]
    dynamic_slice x16 -> x0, local copies, waits for them, and re-layouts: 10.3 us -> none  [the longest x8 5.63 us: one_block(): filter_block = lax.dynamic_slice_in_dim(filters, begin, block_size, 0)]
    while x8 -> x0, local copies, waits for them, and re-layouts: 9.64 us -> none
    concatenate x3 -> x0, other arithmetic: 8.2 us -> none  [the longest x1 3.38 us: shards(): window = jnp.concatenate([received, normed], axis=0)]
  transfers between devices with their start and end apart: 5 -> 11, of which waited for: 5 -> 3; matrix products, arithmetic and copies ran while one was open for 5% -> 5% of each run, Pallas kernels for 0% -> 22%
where the time goes in v5:
time: 67.4 us; the launch traced here: 66.8 us
  Pallas kernels  21.7 us (32%)
  starting transfers between devices  18.5 us (27%)
  waiting for transfers between devices  13.1 us (19%)
  local copies, waits for them, and re-layouts  8.84 us (13%)
  other arithmetic  2.49 us (4%)
  between operations  2.23 us (3%)
    pallas_call x6, Pallas kernels, run(): pl.pallas_call(kernel, out_shape=out_shape, in_specs=[pl.BlockSpec(memory...  21.7 us
    ppermute x11, starting transfers between devices, permuted(): return lax.ppermute(x, 'ctx', pairs)  18.5 us
    ppermute x11, waiting for transfers between devices, permuted(): return lax.ppermute(x, 'ctx', pairs)  13.1 us
    unnamed x18, local copies, waits for them, and re-layouts  8.19 us
  transfers between devices with their start and end apart: 11, of which 3 were waited for; matrix products, arithmetic and copies ran while one was open for 5% of the time, Pallas kernels for 22%

profile of v5, /device:TPU:28, one launch (start us, length us, event | category | flops | bytes accessed | tf_op | source)
XLA Modules:
  0.0 66.8 jit_solution(8537012352454339613)
XLA Ops:
  0.0 1.8 %collective-permute-start.3 = (bf16[128,4096]{1,0:T(8,128)(2,1)}, bf16[128,4096]{1,0:T(8,128)(2,1)S(1)}, u32[]{:S(2)}, u32[]{:S(2)}) collective-permute-start(bf16[128,4096]{1,0:T(8,128)(2,1)} %refs_4_.3), channel_id=1, source_target_pairs={{0,2},{4,6},{8,10},{12,14},{16,18},{20,22},{24,26},{28,30},{1,3},{... | collective-permute-start | bytes 3145736 | tf_op jit(solution)/shard_map/ppermute | solution.py:22
  1.8 2.3 %collective-permute-start.1 = (bf16[128,4096]{1,0:T(8,128)(2,1)}, bf16[128,4096]{1,0:T(8,128)(2,1)S(1)}, u32[]{:S(2)}, u32[]{:S(2)}) collective-permute-start(bf16[128,4096]{1,0:T(8,128)(2,1)} %refs_2_.3), channel_id=1, source_target_pairs={{4,2},{8,6},{12,10},{16,14},{20,18},{24,22},{28,26},{5,3},{9,7},{1... | collective-permute-start | bytes 3145736 | tf_op jit(solution)/shard_map/ppermute | solution.py:22
  4.1 1.4 %collective-permute-start.2 = (bf16[128,4096]{1,0:T(8,128)(2,1)}, bf16[128,4096]{1,0:T(8,128)(2,1)S(1)}, u32[]{:S(2)}, u32[]{:S(2)}) collective-permute-start(bf16[128,4096]{1,0:T(8,128)(2,1)} %refs_3_.3), channel_id=1, source_target_pairs={{0,2},{4,6},{8,10},{12,14},{16,18},{20,22},{24,26},{28,30},{1,3},{... | collective-permute-start | bytes 3145736 | tf_op jit(solution)/shard_map/ppermute | solution.py:22
  11.4 5.9 %taps.1 = (bf16[32,128,1024]{2,1,0:T(8,128)(2,1)S(1)}, bf16[32,128,1024]{2,1,0:T(8,128)(2,1)S(1)}) custom-call(s32[4]{0:T(128)S(1)} %pad_add_fusion.facts_ref.refs_0_, s32[128,1]{1,0:T(8,128)S(1)} %copy.11.st_ref.refs_1_, bf16[256,128]{1,0:T(8,128)(2,1)S(1)} %copy-done.6), custom_call_target="tpu_custom_call" | custom-call | flops 1048576 | bytes 65536 | tf_op jit(solution)/shard_map/taps/pallas_call | solution.py:347
  17.3 1.3 %collective-permute-start = (bf16[128,4096]{1,0:T(8,128)(2,1)}, bf16[128,4096]{1,0:T(8,128)(2,1)S(1)}, u32[]{:S(2)}, u32[]{:S(2)}) collective-permute-start(bf16[128,4096]{1,0:T(8,128)(2,1)} %refs_3_.3), channel_id=1, source_target_pairs={{2,4},{6,8},{10,12},{14,16},{18,20},{22,24},{26,28},{3,5},{7,9},{1... | collective-permute-start | bytes 3145736 | tf_op jit(solution)/shard_map/ppermute | solution.py:22
  18.7 1.2 %copy-done = bf16[128,4096]{1,0:T(8,128)(2,1)S(1)} copy-done((bf16[128,4096]{1,0:T(8,128)(2,1)S(1)}, bf16[128,4096]{1,0:T(8,128)(2,1)}, u32[]{:S(2)}) %copy-start) | copy-done | bytes 1048600
  19.9 1.2 %copy-done.2 = bf16[128,4096]{1,0:T(8,128)(2,1)S(1)} copy-done((bf16[128,4096]{1,0:T(8,128)(2,1)S(1)}, bf16[128,4096]{1,0:T(8,128)(2,1)}, u32[]{:S(2)}) %copy-start.2) | copy-done | bytes 1048600
  21.1 1.2 %copy-done.4 = bf16[128,4096]{1,0:T(8,128)(2,1)S(1)} copy-done((bf16[128,4096]{1,0:T(8,128)(2,1)S(1)}, bf16[128,4096]{1,0:T(8,128)(2,1)}, u32[]{:S(2)}) %copy-start.4) | copy-done | bytes 1048600
  22.9 1.3 %collective-permute-start.5 = (bf16[17,128,128]{2,1,0:T(8,128)(2,1)S(1)}, bf16[17,128,128]{2,1,0:T(8,128)(2,1)S(1)}, u32[]{:S(2)}, u32[]{:S(2)}) collective-permute-start(bf16[17,128,128]{2,1,0:T(8,128)(2,1)S(1)} %get-tuple-element.23), channel_id=1, source_target_pairs={{2,4},{6,8},{10,12},{14,16},{18,20},{22,24},{26,28},{3,5},{7,9},{1... | collective-permute-start | bytes 1671176 | tf_op jit(solution)/shard_map/ppermute | solution.py:22
  24.2 1.3 %collective-permute-start.4 = (bf16[17,128,128]{2,1,0:T(8,128)(2,1)S(1)}, bf16[17,128,128]{2,1,0:T(8,128)(2,1)S(1)}, u32[]{:S(2)}, u32[]{:S(2)}) collective-permute-start(bf16[17,128,128]{2,1,0:T(8,128)(2,1)S(1)} %get-tuple-element.22), channel_id=1, source_target_pairs={{2,4},{6,8},{10,12},{14,16},{18,20},{22,24},{26,28},{3,5},{7,9},{1... | collective-permute-start | bytes 1671176 | tf_op jit(solution)/shard_map/ppermute | solution.py:22
  25.5 3.9 %collective-permute-start.7 = (bf16[128,4096]{1,0:T(8,128)(2,1)S(1)}, bf16[128,4096]{1,0:T(8,128)(2,1)S(1)}, u32[]{:S(2)}, u32[]{:S(2)}) collective-permute-start(bf16[128,4096]{1,0:T(8,128)(2,1)S(1)} %copy-done.2), channel_id=1, source_target_pairs={{0,2},{4,6},{8,10},{12,14},{16,18},{20,22},{24,26},{28,30},{1,3},{... | collective-permute-start | bytes 3145736 | tf_op jit(solution)/shard_map/ppermute | solution.py:22
  29.4 5.1 %collective-permute-done.refs_5_.kp_ref = bf16[128,4096]{1,0:T(8,128)(2,1)S(1)} collective-permute-done((bf16[128,4096]{1,0:T(8,128)(2,1)}, bf16[128,4096]{1,0:T(8,128)(2,1)S(1)}, u32[]{:S(2)}, u32[]{:S(2)}) %collective-permute-start) | collective-permute-done | bytes 1048608 | tf_op jit(solution)/shard_map/ppermute | solution.py:22
  34.6 1.3 %collective-permute-start.8 = (bf16[128,4096]{1,0:T(8,128)(2,1)S(1)}, bf16[128,4096]{1,0:T(8,128)(2,1)S(1)}, u32[]{:S(2)}, u32[]{:S(2)}) collective-permute-start(bf16[128,4096]{1,0:T(8,128)(2,1)S(1)} %collective-permute-done.refs_5_.kp_ref), channel_id=1, source_target_pairs={{0,2},{4,6},{8,10},{12,14},{16,18},{20,22},{24,26},{28,30},{1,3},{... | collective-permute-start | bytes 3145736 | tf_op jit(solution)/shard_map/ppermute | solution.py:22
  35.9 1.3 %collective-permute-start.6 = (bf16[128,4096]{1,0:T(8,128)(2,1)S(1)}, bf16[128,4096]{1,0:T(8,128)(2,1)S(1)}, u32[]{:S(2)}, u32[]{:S(2)}) collective-permute-start(bf16[128,4096]{1,0:T(8,128)(2,1)S(1)} %get-tuple-element.24), channel_id=1, source_target_pairs={{2,4},{6,8},{10,12},{14,16},{18,20},{22,24},{26,28},{3,5},{7,9},{1... | collective-permute-start | bytes 3145736 | tf_op jit(solution)/shard_map/ppermute | solution.py:22
  37.2 3.3 %collective-permute-done.5.refs_6_.vp1_ref = bf16[17,128,128]{2,1,0:T(8,128)(2,1)S(1)} collective-permute-done((bf16[17,128,128]{2,1,0:T(8,128)(2,1)S(1)}, bf16[17,128,128]{2,1,0:T(8,128)(2,1)S(1)}, u32[]{:S(2)}, u32[]{:S(2)}) %collective-permute-start.5) | collective-permute-done | bytes 557088 | tf_op jit(solution)/shard_map/ppermute | solution.py:22
  40.5 1.3 %collective-permute-start.10 = (bf16[17,128,128]{2,1,0:T(8,128)(2,1)S(1)}, bf16[17,128,128]{2,1,0:T(8,128)(2,1)S(1)}, u32[]{:S(2)}, u32[]{:S(2)}) collective-permute-start(bf16[17,128,128]{2,1,0:T(8,128)(2,1)S(1)} %collective-permute-done.5.refs_6_.vp1_ref), channel_id=1, source_target_pairs={{0,2},{4,6},{8,10},{12,14},{16,18},{20,22},{24,26},{28,30},{1,3},{... | collective-permute-start | bytes 1671176 | tf_op jit(solution)/shard_map/ppermute | solution.py:22
  41.9 4.6 %collective-permute-done.4.refs_6_.vp0_ref = bf16[17,128,128]{2,1,0:T(8,128)(2,1)S(1)} collective-permute-done((bf16[17,128,128]{2,1,0:T(8,128)(2,1)S(1)}, bf16[17,128,128]{2,1,0:T(8,128)(2,1)S(1)}, u32[]{:S(2)}, u32[]{:S(2)}) %collective-permute-start.4) | collective-permute-done | bytes 557088 | tf_op jit(solution)/shard_map/ppermute | solution.py:22
  46.5 1.3 %collective-permute-start.9 = (bf16[17,128,128]{2,1,0:T(8,128)(2,1)S(1)}, bf16[17,128,128]{2,1,0:T(8,128)(2,1)S(1)}, u32[]{:S(2)}, u32[]{:S(2)}) collective-permute-start(bf16[17,128,128]{2,1,0:T(8,128)(2,1)S(1)} %collective-permute-done.4.refs_6_.vp0_ref), channel_id=1, source_target_pairs={{0,2},{4,6},{8,10},{12,14},{16,18},{20,22},{24,26},{28,30},{1,3},{... | collective-permute-start | bytes 1671176 | tf_op jit(solution)/shard_map/ppermute | solution.py:22
  49.1 1.2 %copy-done.3 = bf16[128,4096]{1,0:T(8,128)(2,1)S(1)} copy-done((bf16[128,4096]{1,0:T(8,128)(2,1)S(1)}, bf16[128,4096]{1,0:T(8,128)(2,1)}, u32[]{:S(2)}) %copy-start.3) | copy-done | bytes 1048600
  50.3 1.2 %copy-done.5 = bf16[128,4096]{1,0:T(8,128)(2,1)S(1)} copy-done((bf16[128,4096]{1,0:T(8,128)(2,1)S(1)}, bf16[128,4096]{1,0:T(8,128)(2,1)}, u32[]{:S(2)}) %copy-start.5) | copy-done | bytes 1048600
  51.5 2.3 %attention.3 = (bf16[16,128,128]{2,1,0:T(8,128)(2,1)S(1)}, bf16[16,128,128]{2,1,0:T(8,128)(2,1)S(1)}, f32[128,128]{1,0:T(8,128)S(1)}, f32[128,128]{1,0:T(8,128)S(1)}) custom-call(s32[4]{0:T(128)S(1)} %pad_add_fusion.facts_ref.refs_0_, s32[128,1]{1,0:T(8,128)S(1)} %copy.11.st_ref.refs_1_, bf16[128,4096]{1,0:T(8,128)(2,1)S(1)} %copy-done.3, ...), custom_call_target="tpu_custom_call" | custom-call | flops 1048576 | bytes 65536 | tf_op jit(solution)/shard_map/attention/pallas_call | solution.py:347
  53.9 2.3 %attention.2 = (bf16[16,128,128]{2,1,0:T(8,128)(2,1)S(1)}, bf16[16,128,128]{2,1,0:T(8,128)(2,1)S(1)}, f32[128,128]{1,0:T(8,128)S(1)}, f32[128,128]{1,0:T(8,128)S(1)}) custom-call(s32[4]{0:T(128)S(1)} %pad_add_fusion.facts_ref.refs_0_, s32[128,1]{1,0:T(8,128)S(1)} %copy.11.st_ref.refs_1_, bf16[128,4096]{1,0:T(8,128)(2,1)S(1)} %copy-done.3, ...), custom_call_target="tpu_custom_call" | custom-call | flops 1048576 | bytes 65536 | tf_op jit(solution)/shard_map/attention/pallas_call | solution.py:347
  56.3 3.5 %own.1.part_ref = f32[128,4096]{1,0:T(8,128)S(1)} custom-call(s32[4]{0:T(128)S(1)} %pad_add_fusion.facts_ref.refs_0_, bf16[16,128,128]{2,1,0:T(8,128)(2,1)S(1)} %get-tuple-element.30.att0_ref, bf16[16,128,128]{2,1,0:T(8,128)(2,1)S(1)} %get-tuple-element.31.att1_ref, f32[128,128]{1,0:T(8,128)S(1)} %get-tuple-element.32.sq0_ref, ...), custom_call_target="tpu_custom_call" | custom-call | flops 1048576 | bytes 65536 | tf_op jit(solution)/shard_map/own/pallas_call | solution.py:347
  59.7 7.1 %finish.1 = bf16[128,4096]{1,0:T(8,128)(2,1)} custom-call(s32[4]{0:T(128)S(1)} %pad_add_fusion.facts_ref.refs_0_, s32[128,1]{1,0:T(8,128)S(1)} %copy.11.st_ref.refs_1_, bf16[128,4096]{1,0:T(8,128)(2,1)S(1)} %collective-permute-done.refs_5_.kp_ref, bf16[17,128,128]{2,1,0:T(8,128)(2,1)S(1)} %collective-permute-done.4.refs_6_.vp0_ref, ...), custom_call_target="tpu_custom_call" | custom-call | flops 1048576 | bytes 65536 | tf_op jit(solution)/shard_map/finish/pallas_call | solution.py:347
  (32 shorter events, 5.8 us)
Async XLA Ops:
  0.0 18.6 %collective-permute-start.3 = (bf16[128,4096]{1,0:T(8,128)(2,1)}, bf16[128,4096]{1,0:T(8,128)(2,1)S(1)}, u32[]{:S(2)}, u32[]{:S(2)}) collective-permute-start(bf16[128,4096]{1,0:T(8,128)(2,1)} %refs_4_.3), channel_id=1, source_target_pairs={{0,2},{4,6},{8,10},{12,14},{16,18},{20,22},{24,26},{28,30},{1,3},{... | collective-permute-start | bytes 3145736 | tf_op jit(solution)/shard_map/ppermute | solution.py:22
  1.8 16.9 %collective-permute-start.1 = (bf16[128,4096]{1,0:T(8,128)(2,1)}, bf16[128,4096]{1,0:T(8,128)(2,1)S(1)}, u32[]{:S(2)}, u32[]{:S(2)}) collective-permute-start(bf16[128,4096]{1,0:T(8,128)(2,1)} %refs_2_.3), channel_id=1, source_target_pairs={{4,2},{8,6},{12,10},{16,14},{20,18},{24,22},{28,26},{5,3},{9,7},{1... | collective-permute-start | bytes 3145736 | tf_op jit(solution)/shard_map/ppermute | solution.py:22
  4.1 14.6 %collective-permute-start.2 = (bf16[128,4096]{1,0:T(8,128)(2,1)}, bf16[128,4096]{1,0:T(8,128)(2,1)S(1)}, u32[]{:S(2)}, u32[]{:S(2)}) collective-permute-start(bf16[128,4096]{1,0:T(8,128)(2,1)} %refs_3_.3), channel_id=1, source_target_pairs={{0,2},{4,6},{8,10},{12,14},{16,18},{20,22},{24,26},{28,30},{1,3},{... | collective-permute-start | bytes 3145736 | tf_op jit(solution)/shard_map/ppermute | solution.py:22
  10.6 0.8 %copy-start.6 = (bf16[256,128]{1,0:T(8,128)(2,1)S(1)}, bf16[256,128]{1,0:T(8,128)(2,1)}, u32[]{:S(2)}) copy-start(bf16[256,128]{1,0:T(8,128)(2,1)} %filters_ref.1) | copy-start | bytes 196612
  17.3 17.2 %collective-permute-start = (bf16[128,4096]{1,0:T(8,128)(2,1)}, bf16[128,4096]{1,0:T(8,128)(2,1)S(1)}, u32[]{:S(2)}, u32[]{:S(2)}) collective-permute-start(bf16[128,4096]{1,0:T(8,128)(2,1)} %refs_3_.3), channel_id=1, source_target_pairs={{2,4},{6,8},{10,12},{14,16},{18,20},{22,24},{26,28},{3,5},{7,9},{1... | collective-permute-start | bytes 3145736 | tf_op jit(solution)/shard_map/ppermute | solution.py:22
  18.7 1.2 %copy-start = (bf16[128,4096]{1,0:T(8,128)(2,1)S(1)}, bf16[128,4096]{1,0:T(8,128)(2,1)}, u32[]{:S(2)}) copy-start(bf16[128,4096]{1,0:T(8,128)(2,1)} %refs_3_.3) | copy-start | bytes 3145732
  19.9 1.2 %copy-start.2 = (bf16[128,4096]{1,0:T(8,128)(2,1)S(1)}, bf16[128,4096]{1,0:T(8,128)(2,1)}, u32[]{:S(2)}) copy-start(bf16[128,4096]{1,0:T(8,128)(2,1)} %refs_2_.3) | copy-start | bytes 3145732
  21.1 1.2 %copy-start.4 = (bf16[128,4096]{1,0:T(8,128)(2,1)S(1)}, bf16[128,4096]{1,0:T(8,128)(2,1)}, u32[]{:S(2)}) copy-start(bf16[128,4096]{1,0:T(8,128)(2,1)} %refs_4_.3) | copy-start | bytes 3145732
  22.4 33.9 %copy-start.7 = (f32[4096]{0:T(1024)S(1)}, f32[4096]{0:T(1024)}, u32[]{:S(2)}) copy-start(f32[4096]{0:T(1024)} %param.11) | copy-start | bytes 49156
  22.4 33.9 %copy-start.8 = (f32[4096]{0:T(1024)S(1)}, f32[4096]{0:T(1024)}, u32[]{:S(2)}) copy-start(f32[4096]{0:T(1024)} %param.13) | copy-start | bytes 49156
  22.9 17.6 %collective-permute-start.5 = (bf16[17,128,128]{2,1,0:T(8,128)(2,1)S(1)}, bf16[17,128,128]{2,1,0:T(8,128)(2,1)S(1)}, u32[]{:S(2)}, u32[]{:S(2)}) collective-permute-start(bf16[17,128,128]{2,1,0:T(8,128)(2,1)S(1)} %get-tuple-element.23), channel_id=1, source_target_pairs={{2,4},{6,8},{10,12},{14,16},{18,20},{22,24},{26,28},{3,5},{7,9},{1... | collective-permute-start | bytes 1671176 | tf_op jit(solution)/shard_map/ppermute | solution.py:22
  24.2 22.3 %collective-permute-start.4 = (bf16[17,128,128]{2,1,0:T(8,128)(2,1)S(1)}, bf16[17,128,128]{2,1,0:T(8,128)(2,1)S(1)}, u32[]{:S(2)}, u32[]{:S(2)}) collective-permute-start(bf16[17,128,128]{2,1,0:T(8,128)(2,1)S(1)} %get-tuple-element.22), channel_id=1, source_target_pairs={{2,4},{6,8},{10,12},{14,16},{18,20},{22,24},{26,28},{3,5},{7,9},{1... | collective-permute-start | bytes 1671176 | tf_op jit(solution)/shard_map/ppermute | solution.py:22
  25.5 22.3 %collective-permute-start.7 = (bf16[128,4096]{1,0:T(8,128)(2,1)S(1)}, bf16[128,4096]{1,0:T(8,128)(2,1)S(1)}, u32[]{:S(2)}, u32[]{:S(2)}) collective-permute-start(bf16[128,4096]{1,0:T(8,128)(2,1)S(1)} %copy-done.2), channel_id=1, source_target_pairs={{0,2},{4,6},{8,10},{12,14},{16,18},{20,22},{24,26},{28,30},{1,3},{... | collective-permute-start | bytes 3145736 | tf_op jit(solution)/shard_map/ppermute | solution.py:22
  34.6 13.3 %collective-permute-start.8 = (bf16[128,4096]{1,0:T(8,128)(2,1)S(1)}, bf16[128,4096]{1,0:T(8,128)(2,1)S(1)}, u32[]{:S(2)}, u32[]{:S(2)}) collective-permute-start(bf16[128,4096]{1,0:T(8,128)(2,1)S(1)} %collective-permute-done.refs_5_.kp_ref), channel_id=1, source_target_pairs={{0,2},{4,6},{8,10},{12,14},{16,18},{20,22},{24,26},{28,30},{1,3},{... | collective-permute-start | bytes 3145736 | tf_op jit(solution)/shard_map/ppermute | solution.py:22
  35.9 23.8 %collective-permute-start.6 = (bf16[128,4096]{1,0:T(8,128)(2,1)S(1)}, bf16[128,4096]{1,0:T(8,128)(2,1)S(1)}, u32[]{:S(2)}, u32[]{:S(2)}) collective-permute-start(bf16[128,4096]{1,0:T(8,128)(2,1)S(1)} %get-tuple-element.24), channel_id=1, source_target_pairs={{2,4},{6,8},{10,12},{14,16},{18,20},{22,24},{26,28},{3,5},{7,9},{1... | collective-permute-start | bytes 3145736 | tf_op jit(solution)/shard_map/ppermute | solution.py:22
  40.5 7.3 %collective-permute-start.10 = (bf16[17,128,128]{2,1,0:T(8,128)(2,1)S(1)}, bf16[17,128,128]{2,1,0:T(8,128)(2,1)S(1)}, u32[]{:S(2)}, u32[]{:S(2)}) collective-permute-start(bf16[17,128,128]{2,1,0:T(8,128)(2,1)S(1)} %collective-permute-done.5.refs_6_.vp1_ref), channel_id=1, source_target_pairs={{0,2},{4,6},{8,10},{12,14},{16,18},{20,22},{24,26},{28,30},{1,3},{... | collective-permute-start | bytes 1671176 | tf_op jit(solution)/shard_map/ppermute | solution.py:22
  46.5 7.4 %collective-permute-start.9 = (bf16[17,128,128]{2,1,0:T(8,128)(2,1)S(1)}, bf16[17,128,128]{2,1,0:T(8,128)(2,1)S(1)}, u32[]{:S(2)}, u32[]{:S(2)}) collective-permute-start(bf16[17,128,128]{2,1,0:T(8,128)(2,1)S(1)} %collective-permute-done.4.refs_6_.vp0_ref), channel_id=1, source_target_pairs={{0,2},{4,6},{8,10},{12,14},{16,18},{20,22},{24,26},{28,30},{1,3},{... | collective-permute-start | bytes 1671176 | tf_op jit(solution)/shard_map/ppermute | solution.py:22
  47.9 1.2 %copy-start.1 = (bf16[128,4096]{1,0:T(8,128)(2,1)S(1)}, bf16[128,4096]{1,0:T(8,128)(2,1)}, u32[]{:S(2)}) copy-start(bf16[128,4096]{1,0:T(8,128)(2,1)} %refs_3_.3) | copy-start | bytes 3145732
  49.1 1.2 %copy-start.3 = (bf16[128,4096]{1,0:T(8,128)(2,1)S(1)}, bf16[128,4096]{1,0:T(8,128)(2,1)}, u32[]{:S(2)}) copy-start(bf16[128,4096]{1,0:T(8,128)(2,1)} %refs_2_.3) | copy-start | bytes 3145732
  50.3 1.2 %copy-start.5 = (bf16[128,4096]{1,0:T(8,128)(2,1)S(1)}, bf16[128,4096]{1,0:T(8,128)(2,1)}, u32[]{:S(2)}) copy-start(bf16[128,4096]{1,0:T(8,128)(2,1)} %refs_4_.3) | copy-start | bytes 3145732

commit v6 on v5

--- a/solution.py
+++ b/solution.py
@@ -164,92 +164,6 @@
             b_ref[half] = packed.astype(jnp.bfloat16)
 
 
-def attention_kernel(part, facts_ref, st_ref, q_ref, ko_ref, vo_ref, kp_ref, vp_ref, qn_ref, kn_ref, vn_ref, kf_ref, vf_ref, att_ref, near_ref, sq_ref, sq_near_ref, bias_own, bias_prev):
-    rows = q_ref.shape[0]
-    odd = facts_ref[ODD] == 1
-    half = att_ref.shape[0]
-    low = jnp.where((facts_ref[ODD] == 0) & (facts_ref[BEFORE] > rows), 0, -(2**20))
-    bias_own[...] = bias_of(rows, 3 * rows, 0, -2 * rows, jnp.maximum(st_ref[...], low))
-    sq_ref[...] = jnp.zeros_like(sq_ref)
-    sq_near_ref[...] = jnp.zeros_like(sq_near_ref)
-
-    @pl.when(odd)
-    def _():
-        bias_prev[...] = bias_of(rows, 2 * rows, -rows, -2 * rows, st_ref[0:1, :])
-
-        def heads(first):
-            at = lambda h: columns(part * half + first + h)
-            squares = [sq_ref[...], sq_near_ref[...]]
-
-            def use_own(h, o, l, top):
-                a = (o / l).astype(jnp.bfloat16)
-                att_ref[first + h] = a
-                a = a.astype(jnp.float32)
-                squares[0] += a * a
-
-            def use_near(h, o, l, top):
-                a = (o / l).astype(jnp.bfloat16)
-                near_ref[first + h] = a
-                a = a.astype(jnp.float32)
-                squares[1] += a * a
-
-            attend(
-                UNROLL,
-                lambda h: q_ref[:, at(h)],
-                lambda h: jnp.concatenate([kf_ref[:, at(h)], kn_ref[:, at(h)], ko_ref[:, at(h)]], axis=0),
-                lambda h: jnp.concatenate([vf_ref[first + h], vn_ref[:, at(h)], vo_ref[:, at(h)]], axis=0),
-                bias_own[...],
-                use_own,
-            )
-            attend(
-                UNROLL,
-                lambda h: qn_ref[:, at(h)],
-                lambda h: jnp.concatenate([kf_ref[:, at(h)], kn_ref[:, at(h)]], axis=0),
-                lambda h: jnp.concatenate([vf_ref[first + h], vn_ref[:, at(h)]], axis=0),
-                bias_prev[...],
-                use_near,
-            )
-            sq_ref[...] = squares[0]
-            sq_near_ref[...] = squares[1]
-
-        each(half, heads)
-
-    @pl.when(jnp.logical_not(odd))
-    def _():
-        lane = lax.broadcasted_iota(jnp.int32, (rows, LANES), 1)
-
-        def heads(first):
-            at = lambda h: columns(part * half + first + h)
-            packed = vp_ref[half].astype(jnp.float32)
-            stat = packed + pltpu.roll(packed, LANES - half, 1) + pltpu.roll(packed, LANES - 2 * half, 1)
-            stat = jnp.where(facts_ref[BEFORE] > rows, stat, NEG)
-            squares = [sq_ref[...]]
-
-            def use(h, o, l, top):
-                lse = jnp.sum(jnp.where(lane == first + h, stat, 0.0), axis=1, keepdims=True)
-                top = top * FACTOR
-                high = jnp.maximum(top, lse)
-                here = jnp.exp2(top - high)
-                there = jnp.exp2(lse - high)
-                o = o * here + vp_ref[first + h].astype(jnp.float32) * there
-                a = (o / (l * here + there)).astype(jnp.bfloat16)
-                att_ref[first + h] = a
-                a = a.astype(jnp.float32)
-                squares[0] += a * a
-
-            attend(
-                UNROLL,
-                lambda h: q_ref[:, at(h)],
-                lambda h: jnp.concatenate([kp_ref[:, at(h)], ko_ref[:, at(h)]], axis=0),
-                lambda h: jnp.concatenate([vp_ref[first + h], vo_ref[:, at(h)]], axis=0),
-                bias_own[:, rows:],
-                use,
-            )
-            sq_ref[...] = squares[0]
-
-        each(half, heads)
-
-
 def scale_of(squares, width):
     total = jnp.sum(squares, axis=1, keepdims=True)
     return jnp.broadcast_to(lax.rsqrt(total * (1.0 / width) + 1e-06), squares.shape)
@@ -261,37 +175,133 @@
     return jnp.concatenate([jnp.where(lane_group == g, x, jnp.zeros_like(x)) for g in range(groups)], axis=0)
 
 
-def own_kernel(facts_ref, att0_ref, att1_ref, sq0_ref, sq1_ref, taps_ref, gain_ref, bypass_ref, out_ref, scale):
-    half, rows, _ = att0_ref.shape
-    scale[...] = scale_of(sq0_ref[...] + sq1_ref[...], 2 * half * LANES)
-    for part, att_ref in enumerate((att0_ref, att1_ref)):
-
-        def tiles(first):
-            for c in range(UNROLL):
-                tile = part * half + first + c
-                cols = columns(tile)
-                x = (att_ref[first + c].astype(jnp.float32) * scale[...] * gain_ref[:, cols]).astype(jnp.bfloat16)
-                y = jnp.dot(taps_ref[tile], spread(x, taps_ref.shape[2] // rows), preferred_element_type=jnp.float32)
-                out_ref[:, cols] = y + bypass_ref[:, cols] * x.astype(jnp.float32)
-
-        each(half, tiles)
-
-
-def finish_kernel(facts_ref, st_ref, kp_ref, vp0_ref, vp1_ref, c_ref, near0_ref, near1_ref, sq0_ref, sq1_ref, part_ref, taps_ref, gain_ref, out_ref, prev, squares, scale, bias):
+def convolve_own(att, squares, scale, taps_ref, gain_ref, bypass_ref, out_ref):
+    count, rows, _ = att.shape
+    scale[...] = scale_of(squares, count * LANES)
+
+    def tiles(first):
+        for c in range(UNROLL):
+            cols = columns(first + c)
+            x = (att[first + c].astype(jnp.float32) * scale[...] * gain_ref[:, cols]).astype(jnp.bfloat16)
+            y = jnp.dot(taps_ref[first + c], spread(x, taps_ref.shape[2] // rows), preferred_element_type=jnp.float32)
+            out_ref[:, cols] = y + bypass_ref[:, cols] * x.astype(jnp.float32)
+
+    each(count, tiles)
+
+
+def even_kernel(facts_ref, st_ref, q_ref, ko_ref, vo_ref, kp_ref, vp0_ref, vp1_ref, qn_ref, kn_ref, kf_ref, taps_ref, gain_ref, bypass_ref, three_ref, two_ref, out_ref, att, squares, scale, bias_own, bias_prev):
+    rows = q_ref.shape[0]
+    odd = facts_ref[ODD] == 1
+    half = vp0_ref.shape[0] - 1
+    low = jnp.where((facts_ref[ODD] == 0) & (facts_ref[BEFORE] > rows), 0, -(2**20))
+    bias_own[...] = bias_of(rows, 3 * rows, 0, -2 * rows, jnp.maximum(st_ref[...], low))
+
+    @pl.when(odd)
+    def _():
+        bias_prev[...] = bias_of(rows, 2 * rows, -rows, -2 * rows, st_ref[0:1, :])
+
+        def heads(first):
+            def scores(h):
+                at = columns(first + h)
+                key = jnp.concatenate([kf_ref[:, at], kn_ref[:, at], ko_ref[:, at]], axis=0)
+                return scores_of(q_ref[:, at], key), scores_of(qn_ref[:, at], key[: 2 * rows])
+
+            ahead = scores(0)
+            for h in range(UNROLL):
+                now = ahead
+                if h + 1 < UNROLL:
+                    ahead = scores(h + 1)
+                three_ref[first + h] = raised(now[0], bias_own[...])[0]
+                two_ref[first + h] = raised(now[1], bias_prev[...])[0]
+
+        each(2 * half, heads)
+
+    @pl.when(jnp.logical_not(odd))
+    def _():
+        lane = lax.broadcasted_iota(jnp.int32, (rows, LANES), 1)
+        squares[...] = jnp.zeros_like(squares)
+        for part, vp_ref in enumerate((vp0_ref, vp1_ref)):
+
+            def heads(first):
+                at = lambda h: columns(part * half + first + h)
+                packed = vp_ref[half].astype(jnp.float32)
+                stat = packed + pltpu.roll(packed, LANES - half, 1) + pltpu.roll(packed, LANES - 2 * half, 1)
+                stat = jnp.where(facts_ref[BEFORE] > rows, stat, NEG)
+                total = [squares[...]]
+
+                def use(h, o, l, top):
+                    lse = jnp.sum(jnp.where(lane == first + h, stat, 0.0), axis=1, keepdims=True)
+                    top = top * FACTOR
+                    high = jnp.maximum(top, lse)
+                    here = jnp.exp2(top - high)
+                    there = jnp.exp2(lse - high)
+                    o = o * here + vp_ref[first + h].astype(jnp.float32) * there
+                    a = (o / (l * here + there)).astype(jnp.bfloat16)
+                    att[part * half + first + h] = a
+                    a = a.astype(jnp.float32)
+                    total[0] += a * a
+
+                attend(
+                    UNROLL,
+                    lambda h: q_ref[:, at(h)],
+                    lambda h: jnp.concatenate([kp_ref[:, at(h)], ko_ref[:, at(h)]], axis=0),
+                    lambda h: jnp.concatenate([vp_ref[first + h], vo_ref[:, at(h)]], axis=0),
+                    bias_own[:, rows:],
+                    use,
+                )
+                squares[...] = total[0]
+
+            each(half, heads)
+        convolve_own(att, squares[...], scale, taps_ref, gain_ref, bypass_ref, out_ref)
+
+
+def odd_kernel(facts_ref, three_ref, two_ref, vo_ref, vn_ref, vf0_ref, vf1_ref, taps_ref, gain_ref, bypass_ref, near_ref, sq_near_ref, out_ref, att, squares, scale):
+    rows = vo_ref.shape[0]
+    half = vf0_ref.shape[0] - 1
+
+    @pl.when(facts_ref[ODD] == 1)
+    def _():
+        squares[...] = jnp.zeros_like(squares)
+        sq_near_ref[...] = jnp.zeros_like(sq_near_ref)
+        for part, vf_ref in enumerate((vf0_ref, vf1_ref)):
+
+            def heads(first):
+                total, total_near = squares[...], sq_near_ref[...]
+                for h in range(UNROLL):
+                    head = part * half + first + h
+                    at = columns(head)
+                    value = jnp.concatenate([vf_ref[first + h], vn_ref[:, at], vo_ref[:, at]], axis=0)
+                    o, l = summed(three_ref[head], value)
+                    a = (o / l).astype(jnp.bfloat16)
+                    att[head] = a
+                    a = a.astype(jnp.float32)
+                    total += a * a
+                    o, l = summed(two_ref[head], value[: 2 * rows])
+                    a = (o / l).astype(jnp.bfloat16)
+                    near_ref[head] = a
+                    a = a.astype(jnp.float32)
+                    total_near += a * a
+                squares[...] = total
+                sq_near_ref[...] = total_near
+
+            each(half, heads)
+        convolve_own(att, squares[...], scale, taps_ref, gain_ref, bypass_ref, out_ref)
+
+
+def finish_kernel(facts_ref, st_ref, kp_ref, vp0_ref, vp1_ref, c_ref, near_ref, sq_ref, even_ref, odd_ref, taps_ref, gain_ref, out_ref, prev, squares, scale, bias):
     rows = st_ref.shape[0]
-    half = near0_ref.shape[0]
+    half = vp0_ref.shape[0] - 1
     width = prev.shape[0] * LANES
     odd = facts_ref[ODD] == 1
     shared = facts_ref[BEFORE] > rows
 
     @pl.when(odd)
     def _():
-        squares[...] = sq0_ref[...] + sq1_ref[...]
-        for part, near_ref in enumerate((near0_ref, near1_ref)):
-
-            @pl.loop(0, half)
-            def _(h):
-                prev[part * half + h] = near_ref[h]
+        squares[...] = sq_ref[...]
+
+        @pl.loop(0, 2 * half)
+        def _(h):
+            prev[h] = near_ref[h]
 
     @pl.when(jnp.logical_not(odd) & shared)
     def _():
@@ -336,7 +346,7 @@
             cols = columns(first + c)
             x = (prev[first + c].astype(jnp.float32) * scale[...] * gain_ref[:, cols]).astype(jnp.bfloat16)
             y = jnp.dot(taps_ref[first + c], spread(x, taps_ref.shape[2] // rows), preferred_element_type=jnp.float32)
-            out_ref[:, cols] = (y + part_ref[:, cols]).astype(jnp.bfloat16)
+            out_ref[:, cols] = (y + jnp.where(odd, odd_ref[:, cols], even_ref[:, cols])).astype(jnp.bfloat16)
 
     each(2 * half, tiles)
 
@@ -384,12 +394,12 @@
         [pltpu.VMEM((rows, 2 * rows), jnp.bfloat16), pltpu.VMEM((heads, groups // heads, taps), jnp.float32)],
         (st, filters),
     )
-    key_across = permuted(after(key_rows, taps_far), across)
+    key_across = permuted(after(key_rows, facts), across)
 
     slot_b0, slot_b1, slot_c = run(
         share_kernel,
         "share",
-        facts,
+        after(facts, taps_far),
         (bf16(half + 1, rows, HEAD_DIM), bf16(half + 1, rows, HEAD_DIM), bf16(rows, width)),
         [pltpu.VMEM((2 * rows, 2 * rows), jnp.float32), pltpu.VMEM((rows, LANES), jnp.float32)],
         (query_back, queries, key_near, key_rows, value_near, value_rows),
@@ -399,28 +409,28 @@
     key_far = permuted(after(key_across, slot_c), within)
     value_far = [permuted(x, within) for x in b_across]
 
-    att, near, squares, near_squares = zip(
-        *[
-            run(
-                lambda *refs, part=part: attention_kernel(part, *refs),
-                "attention",
-                facts,
-                (bf16(half, rows, HEAD_DIM), bf16(half, rows, HEAD_DIM), f32(rows, LANES), f32(rows, LANES)),
-                [pltpu.VMEM((rows, 3 * rows), jnp.float32), pltpu.VMEM((rows, 2 * rows), jnp.float32)],
-                (st, queries, key_rows, value_rows, key_across, b_across[part], query_near, key_near, value_near, key_far, value_far[part]),
-            )
-            for part in range(2)
-        ]
+    gain = norm_gain.reshape(1, width)
+    skip = bypass.reshape(1, width)
+    own_scratch = [
+        pltpu.VMEM((heads, rows, HEAD_DIM), jnp.bfloat16),
+        pltpu.VMEM((rows, LANES), jnp.float32),
+        pltpu.VMEM((rows, LANES), jnp.float32),
+    ]
+    three, two, even_part = run(
+        even_kernel,
+        "even",
+        facts,
+        (bf16(heads, rows, 3 * rows), bf16(heads, rows, 2 * rows), f32(rows, width)),
+        own_scratch + [pltpu.VMEM((rows, 3 * rows), jnp.float32), pltpu.VMEM((rows, 2 * rows), jnp.float32)],
+        (st, queries, key_rows, value_rows, key_across, *b_across, query_near, key_near, key_far, taps_near, gain, skip),
     )
-
-    gain = norm_gain.reshape(1, width)
-    part = run(
-        own_kernel,
-        "own",
+    near, near_squares, odd_part = run(
+        odd_kernel,
+        "odd",
         facts,
-        f32(rows, width),
-        [pltpu.VMEM((rows, LANES), jnp.float32)],
-        (*att, *squares, taps_near, gain, bypass.reshape(1, width)),
+        (bf16(heads, rows, HEAD_DIM), f32(rows, LANES), f32(rows, width)),
+        own_scratch,
+        (three, two, value_rows, value_near, *value_far, taps_near, gain, skip),
     )
     return run(
         finish_kernel,
@@ -433,7 +443,7 @@
             pltpu.VMEM((rows, LANES), jnp.float32),
             pltpu.VMEM((rows, rows), jnp.float32),
         ],
-        (st, key_across, *b_across, c_across, *near, *near_squares, part, taps_far, gain),
+        (st, key_across, *b_across, c_across, near, near_squares, even_part, odd_part, taps_far, gain),
     )
 
 

time: 67.4 us -> 63.5 us (0.942)
  starting transfers between devices: 18.5 us -> 23.4 us
  local copies, waits for them, and re-layouts: 8.84 us -> 5.23 us
  waiting for transfers between devices: 13.1 us -> 10 us
  Pallas kernels: 21.7 us -> 19.6 us
    ppermute x11, starting transfers between devices: 18.5 us -> 23.4 us  [permuted(): return lax.ppermute(x, 'ctx', pairs)]
    unnamed x18 -> x14, local copies, waits for them, and re-layouts: 8.19 us -> 4.52 us
    ppermute x11, waiting for transfers between devices: 13.1 us -> 10 us  [permuted(): return lax.ppermute(x, 'ctx', pairs)]
    pallas_call x6 -> x5, Pallas kernels: 21.7 us -> 19.6 us  [run(): pl.pallas_call(kernel, out_shape=out_shape, in_specs=[pl.BlockSpec(memory...]
  transfers between devices with their start and end apart: 11 -> 11, of which waited for: 3 -> 3; matrix products, arithmetic and copies ran while one was open for 5% -> 5% of each run, Pallas kernels for 22% -> 23%
where the time goes in v6:
time: 63.5 us; the launch traced here: 63 us
  starting transfers between devices  23.4 us (37%)
  Pallas kernels  19.6 us (31%)
  waiting for transfers between devices  10 us (16%)
  local copies, waits for them, and re-layouts  5.23 us (8%)
  other arithmetic  2.49 us (4%)
  between operations  2.28 us (4%)
    ppermute x11, starting transfers between devices, permuted(): return lax.ppermute(x, 'ctx', pairs)  23.4 us
    pallas_call x5, Pallas kernels, run(): pl.pallas_call(kernel, out_shape=out_shape, in_specs=[pl.BlockSpec(memory...  19.6 us
    ppermute x11, waiting for transfers between devices, permuted(): return lax.ppermute(x, 'ctx', pairs)  10 us
    unnamed x14, local copies, waits for them, and re-layouts  4.52 us
  transfers between devices with their start and end apart: 11, of which 3 were waited for; matrix products, arithmetic and copies ran while one was open for 5% of the time, Pallas kernels for 23%

profile of v6, /device:TPU:28, one launch (start us, length us, event | category | flops | bytes accessed | tf_op | source)
XLA Modules:
  0.0 63.0 jit_solution(1489868657926277247)
XLA Ops:
  0.0 3.7 %collective-permute-start.1 = (bf16[128,4096]{1,0:T(8,128)(2,1)}, bf16[128,4096]{1,0:T(8,128)(2,1)}, u32[]{:S(2)}, u32[]{:S(2)}) collective-permute-start(bf16[128,4096]{1,0:T(8,128)(2,1)} %q_ref.3), channel_id=1, source_target_pairs={{4,2},{8,6},{12,10},{16,14},{20,18},{24,22},{28,26},{5,3},{9,7},{1... | collective-permute-start | bytes 3145736 | tf_op jit(solution)/shard_map/ppermute | solution.py:22
  3.7 1.3 %collective-permute-start.2 = (bf16[128,4096]{1,0:T(8,128)(2,1)}, bf16[128,4096]{1,0:T(8,128)(2,1)S(1)}, u32[]{:S(2)}, u32[]{:S(2)}) collective-permute-start(bf16[128,4096]{1,0:T(8,128)(2,1)} %ko_ref.3), channel_id=1, source_target_pairs={{0,2},{4,6},{8,10},{12,14},{16,18},{20,22},{24,26},{28,30},{1,3},{... | collective-permute-start | bytes 3145736 | tf_op jit(solution)/shard_map/ppermute | solution.py:22
  5.1 1.4 %collective-permute-start.3 = (bf16[128,4096]{1,0:T(8,128)(2,1)}, bf16[128,4096]{1,0:T(8,128)(2,1)S(1)}, u32[]{:S(2)}, u32[]{:S(2)}) collective-permute-start(bf16[128,4096]{1,0:T(8,128)(2,1)} %vo_ref.5), channel_id=1, source_target_pairs={{0,2},{4,6},{8,10},{12,14},{16,18},{20,22},{24,26},{28,30},{1,3},{... | collective-permute-start | bytes 3145736 | tf_op jit(solution)/shard_map/ppermute | solution.py:22
  6.5 0.8 %reduce-window.8 = s32[10,1]{0,1:T(1,128)S(1)} reduce-window(s32[10,1]{0,1:T(1,128)} %bitcast.22, s32[]{:T(128)} %constant.37.clone.1), window={size=10x1 pad=9_0x0_0}, to_apply=%region_0.0 | reduce-window | flops 90 | bytes 84 | tf_op jit(solution)/shard_map/reduce-window.3
  7.3 0.8 %select_reduce_fusion = s32[129]{0:T(256)S(1)} fusion(s32[10]{0:T(128)} %param.10, s32[129]{0:T(256)S(1)} %iota_add_fusion, s32[10]{0:T(128)S(1)} %bitcast.20), kind=kLoop, calls=%fused_computation | loop fusion | flops 3741 | bytes 1112 | tf_op jit(solution)/shard_map/reduce_sum | solution.py:33
  11.6 1.3 %collective-permute-start = (bf16[128,4096]{1,0:T(8,128)(2,1)}, bf16[128,4096]{1,0:T(8,128)(2,1)S(1)}, u32[]{:S(2)}, u32[]{:S(2)}) collective-permute-start(bf16[128,4096]{1,0:T(8,128)(2,1)} %ko_ref.3), channel_id=1, source_target_pairs={{2,4},{6,8},{10,12},{14,16},{18,20},{22,24},{26,28},{3,5},{7,9},{1... | collective-permute-start | bytes 3145736 | tf_op jit(solution)/shard_map/ppermute | solution.py:22
  13.0 0.8 %copy-done.6 = bf16[256,128]{1,0:T(8,128)(2,1)S(1)} copy-done((bf16[256,128]{1,0:T(8,128)(2,1)S(1)}, bf16[256,128]{1,0:T(8,128)(2,1)}, u32[]{:S(2)}) %copy-start.6) | copy-done | bytes 65560
  13.8 5.9 %taps.1 = (bf16[32,128,1024]{2,1,0:T(8,128)(2,1)S(1)}, bf16[32,128,1024]{2,1,0:T(8,128)(2,1)S(1)}) custom-call(s32[4]{0:T(128)S(1)} %pad_add_fusion.facts_ref, s32[128,1]{1,0:T(8,128)S(1)} %copy.10.st_ref, bf16[256,128]{1,0:T(8,128)(2,1)S(1)} %copy-done.6), custom_call_target="tpu_custom_call" | custom-call | flops 1048576 | bytes 65536 | tf_op jit(solution)/shard_map/taps/pallas_call | solution.py:357
  19.8 1.2 %copy-done = bf16[128,4096]{1,0:T(8,128)(2,1)S(1)} copy-done((bf16[128,4096]{1,0:T(8,128)(2,1)S(1)}, bf16[128,4096]{1,0:T(8,128)(2,1)}, u32[]{:S(2)}) %copy-start) | copy-done | bytes 1048600
  21.0 1.2 %copy-done.1 = bf16[128,4096]{1,0:T(8,128)(2,1)S(1)} copy-done((bf16[128,4096]{1,0:T(8,128)(2,1)S(1)}, bf16[128,4096]{1,0:T(8,128)(2,1)}, u32[]{:S(2)}) %copy-start.1) | copy-done | bytes 1048600
  22.2 1.2 %copy-done.2 = bf16[128,4096]{1,0:T(8,128)(2,1)S(1)} copy-done((bf16[128,4096]{1,0:T(8,128)(2,1)S(1)}, bf16[128,4096]{1,0:T(8,128)(2,1)}, u32[]{:S(2)}) %copy-start.2) | copy-done | bytes 1048600
  23.4 1.3 %share.1 = (bf16[17,128,128]{2,1,0:T(8,128)(2,1)S(1)}, bf16[17,128,128]{2,1,0:T(8,128)(2,1)S(1)}, bf16[128,4096]{1,0:T(8,128)(2,1)S(1)}) custom-call(s32[4]{0:T(128)S(1)} %pad_add_fusion.facts_ref, bf16[128,4096]{1,0:T(8,128)(2,1)} %collective-permute-done.1.qb_ref, bf16[128,4096]{1,0:T(8,128)(2,1)S(1)} %copy-done.2, ...), custom_call_target="tpu_custom_call" | custom-call | flops 1048576 | bytes 65536 | tf_op jit(solution)/shard_map/share/pallas_call | solution.py:357
  24.8 1.3 %collective-permute-start.4 = (bf16[17,128,128]{2,1,0:T(8,128)(2,1)S(1)}, bf16[17,128,128]{2,1,0:T(8,128)(2,1)S(1)}, u32[]{:S(2)}, u32[]{:S(2)}) collective-permute-start(bf16[17,128,128]{2,1,0:T(8,128)(2,1)S(1)} %get-tuple-element.22), channel_id=1, source_target_pairs={{2,4},{6,8},{10,12},{14,16},{18,20},{22,24},{26,28},{3,5},{7,9},{1... | collective-permute-start | bytes 1671176 | tf_op jit(solution)/shard_map/ppermute | solution.py:22
  26.1 1.3 %collective-permute-start.5 = (bf16[17,128,128]{2,1,0:T(8,128)(2,1)S(1)}, bf16[17,128,128]{2,1,0:T(8,128)(2,1)S(1)}, u32[]{:S(2)}, u32[]{:S(2)}) collective-permute-start(bf16[17,128,128]{2,1,0:T(8,128)(2,1)S(1)} %get-tuple-element.23), channel_id=1, source_target_pairs={{2,4},{6,8},{10,12},{14,16},{18,20},{22,24},{26,28},{3,5},{7,9},{1... | collective-permute-start | bytes 1671176 | tf_op jit(solution)/shard_map/ppermute | solution.py:22
  27.4 7.8 %collective-permute-start.7 = (bf16[128,4096]{1,0:T(8,128)(2,1)S(1)}, bf16[128,4096]{1,0:T(8,128)(2,1)S(1)}, u32[]{:S(2)}, u32[]{:S(2)}) collective-permute-start(bf16[128,4096]{1,0:T(8,128)(2,1)S(1)} %copy-done.2), channel_id=1, source_target_pairs={{0,2},{4,6},{8,10},{12,14},{16,18},{20,22},{24,26},{28,30},{1,3},{... | collective-permute-start | bytes 3145736 | tf_op jit(solution)/shard_map/ppermute | solution.py:22
  35.2 1.4 %collective-permute-start.8 = (bf16[128,4096]{1,0:T(8,128)(2,1)S(1)}, bf16[128,4096]{1,0:T(8,128)(2,1)S(1)}, u32[]{:S(2)}, u32[]{:S(2)}) collective-permute-start(bf16[128,4096]{1,0:T(8,128)(2,1)S(1)} %collective-permute-done.kp_ref), channel_id=1, source_target_pairs={{0,2},{4,6},{8,10},{12,14},{16,18},{20,22},{24,26},{28,30},{1,3},{... | collective-permute-start | bytes 3145736 | tf_op jit(solution)/shard_map/ppermute | solution.py:22
  36.6 1.3 %collective-permute-start.6 = (bf16[128,4096]{1,0:T(8,128)(2,1)S(1)}, bf16[128,4096]{1,0:T(8,128)(2,1)S(1)}, u32[]{:S(2)}, u32[]{:S(2)}) collective-permute-start(bf16[128,4096]{1,0:T(8,128)(2,1)S(1)} %get-tuple-element.24), channel_id=1, source_target_pairs={{2,4},{6,8},{10,12},{14,16},{18,20},{22,24},{26,28},{3,5},{7,9},{1... | collective-permute-start | bytes 3145736 | tf_op jit(solution)/shard_map/ppermute | solution.py:22
  37.9 3.1 %collective-permute-done.4.vp0_ref = bf16[17,128,128]{2,1,0:T(8,128)(2,1)S(1)} collective-permute-done((bf16[17,128,128]{2,1,0:T(8,128)(2,1)S(1)}, bf16[17,128,128]{2,1,0:T(8,128)(2,1)S(1)}, u32[]{:S(2)}, u32[]{:S(2)}) %collective-permute-start.4) | collective-permute-done | bytes 557088 | tf_op jit(solution)/shard_map/ppermute | solution.py:22
  41.0 1.3 %collective-permute-start.9 = (bf16[17,128,128]{2,1,0:T(8,128)(2,1)S(1)}, bf16[17,128,128]{2,1,0:T(8,128)(2,1)S(1)}, u32[]{:S(2)}, u32[]{:S(2)}) collective-permute-start(bf16[17,128,128]{2,1,0:T(8,128)(2,1)S(1)} %collective-permute-done.4.vp0_ref), channel_id=1, source_target_pairs={{0,2},{4,6},{8,10},{12,14},{16,18},{20,22},{24,26},{28,30},{1,3},{... | collective-permute-start | bytes 1671176 | tf_op jit(solution)/shard_map/ppermute | solution.py:22
  42.3 4.6 %collective-permute-done.5.vp1_ref = bf16[17,128,128]{2,1,0:T(8,128)(2,1)S(1)} collective-permute-done((bf16[17,128,128]{2,1,0:T(8,128)(2,1)S(1)}, bf16[17,128,128]{2,1,0:T(8,128)(2,1)S(1)}, u32[]{:S(2)}, u32[]{:S(2)}) %collective-permute-start.5) | collective-permute-done | bytes 557088 | tf_op jit(solution)/shard_map/ppermute | solution.py:22
  46.9 1.3 %collective-permute-start.10 = (bf16[17,128,128]{2,1,0:T(8,128)(2,1)S(1)}, bf16[17,128,128]{2,1,0:T(8,128)(2,1)S(1)}, u32[]{:S(2)}, u32[]{:S(2)}) collective-permute-start(bf16[17,128,128]{2,1,0:T(8,128)(2,1)S(1)} %collective-permute-done.5.vp1_ref), channel_id=1, source_target_pairs={{0,2},{4,6},{8,10},{12,14},{16,18},{20,22},{24,26},{28,30},{1,3},{... | collective-permute-start | bytes 1671176 | tf_op jit(solution)/shard_map/ppermute | solution.py:22
  48.3 7.0 %even.1 = (bf16[32,128,384]{2,1,0:T(8,128)(2,1)S(1)}, bf16[32,128,256]{2,1,0:T(8,128)(2,1)S(1)}, f32[128,4096]{1,0:T(8,128)S(1)}) custom-call(s32[4]{0:T(128)S(1)} %pad_add_fusion.facts_ref, s32[128,1]{1,0:T(8,128)S(1)} %copy.10.st_ref, bf16[128,4096]{1,0:T(8,128)(2,1)S(1)} %copy-done.3, bf16[128,4096]{1,0:T(8,128)(2,1)S(1)} %copy-done.1, ...), custom_call_target="tpu_custom_call" | custom-call | flops 1048576 | bytes 65536 | tf_op jit(solution)/shard_map/even/pallas_call | solution.py:357
  55.9 2.3 %collective-permute-done.6.c_ref = bf16[128,4096]{1,0:T(8,128)(2,1)S(1)} collective-permute-done((bf16[128,4096]{1,0:T(8,128)(2,1)S(1)}, bf16[128,4096]{1,0:T(8,128)(2,1)S(1)}, u32[]{:S(2)}, u32[]{:S(2)}) %collective-permute-start.6) | collective-permute-done | bytes 1048608 | tf_op jit(solution)/shard_map/ppermute | solution.py:22
  58.2 4.9 %finish.1 = bf16[128,4096]{1,0:T(8,128)(2,1)} custom-call(s32[4]{0:T(128)S(1)} %pad_add_fusion.facts_ref, s32[128,1]{1,0:T(8,128)S(1)} %copy.10.st_ref, bf16[128,4096]{1,0:T(8,128)(2,1)S(1)} %collective-permute-done.kp_ref, bf16[17,128,128]{2,1,0:T(8,128)(2,1)S(1)} %collective-permute-done.4.vp0_ref, ...), custom_call_target="tpu_custom_call" | custom-call | flops 1048576 | bytes 65536 | tf_op jit(solution)/shard_map/finish/pallas_call | solution.py:357
  (27 shorter events, 2.1 us)
Async XLA Ops:
  0.0 19.7 %collective-permute-start.1 = (bf16[128,4096]{1,0:T(8,128)(2,1)}, bf16[128,4096]{1,0:T(8,128)(2,1)}, u32[]{:S(2)}, u32[]{:S(2)}) collective-permute-start(bf16[128,4096]{1,0:T(8,128)(2,1)} %q_ref.3), channel_id=1, source_target_pairs={{4,2},{8,6},{12,10},{16,14},{20,18},{24,22},{28,26},{5,3},{9,7},{1... | collective-permute-start | bytes 3145736 | tf_op jit(solution)/shard_map/ppermute | solution.py:22
  3.7 16.0 %collective-permute-start.2 = (bf16[128,4096]{1,0:T(8,128)(2,1)}, bf16[128,4096]{1,0:T(8,128)(2,1)S(1)}, u32[]{:S(2)}, u32[]{:S(2)}) collective-permute-start(bf16[128,4096]{1,0:T(8,128)(2,1)} %ko_ref.3), channel_id=1, source_target_pairs={{0,2},{4,6},{8,10},{12,14},{16,18},{20,22},{24,26},{28,30},{1,3},{... | collective-permute-start | bytes 3145736 | tf_op jit(solution)/shard_map/ppermute | solution.py:22
  5.1 14.7 %collective-permute-start.3 = (bf16[128,4096]{1,0:T(8,128)(2,1)}, bf16[128,4096]{1,0:T(8,128)(2,1)S(1)}, u32[]{:S(2)}, u32[]{:S(2)}) collective-permute-start(bf16[128,4096]{1,0:T(8,128)(2,1)} %vo_ref.5), channel_id=1, source_target_pairs={{0,2},{4,6},{8,10},{12,14},{16,18},{20,22},{24,26},{28,30},{1,3},{... | collective-permute-start | bytes 3145736 | tf_op jit(solution)/shard_map/ppermute | solution.py:22
  11.6 23.7 %collective-permute-start = (bf16[128,4096]{1,0:T(8,128)(2,1)}, bf16[128,4096]{1,0:T(8,128)(2,1)S(1)}, u32[]{:S(2)}, u32[]{:S(2)}) collective-permute-start(bf16[128,4096]{1,0:T(8,128)(2,1)} %ko_ref.3), channel_id=1, source_target_pairs={{2,4},{6,8},{10,12},{14,16},{18,20},{22,24},{26,28},{3,5},{7,9},{1... | collective-permute-start | bytes 3145736 | tf_op jit(solution)/shard_map/ppermute | solution.py:22
  13.0 0.8 %copy-start.6 = (bf16[256,128]{1,0:T(8,128)(2,1)S(1)}, bf16[256,128]{1,0:T(8,128)(2,1)}, u32[]{:S(2)}) copy-start(bf16[256,128]{1,0:T(8,128)(2,1)} %filters_ref.1) | copy-start | bytes 196612
  13.8 34.5 %copy-start.4 = (f32[4096]{0:T(1024)S(1)}, f32[4096]{0:T(1024)}, u32[]{:S(2)}) copy-start(f32[4096]{0:T(1024)} %param.11) | copy-start | bytes 49156
  13.8 34.5 %copy-start.5 = (f32[4096]{0:T(1024)S(1)}, f32[4096]{0:T(1024)}, u32[]{:S(2)}) copy-start(f32[4096]{0:T(1024)} %param.13) | copy-start | bytes 49156
  19.8 1.2 %copy-start = (bf16[128,4096]{1,0:T(8,128)(2,1)S(1)}, bf16[128,4096]{1,0:T(8,128)(2,1)}, u32[]{:S(2)}) copy-start(bf16[128,4096]{1,0:T(8,128)(2,1)} %vo_ref.5) | copy-start | bytes 3145732
  21.0 1.2 %copy-start.1 = (bf16[128,4096]{1,0:T(8,128)(2,1)S(1)}, bf16[128,4096]{1,0:T(8,128)(2,1)}, u32[]{:S(2)}) copy-start(bf16[128,4096]{1,0:T(8,128)(2,1)} %ko_ref.3) | copy-start | bytes 3145732
  22.2 1.2 %copy-start.2 = (bf16[128,4096]{1,0:T(8,128)(2,1)S(1)}, bf16[128,4096]{1,0:T(8,128)(2,1)}, u32[]{:S(2)}) copy-start(bf16[128,4096]{1,0:T(8,128)(2,1)} %q_ref.3) | copy-start | bytes 3145732
  23.4 24.9 %copy-start.3 = (bf16[128,4096]{1,0:T(8,128)(2,1)S(1)}, bf16[128,4096]{1,0:T(8,128)(2,1)}, u32[]{:S(2)}) copy-start(bf16[128,4096]{1,0:T(8,128)(2,1)} %q_ref.3) | copy-start | bytes 3145732
  24.8 16.2 %collective-permute-start.4 = (bf16[17,128,128]{2,1,0:T(8,128)(2,1)S(1)}, bf16[17,128,128]{2,1,0:T(8,128)(2,1)S(1)}, u32[]{:S(2)}, u32[]{:S(2)}) collective-permute-start(bf16[17,128,128]{2,1,0:T(8,128)(2,1)S(1)} %get-tuple-element.22), channel_id=1, source_target_pairs={{2,4},{6,8},{10,12},{14,16},{18,20},{22,24},{26,28},{3,5},{7,9},{1... | collective-permute-start | bytes 1671176 | tf_op jit(solution)/shard_map/ppermute | solution.py:22
  26.1 20.8 %collective-permute-start.5 = (bf16[17,128,128]{2,1,0:T(8,128)(2,1)S(1)}, bf16[17,128,128]{2,1,0:T(8,128)(2,1)S(1)}, u32[]{:S(2)}, u32[]{:S(2)}) collective-permute-start(bf16[17,128,128]{2,1,0:T(8,128)(2,1)S(1)} %get-tuple-element.23), channel_id=1, source_target_pairs={{2,4},{6,8},{10,12},{14,16},{18,20},{22,24},{26,28},{3,5},{7,9},{1... | collective-permute-start | bytes 1671176 | tf_op jit(solution)/shard_map/ppermute | solution.py:22
  27.4 20.9 %collective-permute-start.7 = (bf16[128,4096]{1,0:T(8,128)(2,1)S(1)}, bf16[128,4096]{1,0:T(8,128)(2,1)S(1)}, u32[]{:S(2)}, u32[]{:S(2)}) collective-permute-start(bf16[128,4096]{1,0:T(8,128)(2,1)S(1)} %copy-done.2), channel_id=1, source_target_pairs={{0,2},{4,6},{8,10},{12,14},{16,18},{20,22},{24,26},{28,30},{1,3},{... | collective-permute-start | bytes 3145736 | tf_op jit(solution)/shard_map/ppermute | solution.py:22
  35.2 13.0 %collective-permute-start.8 = (bf16[128,4096]{1,0:T(8,128)(2,1)S(1)}, bf16[128,4096]{1,0:T(8,128)(2,1)S(1)}, u32[]{:S(2)}, u32[]{:S(2)}) collective-permute-start(bf16[128,4096]{1,0:T(8,128)(2,1)S(1)} %collective-permute-done.kp_ref), channel_id=1, source_target_pairs={{0,2},{4,6},{8,10},{12,14},{16,18},{20,22},{24,26},{28,30},{1,3},{... | collective-permute-start | bytes 3145736 | tf_op jit(solution)/shard_map/ppermute | solution.py:22
  36.6 21.6 %collective-permute-start.6 = (bf16[128,4096]{1,0:T(8,128)(2,1)S(1)}, bf16[128,4096]{1,0:T(8,128)(2,1)S(1)}, u32[]{:S(2)}, u32[]{:S(2)}) collective-permute-start(bf16[128,4096]{1,0:T(8,128)(2,1)S(1)} %get-tuple-element.24), channel_id=1, source_target_pairs={{2,4},{6,8},{10,12},{14,16},{18,20},{22,24},{26,28},{3,5},{7,9},{1... | collective-permute-start | bytes 3145736 | tf_op jit(solution)/shard_map/ppermute | solution.py:22
  41.0 14.3 %collective-permute-start.9 = (bf16[17,128,128]{2,1,0:T(8,128)(2,1)S(1)}, bf16[17,128,128]{2,1,0:T(8,128)(2,1)S(1)}, u32[]{:S(2)}, u32[]{:S(2)}) collective-permute-start(bf16[17,128,128]{2,1,0:T(8,128)(2,1)S(1)} %collective-permute-done.4.vp0_ref), channel_id=1, source_target_pairs={{0,2},{4,6},{8,10},{12,14},{16,18},{20,22},{24,26},{28,30},{1,3},{... | collective-permute-start | bytes 1671176 | tf_op jit(solution)/shard_map/ppermute | solution.py:22
  46.9 8.4 %collective-permute-start.10 = (bf16[17,128,128]{2,1,0:T(8,128)(2,1)S(1)}, bf16[17,128,128]{2,1,0:T(8,128)(2,1)S(1)}, u32[]{:S(2)}, u32[]{:S(2)}) collective-permute-start(bf16[17,128,128]{2,1,0:T(8,128)(2,1)S(1)} %collective-permute-done.5.vp1_ref), channel_id=1, source_target_pairs={{0,2},{4,6},{8,10},{12,14},{16,18},{20,22},{24,26},{28,30},{1,3},{... | collective-permute-start | bytes 1671176 | tf_op jit(solution)/shard_map/ppermute | solution.py:22

commit v7 on v6

--- a/solution.py
+++ b/solution.py
@@ -26,15 +26,32 @@
     return lax.optimization_barrier((x, *others))[0]
 
 
-def places(lengths, first_row, count):
-    ends = jnp.cumsum(lengths)
-    position = first_row + jnp.arange(count + 1, dtype=jnp.int32)
-    passed = ends[None, :] <= position[:, None]
-    starts = jnp.sum(jnp.where(passed, lengths[None, :], 0), axis=1) - first_row
-    past = jnp.min(jnp.where(passed[count], jnp.int32(2**30), ends)) - first_row - count
-    odd = (first_row // count) % 2
-    facts = jnp.stack([odd, -starts[0], count - starts[count], past]).astype(jnp.int32)
-    return starts[:count].astype(jnp.int32).reshape(count, 1), facts
+def facts_of(place_ref, lengths_ref, rows):
+    first = place_ref[0] * rows
+    after_last = first + rows
+
+    def look(d, carry):
+        begin, start, next_start, past = carry
+        end = begin + lengths_ref[d]
+        start = jnp.where((begin <= first) & (first < end), begin, start)
+        here = (begin <= after_last) & (after_last < end)
+        next_start = jnp.where(here, begin, next_start)
+        past = jnp.where(here, end, past)
+        return end, start, next_start, past
+
+    _, start, next_start, past = lax.fori_loop(0, lengths_ref.shape[0], look, (jnp.int32(0), first, after_last, after_last))
+    return lax.rem(place_ref[0], 2), first - start, after_last - next_start, past - after_last
+
+
+def starts_of(place_ref, lengths_ref, rows):
+    first = place_ref[0] * rows
+    position = lax.broadcasted_iota(jnp.int32, (rows, 1), 0)
+
+    def look(d, carry):
+        begin, starts = carry
+        return begin + lengths_ref[d], jnp.where(position >= begin, begin, starts)
+
+    return lax.fori_loop(0, lengths_ref.shape[0], look, (-first, jnp.full((rows, 1), -first, jnp.int32)))[1]
 
 
 def bias_of(rows, columns, row_first, key_first, start):
@@ -85,11 +102,10 @@
         body(step * UNROLL)
 
 
-def taps_kernel(facts_ref, st_ref, filters_ref, far_ref, near_ref, keep, lines):
-    rows = st_ref.shape[0]
-    tiles = far_ref.shape[0]
+def taps_kernel(place_ref, lengths_ref, filters_ref, far_ref, near_ref, keep, lines):
+    tiles, rows, _ = far_ref.shape
     groups = filters_ref.shape[0] // tiles
-    st = st_ref[...]
+    st = starts_of(place_ref, lengths_ref, rows)
     row = lax.broadcasted_iota(jnp.int32, (rows, 2 * rows), 0)
     key = lax.broadcasted_iota(jnp.int32, (rows, 2 * rows), 1) - rows
     keep[...] = jnp.where((key >= st) & (key <= row) & (key > row - rows), 1.0, 0.0).astype(jnp.bfloat16)
@@ -109,11 +125,24 @@
             near_ref[c, :, cols] = ring * keep[:, rows:]
 
 
-def share_kernel(facts_ref, qb_ref, q_ref, kn_ref, ko_ref, vn_ref, vo_ref, b0_ref, b1_ref, c_ref, bias, stat_ref):
+def gate_kernel(place_ref, arrived_ref, out_ref):
+    out_ref[0] = place_ref[0]
+
+
+def share_kernel(place_ref, lengths_ref, qb_ref, q_hbm, kn_ref, ko_hbm, vn_ref, vo_hbm, b0_ref, b1_ref, c_ref, q_ref, ko_ref, vo_ref, bias, stat_ref, sems):
     rows = q_ref.shape[0]
-    before = facts_ref[NEXT_BEFORE]
-    past = facts_ref[NEXT_AFTER]
-    odd = facts_ref[ODD] == 1
+    moves = [
+        pltpu.make_async_copy(source, target, sems.at[i])
+        for i, (source, target) in enumerate(((q_hbm, q_ref), (ko_hbm, ko_ref), (vo_hbm, vo_ref)))
+    ]
+    for move in moves:
+        move.start()
+    facts = facts_of(place_ref, lengths_ref, rows)
+    for move in moves:
+        move.wait()
+    before = facts[NEXT_BEFORE]
+    past = facts[NEXT_AFTER]
+    odd = facts[ODD] == 1
     half = b0_ref.shape[0] - 1
 
     @pl.when(odd & (before <= rows))
@@ -189,16 +218,17 @@
     each(count, tiles)
 
 
-def even_kernel(facts_ref, st_ref, q_ref, ko_ref, vo_ref, kp_ref, vp0_ref, vp1_ref, qn_ref, kn_ref, kf_ref, taps_ref, gain_ref, bypass_ref, three_ref, two_ref, out_ref, att, squares, scale, bias_own, bias_prev):
+def even_kernel(place_ref, lengths_ref, q_ref, ko_ref, vo_ref, kp_ref, vp0_ref, vp1_ref, qn_ref, kn_ref, kf_ref, taps_ref, gain_ref, bypass_ref, three_ref, two_ref, out_ref, att, squares, scale, bias_own, bias_prev):
     rows = q_ref.shape[0]
-    odd = facts_ref[ODD] == 1
+    facts = facts_of(place_ref, lengths_ref, rows)
+    odd = facts[ODD] == 1
     half = vp0_ref.shape[0] - 1
-    low = jnp.where((facts_ref[ODD] == 0) & (facts_ref[BEFORE] > rows), 0, -(2**20))
-    bias_own[...] = bias_of(rows, 3 * rows, 0, -2 * rows, jnp.maximum(st_ref[...], low))
+    low = jnp.where((facts[ODD] == 0) & (facts[BEFORE] > rows), 0, -(2**20))
+    bias_own[...] = bias_of(rows, 3 * rows, 0, -2 * rows, jnp.maximum(starts_of(place_ref, lengths_ref, rows), low))
 
     @pl.when(odd)
     def _():
-        bias_prev[...] = bias_of(rows, 2 * rows, -rows, -2 * rows, st_ref[0:1, :])
+        bias_prev[...] = bias_of(rows, 2 * rows, -rows, -2 * rows, -facts[BEFORE])
 
         def heads(first):
             def scores(h):
@@ -226,7 +256,7 @@
                 at = lambda h: columns(part * half + first + h)
                 packed = vp_ref[half].astype(jnp.float32)
                 stat = packed + pltpu.roll(packed, LANES - half, 1) + pltpu.roll(packed, LANES - 2 * half, 1)
-                stat = jnp.where(facts_ref[BEFORE] > rows, stat, NEG)
+                stat = jnp.where(facts[BEFORE] > rows, stat, NEG)
                 total = [squares[...]]
 
                 def use(h, o, l, top):
@@ -255,11 +285,11 @@
         convolve_own(att, squares[...], scale, taps_ref, gain_ref, bypass_ref, out_ref)
 
 
-def odd_kernel(facts_ref, three_ref, two_ref, vo_ref, vn_ref, vf0_ref, vf1_ref, taps_ref, gain_ref, bypass_ref, near_ref, sq_near_ref, out_ref, att, squares, scale):
+def odd_kernel(place_ref, lengths_ref, three_ref, two_ref, vo_ref, vn_ref, vf0_ref, vf1_ref, taps_ref, gain_ref, bypass_ref, near_ref, sq_near_ref, out_ref, att, squares, scale):
     rows = vo_ref.shape[0]
     half = vf0_ref.shape[0] - 1
 
-    @pl.when(facts_ref[ODD] == 1)
+    @pl.when(lax.rem(place_ref[0], 2) == 1)
     def _():
         squares[...] = jnp.zeros_like(squares)
         sq_near_ref[...] = jnp.zeros_like(sq_near_ref)
@@ -288,12 +318,13 @@
         convolve_own(att, squares[...], scale, taps_ref, gain_ref, bypass_ref, out_ref)
 
 
-def finish_kernel(facts_ref, st_ref, kp_ref, vp0_ref, vp1_ref, c_ref, near_ref, sq_ref, even_ref, odd_ref, taps_ref, gain_ref, out_ref, prev, squares, scale, bias):
-    rows = st_ref.shape[0]
+def finish_kernel(place_ref, lengths_ref, kp_ref, vp0_ref, vp1_ref, c_ref, near_ref, sq_ref, even_ref, odd_ref, taps_ref, gain_ref, out_ref, prev, squares, scale, bias):
+    rows = c_ref.shape[0]
+    facts = facts_of(place_ref, lengths_ref, rows)
     half = vp0_ref.shape[0] - 1
     width = prev.shape[0] * LANES
-    odd = facts_ref[ODD] == 1
-    shared = facts_ref[BEFORE] > rows
+    odd = facts[ODD] == 1
+    shared = facts[BEFORE] > rows
 
     @pl.when(odd)
     def _():
@@ -321,7 +352,7 @@
     @pl.when(jnp.logical_not(odd) & jnp.logical_not(shared))
     def _():
         squares[...] = jnp.zeros_like(squares)
-        bias[...] = bias_of(rows, rows, -rows, -rows, st_ref[0:1, :])
+        bias[...] = bias_of(rows, rows, -rows, -rows, -facts[BEFORE])
         for part, vp_ref in enumerate((vp0_ref, vp1_ref)):
 
             def heads(first):
@@ -351,19 +382,20 @@
     each(2 * half, tiles)
 
 
-def run(kernel, name, facts, out_shape, scratch, args):
+def run(kernel, name, known, out_shape, scratch, args, in_place=()):
     many = isinstance(out_shape, tuple)
     vmem = pl.BlockSpec(memory_space=pltpu.VMEM)
+    specs = [pl.BlockSpec(memory_space=pltpu.MemorySpace.HBM) if i in in_place else vmem for i in range(len(args))]
     return pl.pallas_call(
         kernel,
         out_shape=out_shape,
-        in_specs=[pl.BlockSpec(memory_space=pltpu.SMEM)] + [vmem] * len(args),
+        in_specs=[pl.BlockSpec(memory_space=pltpu.SMEM)] * 2 + specs,
         out_specs=(vmem,) * len(out_shape) if many else vmem,
         scratch_shapes=scratch,
         compiler_params=pltpu.CompilerParams(vmem_limit_bytes=VMEM_BYTES),
         cost_estimate=pl.CostEstimate(flops=2**20, bytes_accessed=2**16, transcendentals=0),
         name=name,
-    )(facts, *args)
+    )(*known, *args)
 
 
 def shards(queries, key_rows, value_rows, lengths, norm_gain, filters, bypass):
@@ -372,7 +404,7 @@
     half = heads // 2
     groups, taps = filters.shape
     n = lax.axis_size("ctx")
-    st, facts = places(lengths, lax.axis_index("ctx") * rows, rows)
+    known = lax.axis_index("ctx").astype(jnp.int32).reshape(1), lengths
 
     back = [(i, i - 1) for i in range(2, n, 2)]
     within = [(i, i + 1) for i in range(0, n - 1, 2)]
@@ -382,32 +414,43 @@
     f32 = lambda *shape: jax.ShapeDtypeStruct(shape, jnp.float32)
 
     query_back = permuted(queries, back)
+    query_near = permuted(queries, within)
     key_near = permuted(key_rows, within)
     value_near = permuted(value_rows, within)
-    query_near = permuted(queries, within)
-
-    taps_far, taps_near = run(
-        taps_kernel,
-        "taps",
-        facts,
-        (bf16(heads, rows, groups // heads * rows),) * 2,
-        [pltpu.VMEM((rows, 2 * rows), jnp.bfloat16), pltpu.VMEM((heads, groups // heads, taps), jnp.float32)],
-        (st, filters),
-    )
-    key_across = permuted(after(key_rows, facts), across)
-
-    slot_b0, slot_b1, slot_c = run(
+
+    key_across = permuted(after(key_rows, query_near), across)
+
+    wide = bf16(rows, width)
+    smem = pl.BlockSpec(memory_space=pltpu.SMEM)
+    place = pl.pallas_call(
+        gate_kernel,
+        out_shape=jax.ShapeDtypeStruct((1,), jnp.int32),
+        in_specs=[smem, pl.BlockSpec(memory_space=pl.ANY)],
+        out_specs=smem,
+        cost_estimate=pl.CostEstimate(flops=0, bytes_accessed=16 * 2**20, transcendentals=0),
+        name="gate",
+    )(known[0], query_back)
+    slot_b0, slot_b1, slot_c, query_own, key_own, value_own = run(
         share_kernel,
         "share",
-        after(facts, taps_far),
-        (bf16(half + 1, rows, HEAD_DIM), bf16(half + 1, rows, HEAD_DIM), bf16(rows, width)),
-        [pltpu.VMEM((2 * rows, 2 * rows), jnp.float32), pltpu.VMEM((rows, LANES), jnp.float32)],
+        (place, lengths),
+        (bf16(half + 1, rows, HEAD_DIM), bf16(half + 1, rows, HEAD_DIM), wide, wide, wide, wide),
+        [pltpu.VMEM((2 * rows, 2 * rows), jnp.float32), pltpu.VMEM((rows, LANES), jnp.float32), pltpu.SemaphoreType.DMA((3,))],
         (query_back, queries, key_near, key_rows, value_near, value_rows),
+        (1, 3, 5),
     )
     b_across = [permuted(x, across) for x in (slot_b0, slot_b1)]
     c_across = permuted(slot_c, across)
     key_far = permuted(after(key_across, slot_c), within)
-    value_far = [permuted(x, within) for x in b_across]
+    taps_far, taps_near = run(
+        taps_kernel,
+        "taps",
+        (known[0], after(lengths, slot_c)),
+        (bf16(heads, rows, groups // heads * rows),) * 2,
+        [pltpu.VMEM((rows, 2 * rows), jnp.bfloat16), pltpu.VMEM((heads, groups // heads, taps), jnp.float32)],
+        (filters,),
+    )
+    value_far = [permuted(after(x, taps_far), within) for x in b_across]
 
     gain = norm_gain.reshape(1, width)
     skip = bypass.reshape(1, width)
@@ -419,23 +462,23 @@
     three, two, even_part = run(
         even_kernel,
         "even",
-        facts,
+        known,
         (bf16(heads, rows, 3 * rows), bf16(heads, rows, 2 * rows), f32(rows, width)),
         own_scratch + [pltpu.VMEM((rows, 3 * rows), jnp.float32), pltpu.VMEM((rows, 2 * rows), jnp.float32)],
-        (st, queries, key_rows, value_rows, key_across, *b_across, query_near, key_near, key_far, taps_near, gain, skip),
+        (query_own, key_own, value_own, key_across, *b_across, query_near, key_near, key_far, taps_near, gain, skip),
     )
     near, near_squares, odd_part = run(
         odd_kernel,
         "odd",
-        facts,
+        known,
         (bf16(heads, rows, HEAD_DIM), f32(rows, LANES), f32(rows, width)),
         own_scratch,
-        (three, two, value_rows, value_near, *value_far, taps_near, gain, skip),
+        (three, two, value_own, value_near, *value_far, taps_near, gain, skip),
     )
     return run(
         finish_kernel,
         "finish",
-        facts,
+        known,
         bf16(rows, width),
         [
             pltpu.VMEM((heads, rows, LANES), jnp.bfloat16),
@@ -443,7 +486,7 @@
             pltpu.VMEM((rows, LANES), jnp.float32),
             pltpu.VMEM((rows, rows), jnp.float32),
         ],
-        (st, key_across, *b_across, c_across, near, near_squares, even_part, odd_part, taps_far, gain),
+        (key_across, *b_across, c_across, near, near_squares, even_part, odd_part, taps_far, gain),
     )
 
 

time: 63.5 us -> 76.2 us (1.20)
  the two profiles are of different devices: /device:TPU:28 before, /device:TPU:3 now
where the time goes in v7:
time: 76.2 us; the launch traced here: 75.2 us
  starting transfers between devices  36.5 us (48%)
  Pallas kernels  24.8 us (33%)
  local copies, waits for them, and re-layouts  7.49 us (10%)
  waiting for transfers between devices  6.12 us (8%)
    ppermute x11, starting transfers between devices, permuted(): return lax.ppermute(x, 'ctx', pairs)  36.5 us
    pallas_call x5, Pallas kernels, run(): pl.pallas_call(kernel, out_shape=out_shape, in_specs=[pl.BlockSpec(memory...  24.3 us
    unnamed x22, local copies, waits for them, and re-layouts  7.49 us
    ppermute x11, waiting for transfers between devices, permuted(): return lax.ppermute(x, 'ctx', pairs)  6.12 us
  transfers between devices with their start and end apart: 11, of which 1 were waited for; matrix products, arithmetic and copies ran while one was open for 0% of the time, Pallas kernels for 26%

profile of v7, /device:TPU:3, one launch (start us, length us, event | category | flops | bytes accessed | tf_op | source)
XLA Modules:
  0.0 75.2 jit_solution(13486519062823110816)
XLA Ops:
  0.0 1.3 %collective-permute-start = (bf16[128,4096]{1,0:T(8,128)(2,1)}, bf16[128,4096]{1,0:T(8,128)(2,1)S(1)}, u32[]{:S(2)}, u32[]{:S(2)}) collective-permute-start(bf16[128,4096]{1,0:T(8,128)(2,1)} %q_hbm.1), channel_id=1, source_target_pairs={{0,2},{4,6},{8,10},{12,14},{16,18},{20,22},{24,26},{28,30},{1,3},{... | collective-permute-start | bytes 3145736 | tf_op jit(solution)/shard_map/ppermute | solution.py:22
  1.3 1.3 %collective-permute-start.2 = (bf16[128,4096]{1,0:T(8,128)(2,1)}, bf16[128,4096]{1,0:T(8,128)(2,1)S(1)}, u32[]{:S(2)}, u32[]{:S(2)}) collective-permute-start(bf16[128,4096]{1,0:T(8,128)(2,1)} %q_hbm.1), channel_id=1, source_target_pairs={{4,2},{8,6},{12,10},{16,14},{20,18},{24,22},{28,26},{5,3},{9,7},{1... | collective-permute-start | bytes 3145736 | tf_op jit(solution)/shard_map/ppermute | solution.py:22
  2.6 1.3 %collective-permute-start.3 = (bf16[128,4096]{1,0:T(8,128)(2,1)}, bf16[128,4096]{1,0:T(8,128)(2,1)S(1)}, u32[]{:S(2)}, u32[]{:S(2)}) collective-permute-start(bf16[128,4096]{1,0:T(8,128)(2,1)} %ko_hbm.1), channel_id=1, source_target_pairs={{0,2},{4,6},{8,10},{12,14},{16,18},{20,22},{24,26},{28,30},{1,3},{... | collective-permute-start | bytes 3145736 | tf_op jit(solution)/shard_map/ppermute | solution.py:22
  3.9 1.3 %collective-permute-start.4 = (bf16[128,4096]{1,0:T(8,128)(2,1)}, bf16[128,4096]{1,0:T(8,128)(2,1)S(1)}, u32[]{:S(2)}, u32[]{:S(2)}) collective-permute-start(bf16[128,4096]{1,0:T(8,128)(2,1)} %vo_hbm.1), channel_id=1, source_target_pairs={{0,2},{4,6},{8,10},{12,14},{16,18},{20,22},{24,26},{28,30},{1,3},{... | collective-permute-start | bytes 3145736 | tf_op jit(solution)/shard_map/ppermute | solution.py:22
  5.2 1.0 %copy-done.2 = bf16[128,4096]{1,0:T(8,128)(2,1)} copy-done((bf16[128,4096]{1,0:T(8,128)(2,1)}, bf16[128,4096]{1,0:T(8,128)(2,1)S(1)}, u32[]{:S(2)}) %copy-start.2) | copy-done | bytes 1048600
  6.2 6.4 %collective-permute-start.1 = (bf16[128,4096]{1,0:T(8,128)(2,1)}, bf16[128,4096]{1,0:T(8,128)(2,1)}, u32[]{:S(2)}, u32[]{:S(2)}) collective-permute-start(bf16[128,4096]{1,0:T(8,128)(2,1)} %ko_hbm.1), channel_id=1, source_target_pairs={{2,4},{6,8},{10,12},{14,16},{18,20},{22,24},{26,28},{3,5},{7,9},{1... | collective-permute-start | bytes 3145736 | tf_op jit(solution)/shard_map/ppermute | solution.py:22
  12.5 6.1 %collective-permute-done.2.arrived_ref.qb_ref = bf16[128,4096]{1,0:T(8,128)(2,1)S(1)} collective-permute-done((bf16[128,4096]{1,0:T(8,128)(2,1)}, bf16[128,4096]{1,0:T(8,128)(2,1)S(1)}, u32[]{:S(2)}, u32[]{:S(2)}) %collective-permute-start.2) | collective-permute-done | bytes 1048608 | tf_op jit(solution)/shard_map/ppermute | solution.py:22
  18.6 1.0 %copy-done = bf16[128,4096]{1,0:T(8,128)(2,1)} copy-done((bf16[128,4096]{1,0:T(8,128)(2,1)}, bf16[128,4096]{1,0:T(8,128)(2,1)S(1)}, u32[]{:S(2)}) %copy-start) | copy-done | bytes 1048600
  20.2 1.2 %copy-done.1 = bf16[128,4096]{1,0:T(8,128)(2,1)S(1)} copy-done((bf16[128,4096]{1,0:T(8,128)(2,1)S(1)}, bf16[128,4096]{1,0:T(8,128)(2,1)}, u32[]{:S(2)}) %copy-start.1) | copy-done | bytes 1048600
  21.4 1.2 %copy-done.4 = bf16[128,4096]{1,0:T(8,128)(2,1)S(1)} copy-done((bf16[128,4096]{1,0:T(8,128)(2,1)S(1)}, bf16[128,4096]{1,0:T(8,128)(2,1)}, u32[]{:S(2)}) %copy-start.4) | copy-done | bytes 1048600
  22.6 1.2 %copy-done.5 = bf16[128,4096]{1,0:T(8,128)(2,1)S(1)} copy-done((bf16[128,4096]{1,0:T(8,128)(2,1)S(1)}, bf16[128,4096]{1,0:T(8,128)(2,1)}, u32[]{:S(2)}) %copy-start.5) | copy-done | bytes 1048600
  23.8 1.2 %copy-done.6 = bf16[128,4096]{1,0:T(8,128)(2,1)S(1)} copy-done((bf16[128,4096]{1,0:T(8,128)(2,1)S(1)}, bf16[128,4096]{1,0:T(8,128)(2,1)}, u32[]{:S(2)}) %copy-start.6) | copy-done | bytes 1048600
  25.1 0.7 copy-done.10
  25.7 2.0 %share.1 = (bf16[17,128,128]{2,1,0:T(8,128)(2,1)S(1)}, bf16[17,128,128]{2,1,0:T(8,128)(2,1)S(1)}, bf16[128,4096]{1,0:T(8,128)(2,1)S(1)}, bf16[128,4096]{1,0:T(8,...) custom-call(s32[1]{0:T(128)} %gate.1.place_ref, s32[10]{0:T(128)S(1)} %copy-done.10, ...), custom_call_target="tpu_custom_call" | custom-call | flops 1048576 | bytes 65536 | tf_op jit(solution)/shard_map/share/pallas_call | solution.py:389
  27.8 1.4 %collective-permute-start.6 = (bf16[17,128,128]{2,1,0:T(8,128)(2,1)S(1)}, bf16[17,128,128]{2,1,0:T(8,128)(2,1)S(1)}, u32[]{:S(2)}, u32[]{:S(2)}) collective-permute-start(bf16[17,128,128]{2,1,0:T(8,128)(2,1)S(1)} %get-tuple-element.26), channel_id=1, source_target_pairs={{2,4},{6,8},{10,12},{14,16},{18,20},{22,24},{26,28},{3,5},{7,9},{1... | collective-permute-start | bytes 1671176 | tf_op jit(solution)/shard_map/ppermute | solution.py:22
  29.1 1.3 %collective-permute-start.5 = (bf16[17,128,128]{2,1,0:T(8,128)(2,1)S(1)}, bf16[17,128,128]{2,1,0:T(8,128)(2,1)S(1)}, u32[]{:S(2)}, u32[]{:S(2)}) collective-permute-start(bf16[17,128,128]{2,1,0:T(8,128)(2,1)S(1)} %get-tuple-element.25), channel_id=1, source_target_pairs={{2,4},{6,8},{10,12},{14,16},{18,20},{22,24},{26,28},{3,5},{7,9},{1... | collective-permute-start | bytes 1671176 | tf_op jit(solution)/shard_map/ppermute | solution.py:22
  30.5 1.3 %collective-permute-start.8 = (bf16[128,4096]{1,0:T(8,128)(2,1)}, bf16[128,4096]{1,0:T(8,128)(2,1)S(1)}, u32[]{:S(2)}, u32[]{:S(2)}) collective-permute-start(bf16[128,4096]{1,0:T(8,128)(2,1)} %collective-permute-done.1.kp_ref), channel_id=1, source_target_pairs={{0,2},{4,6},{8,10},{12,14},{16,18},{20,22},{24,26},{28,30},{1,3},{... | collective-permute-start | bytes 3145736 | tf_op jit(solution)/shard_map/ppermute | solution.py:22
  31.8 18.4 %collective-permute-start.7 = (bf16[128,4096]{1,0:T(8,128)(2,1)S(1)}, bf16[128,4096]{1,0:T(8,128)(2,1)S(1)}, u32[]{:S(2)}, u32[]{:S(2)}) collective-permute-start(bf16[128,4096]{1,0:T(8,128)(2,1)S(1)} %get-tuple-element.27), channel_id=1, source_target_pairs={{2,4},{6,8},{10,12},{14,16},{18,20},{22,24},{26,28},{3,5},{7,9},{1... | collective-permute-start | bytes 3145736 | tf_op jit(solution)/shard_map/ppermute | solution.py:22
  50.2 6.0 %taps.1 = (bf16[32,128,1024]{2,1,0:T(8,128)(2,1)S(1)}, bf16[32,128,1024]{2,1,0:T(8,128)(2,1)S(1)}) custom-call(s32[1]{0:T(128)} %bitcast.place_ref, s32[10]{0:T(128)S(1)} %copy-done.10, bf16[256,128]{1,0:T(8,128)(2,1)S(1)} %copy-done.8), custom_call_target="tpu_custom_call" | custom-call | flops 1048576 | bytes 65536 | tf_op jit(solution)/shard_map/taps/pallas_call | solution.py:389
  56.3 1.3 %collective-permute-start.10 = (bf16[17,128,128]{2,1,0:T(8,128)(2,1)S(1)}, bf16[17,128,128]{2,1,0:T(8,128)(2,1)S(1)}, u32[]{:S(2)}, u32[]{:S(2)}) collective-permute-start(bf16[17,128,128]{2,1,0:T(8,128)(2,1)S(1)} %collective-permute-done.6.vp1_ref), channel_id=1, source_target_pairs={{0,2},{4,6},{8,10},{12,14},{16,18},{20,22},{24,26},{28,30},{1,3},{... | collective-permute-start | bytes 1671176 | tf_op jit(solution)/shard_map/ppermute | solution.py:22
  57.6 1.3 %collective-permute-start.9 = (bf16[17,128,128]{2,1,0:T(8,128)(2,1)S(1)}, bf16[17,128,128]{2,1,0:T(8,128)(2,1)S(1)}, u32[]{:S(2)}, u32[]{:S(2)}) collective-permute-start(bf16[17,128,128]{2,1,0:T(8,128)(2,1)S(1)} %collective-permute-done.5.vp0_ref), channel_id=1, source_target_pairs={{0,2},{4,6},{8,10},{12,14},{16,18},{20,22},{24,26},{28,30},{1,3},{... | collective-permute-start | bytes 1671176 | tf_op jit(solution)/shard_map/ppermute | solution.py:22
  58.9 4.9 %even.1 = (bf16[32,128,384]{2,1,0:T(8,128)(2,1)S(1)}, bf16[32,128,256]{2,1,0:T(8,128)(2,1)S(1)}, f32[128,4096]{1,0:T(8,128)S(1)}) custom-call(s32[1]{0:T(128)} %bitcast.place_ref, s32[10]{0:T(128)S(1)} %copy-done.10, bf16[128,4096]{1,0:T(8,128)(2,1)S(1)} %get-tuple-element.28.q_ref, bf16[128,4096]{1,0:T(8,128)(2,1)S(1)} %get-tuple-element.29.ko_ref, ...), custom_call_target="tpu_custom_call" | custom-call | flops 1048576 | bytes 65536 | tf_op jit(solution)/shard_map/even/pallas_call | solution.py:389
  63.8 5.9 %odd.1 = (bf16[32,128,128]{2,1,0:T(8,128)(2,1)S(1)}, f32[128,128]{1,0:T(8,128)S(1)}, f32[128,4096]{1,0:T(8,128)S(1)}) custom-call(s32[1]{0:T(128)} %bitcast.place_ref, s32[10]{0:T(128)S(1)} %copy-done.10, bf16[32,128,384]{2,1,0:T(8,128)(2,1)S(1)} %get-tuple-element.34.three_ref, bf16[32,128,256]{2,1,0:T(8,128)(2,1)S(1)} %get-tuple-element.35.two_ref, ...), custom_call_target="tpu_custom_call" | custom-call | flops 1048576 | bytes 65536 | tf_op jit(solution)/shard_map/odd/pallas_call | solution.py:389
  69.7 5.5 %finish.1 = bf16[128,4096]{1,0:T(8,128)(2,1)} custom-call(s32[1]{0:T(128)} %bitcast.place_ref, s32[10]{0:T(128)S(1)} %copy-done.10, bf16[128,4096]{1,0:T(8,128)(2,1)} %collective-permute-done.1.kp_ref, bf16[17,128,128]{2,1,0:T(8,128)(2,1)S(1)} %collective-permute-done.5.vp0_ref, bf16[17,128,128]{2,1,0:T(8,128)(2,1)S(1)} %collective-permute-done.6.vp1_ref, ...), custom_call_target="tpu_custom_call" | custom-call | flops 1048576 | bytes 65536 | tf_op jit(solution)/shard_map/finish/pallas_call | solution.py:389
  (26 shorter events, 0.6 us)
Async XLA Ops:
  0.0 5.2 %collective-permute-start = (bf16[128,4096]{1,0:T(8,128)(2,1)}, bf16[128,4096]{1,0:T(8,128)(2,1)S(1)}, u32[]{:S(2)}, u32[]{:S(2)}) collective-permute-start(bf16[128,4096]{1,0:T(8,128)(2,1)} %q_hbm.1), channel_id=1, source_target_pairs={{0,2},{4,6},{8,10},{12,14},{16,18},{20,22},{24,26},{28,30},{1,3},{... | collective-permute-start | bytes 3145736 | tf_op jit(solution)/shard_map/ppermute | solution.py:22
  1.3 17.3 %collective-permute-start.2 = (bf16[128,4096]{1,0:T(8,128)(2,1)}, bf16[128,4096]{1,0:T(8,128)(2,1)S(1)}, u32[]{:S(2)}, u32[]{:S(2)}) collective-permute-start(bf16[128,4096]{1,0:T(8,128)(2,1)} %q_hbm.1), channel_id=1, source_target_pairs={{4,2},{8,6},{12,10},{16,14},{20,18},{24,22},{28,26},{5,3},{9,7},{1... | collective-permute-start | bytes 3145736 | tf_op jit(solution)/shard_map/ppermute | solution.py:22
  2.6 17.5 %collective-permute-start.3 = (bf16[128,4096]{1,0:T(8,128)(2,1)}, bf16[128,4096]{1,0:T(8,128)(2,1)S(1)}, u32[]{:S(2)}, u32[]{:S(2)}) collective-permute-start(bf16[128,4096]{1,0:T(8,128)(2,1)} %ko_hbm.1), channel_id=1, source_target_pairs={{0,2},{4,6},{8,10},{12,14},{16,18},{20,22},{24,26},{28,30},{1,3},{... | collective-permute-start | bytes 3145736 | tf_op jit(solution)/shard_map/ppermute | solution.py:22
  3.9 16.2 %collective-permute-start.4 = (bf16[128,4096]{1,0:T(8,128)(2,1)}, bf16[128,4096]{1,0:T(8,128)(2,1)S(1)}, u32[]{:S(2)}, u32[]{:S(2)}) collective-permute-start(bf16[128,4096]{1,0:T(8,128)(2,1)} %vo_hbm.1), channel_id=1, source_target_pairs={{0,2},{4,6},{8,10},{12,14},{16,18},{20,22},{24,26},{28,30},{1,3},{... | collective-permute-start | bytes 3145736 | tf_op jit(solution)/shard_map/ppermute | solution.py:22
  5.2 1.0 %copy-start.2 = (bf16[128,4096]{1,0:T(8,128)(2,1)}, bf16[128,4096]{1,0:T(8,128)(2,1)S(1)}, u32[]{:S(2)}) copy-start(bf16[128,4096]{1,0:T(8,128)(2,1)S(1)} %collective-permute-done.qn_ref) | copy-start | bytes 3145732
  6.2 24.3 %collective-permute-start.1 = (bf16[128,4096]{1,0:T(8,128)(2,1)}, bf16[128,4096]{1,0:T(8,128)(2,1)}, u32[]{:S(2)}, u32[]{:S(2)}) collective-permute-start(bf16[128,4096]{1,0:T(8,128)(2,1)} %ko_hbm.1), channel_id=1, source_target_pairs={{2,4},{6,8},{10,12},{14,16},{18,20},{22,24},{26,28},{3,5},{7,9},{1... | collective-permute-start | bytes 3145736 | tf_op jit(solution)/shard_map/ppermute | solution.py:22
  18.6 1.0 %copy-start = (bf16[128,4096]{1,0:T(8,128)(2,1)}, bf16[128,4096]{1,0:T(8,128)(2,1)S(1)}, u32[]{:S(2)}) copy-start(bf16[128,4096]{1,0:T(8,128)(2,1)S(1)} %collective-permute-done.2.arrived_ref.qb_ref) | copy-start | bytes 3145732
  19.6 30.6 %copy-start.8 = (bf16[256,128]{1,0:T(8,128)(2,1)S(1)}, bf16[256,128]{1,0:T(8,128)(2,1)}, u32[]{:S(2)}) copy-start(bf16[256,128]{1,0:T(8,128)(2,1)} %filters_ref.1) | copy-start | bytes 196612
  19.6 39.3 %copy-start.7 = (f32[4096]{0:T(1024)S(1)}, f32[4096]{0:T(1024)}, u32[]{:S(2)}) copy-start(f32[4096]{0:T(1024)} %param.11) | copy-start | bytes 49156
  19.6 39.3 %copy-start.9 = (f32[4096]{0:T(1024)S(1)}, f32[4096]{0:T(1024)}, u32[]{:S(2)}) copy-start(f32[4096]{0:T(1024)} %param.13) | copy-start | bytes 49156
  20.1 1.2 %copy-start.1 = (bf16[128,4096]{1,0:T(8,128)(2,1)S(1)}, bf16[128,4096]{1,0:T(8,128)(2,1)}, u32[]{:S(2)}) copy-start(bf16[128,4096]{1,0:T(8,128)(2,1)} %copy-done) | copy-start | bytes 3145732
  21.4 1.2 %copy-start.4 = (bf16[128,4096]{1,0:T(8,128)(2,1)S(1)}, bf16[128,4096]{1,0:T(8,128)(2,1)}, u32[]{:S(2)}) copy-start(bf16[128,4096]{1,0:T(8,128)(2,1)} %q_hbm.1) | copy-start | bytes 3145732
  22.6 1.2 %copy-start.5 = (bf16[128,4096]{1,0:T(8,128)(2,1)S(1)}, bf16[128,4096]{1,0:T(8,128)(2,1)}, u32[]{:S(2)}) copy-start(bf16[128,4096]{1,0:T(8,128)(2,1)} %vo_hbm.1) | copy-start | bytes 3145732
  23.8 1.2 %copy-start.6 = (bf16[128,4096]{1,0:T(8,128)(2,1)S(1)}, bf16[128,4096]{1,0:T(8,128)(2,1)}, u32[]{:S(2)}) copy-start(bf16[128,4096]{1,0:T(8,128)(2,1)} %ko_hbm.1) | copy-start | bytes 3145732
  25.0 0.7 copy-start.10
  25.7 33.2 %copy-start.3 = (bf16[128,4096]{1,0:T(8,128)(2,1)S(1)}, bf16[128,4096]{1,0:T(8,128)(2,1)}, u32[]{:S(2)}) copy-start(bf16[128,4096]{1,0:T(8,128)(2,1)} %copy-done.2) | copy-start | bytes 3145732
  27.8 28.5 %collective-permute-start.6 = (bf16[17,128,128]{2,1,0:T(8,128)(2,1)S(1)}, bf16[17,128,128]{2,1,0:T(8,128)(2,1)S(1)}, u32[]{:S(2)}, u32[]{:S(2)}) collective-permute-start(bf16[17,128,128]{2,1,0:T(8,128)(2,1)S(1)} %get-tuple-element.26), channel_id=1, source_target_pairs={{2,4},{6,8},{10,12},{14,16},{18,20},{22,24},{26,28},{3,5},{7,9},{1... | collective-permute-start | bytes 1671176 | tf_op jit(solution)/shard_map/ppermute | solution.py:22
  29.1 28.4 %collective-permute-start.5 = (bf16[17,128,128]{2,1,0:T(8,128)(2,1)S(1)}, bf16[17,128,128]{2,1,0:T(8,128)(2,1)S(1)}, u32[]{:S(2)}, u32[]{:S(2)}) collective-permute-start(bf16[17,128,128]{2,1,0:T(8,128)(2,1)S(1)} %get-tuple-element.25), channel_id=1, source_target_pairs={{2,4},{6,8},{10,12},{14,16},{18,20},{22,24},{26,28},{3,5},{7,9},{1... | collective-permute-start | bytes 1671176 | tf_op jit(solution)/shard_map/ppermute | solution.py:22
  30.5 28.4 %collective-permute-start.8 = (bf16[128,4096]{1,0:T(8,128)(2,1)}, bf16[128,4096]{1,0:T(8,128)(2,1)S(1)}, u32[]{:S(2)}, u32[]{:S(2)}) collective-permute-start(bf16[128,4096]{1,0:T(8,128)(2,1)} %collective-permute-done.1.kp_ref), channel_id=1, source_target_pairs={{0,2},{4,6},{8,10},{12,14},{16,18},{20,22},{24,26},{28,30},{1,3},{... | collective-permute-start | bytes 3145736 | tf_op jit(solution)/shard_map/ppermute | solution.py:22
  31.8 37.9 %collective-permute-start.7 = (bf16[128,4096]{1,0:T(8,128)(2,1)S(1)}, bf16[128,4096]{1,0:T(8,128)(2,1)S(1)}, u32[]{:S(2)}, u32[]{:S(2)}) collective-permute-start(bf16[128,4096]{1,0:T(8,128)(2,1)S(1)} %get-tuple-element.27), channel_id=1, source_target_pairs={{2,4},{6,8},{10,12},{14,16},{18,20},{22,24},{26,28},{3,5},{7,9},{1... | collective-permute-start | bytes 3145736 | tf_op jit(solution)/shard_map/ppermute | solution.py:22
  56.3 7.6 %collective-permute-start.10 = (bf16[17,128,128]{2,1,0:T(8,128)(2,1)S(1)}, bf16[17,128,128]{2,1,0:T(8,128)(2,1)S(1)}, u32[]{:S(2)}, u32[]{:S(2)}) collective-permute-start(bf16[17,128,128]{2,1,0:T(8,128)(2,1)S(1)} %collective-permute-done.6.vp1_ref), channel_id=1, source_target_pairs={{0,2},{4,6},{8,10},{12,14},{16,18},{20,22},{24,26},{28,30},{1,3},{... | collective-permute-start | bytes 1671176 | tf_op jit(solution)/shard_map/ppermute | solution.py:22
  57.6 6.3 %collective-permute-start.9 = (bf16[17,128,128]{2,1,0:T(8,128)(2,1)S(1)}, bf16[17,128,128]{2,1,0:T(8,128)(2,1)S(1)}, u32[]{:S(2)}, u32[]{:S(2)}) collective-permute-start(bf16[17,128,128]{2,1,0:T(8,128)(2,1)S(1)} %collective-permute-done.5.vp0_ref), channel_id=1, source_target_pairs={{0,2},{4,6},{8,10},{12,14},{16,18},{20,22},{24,26},{28,30},{1,3},{... | collective-permute-start | bytes 1671176 | tf_op jit(solution)/shard_map/ppermute | solution.py:22

commit v8 on v6

--- a/solution.py
+++ b/solution.py
@@ -399,7 +399,7 @@
     slot_b0, slot_b1, slot_c = run(
         share_kernel,
         "share",
-        after(facts, taps_far),
+        after(facts, taps_far, query_near),
         (bf16(half + 1, rows, HEAD_DIM), bf16(half + 1, rows, HEAD_DIM), bf16(rows, width)),
         [pltpu.VMEM((2 * rows, 2 * rows), jnp.float32), pltpu.VMEM((rows, LANES), jnp.float32)],
         (query_back, queries, key_near, key_rows, value_near, value_rows),

time: 63.5 us -> 65.7 us (1.035)
  waiting for transfers between devices: 10 us -> 16 us
  starting transfers between devices: 23.4 us -> 19 us
  Pallas kernels: 19.6 us -> 20.3 us
    ppermute x11, waiting for transfers between devices: 10 us -> 16 us  [permuted(): return lax.ppermute(x, 'ctx', pairs)]
    ppermute x11, starting transfers between devices: 23.4 us -> 19 us  [permuted(): return lax.ppermute(x, 'ctx', pairs)]
    pallas_call x5, Pallas kernels: 19.6 us -> 20.3 us  [run(): pl.pallas_call(kernel, out_shape=out_shape, in_specs=[pl.BlockSpec(memory...]
  transfers between devices with their start and end apart: 11 -> 11, of which waited for: 3 -> 4; matrix products, arithmetic and copies ran while one was open for 5% -> 5% of each run, Pallas kernels for 23% -> 24%
where the time goes in v8:
time: 65.7 us; the launch traced here: 65.2 us
  Pallas kernels  20.3 us (31%)
  starting transfers between devices  19 us (29%)
  waiting for transfers between devices  16 us (24%)
  local copies, waits for them, and re-layouts  5.18 us (8%)
  other arithmetic  2.49 us (4%)
  between operations  2.18 us (3%)
    pallas_call x5, Pallas kernels, run(): pl.pallas_call(kernel, out_shape=out_shape, in_specs=[pl.BlockSpec(memory...  20.3 us
    ppermute x11, starting transfers between devices, permuted(): return lax.ppermute(x, 'ctx', pairs)  19 us
    ppermute x11, waiting for transfers between devices, permuted(): return lax.ppermute(x, 'ctx', pairs)  16 us
    unnamed x14, local copies, waits for them, and re-layouts  4.52 us
  transfers between devices with their start and end apart: 11, of which 4 were waited for; matrix products, arithmetic and copies ran while one was open for 5% of the time, Pallas kernels for 24%

profile of v8, /device:TPU:28, one launch (start us, length us, event | category | flops | bytes accessed | tf_op | source)
XLA Modules:
  0.0 65.2 jit_solution(16680067021299385289)
XLA Ops:
  0.0 3.7 %collective-permute-start.2 = (bf16[128,4096]{1,0:T(8,128)(2,1)}, bf16[128,4096]{1,0:T(8,128)(2,1)}, u32[]{:S(2)}, u32[]{:S(2)}) collective-permute-start(bf16[128,4096]{1,0:T(8,128)(2,1)} %q_ref.3), channel_id=1, source_target_pairs={{4,2},{8,6},{12,10},{16,14},{20,18},{24,22},{28,26},{5,3},{9,7},{1... | collective-permute-start | bytes 3145736 | tf_op jit(solution)/shard_map/ppermute | solution.py:22
  3.7 2.3 %collective-permute-start.1 = (bf16[128,4096]{1,0:T(8,128)(2,1)}, bf16[128,4096]{1,0:T(8,128)(2,1)}, u32[]{:S(2)}, u32[]{:S(2)}) collective-permute-start(bf16[128,4096]{1,0:T(8,128)(2,1)} %q_ref.3), channel_id=1, source_target_pairs={{0,2},{4,6},{8,10},{12,14},{16,18},{20,22},{24,26},{28,30},{1,3},{... | collective-permute-start | bytes 3145736 | tf_op jit(solution)/shard_map/ppermute | solution.py:22
  6.0 1.3 %collective-permute-start.3 = (bf16[128,4096]{1,0:T(8,128)(2,1)}, bf16[128,4096]{1,0:T(8,128)(2,1)S(1)}, u32[]{:S(2)}, u32[]{:S(2)}) collective-permute-start(bf16[128,4096]{1,0:T(8,128)(2,1)} %ko_ref.3), channel_id=1, source_target_pairs={{0,2},{4,6},{8,10},{12,14},{16,18},{20,22},{24,26},{28,30},{1,3},{... | collective-permute-start | bytes 3145736 | tf_op jit(solution)/shard_map/ppermute | solution.py:22
  7.3 1.4 %collective-permute-start.4 = (bf16[128,4096]{1,0:T(8,128)(2,1)}, bf16[128,4096]{1,0:T(8,128)(2,1)S(1)}, u32[]{:S(2)}, u32[]{:S(2)}) collective-permute-start(bf16[128,4096]{1,0:T(8,128)(2,1)} %vo_ref.5), channel_id=1, source_target_pairs={{0,2},{4,6},{8,10},{12,14},{16,18},{20,22},{24,26},{28,30},{1,3},{... | collective-permute-start | bytes 3145736 | tf_op jit(solution)/shard_map/ppermute | solution.py:22
  9.6 0.8 %select_reduce_fusion = s32[129]{0:T(256)S(1)} fusion(s32[10]{0:T(128)} %param.10, s32[129]{0:T(256)S(1)} %iota_add_fusion, s32[10]{0:T(128)S(1)} %bitcast.20), kind=kLoop, calls=%fused_computation | loop fusion | flops 3741 | bytes 1112 | tf_op jit(solution)/shard_map/reduce_sum | solution.py:33
  13.7 1.3 %collective-permute-start = (bf16[128,4096]{1,0:T(8,128)(2,1)}, bf16[128,4096]{1,0:T(8,128)(2,1)S(1)}, u32[]{:S(2)}, u32[]{:S(2)}) collective-permute-start(bf16[128,4096]{1,0:T(8,128)(2,1)} %ko_ref.3), channel_id=1, source_target_pairs={{2,4},{6,8},{10,12},{14,16},{18,20},{22,24},{26,28},{3,5},{7,9},{1... | collective-permute-start | bytes 3145736 | tf_op jit(solution)/shard_map/ppermute | solution.py:22
  15.1 0.8 %copy-done.6 = bf16[256,128]{1,0:T(8,128)(2,1)S(1)} copy-done((bf16[256,128]{1,0:T(8,128)(2,1)S(1)}, bf16[256,128]{1,0:T(8,128)(2,1)}, u32[]{:S(2)}) %copy-start.6) | copy-done | bytes 65560
  16.0 5.9 %taps.1 = (bf16[32,128,1024]{2,1,0:T(8,128)(2,1)S(1)}, bf16[32,128,1024]{2,1,0:T(8,128)(2,1)S(1)}) custom-call(s32[4]{0:T(128)S(1)} %pad_add_fusion.facts_ref, s32[128,1]{1,0:T(8,128)S(1)} %copy.10.st_ref, bf16[256,128]{1,0:T(8,128)(2,1)S(1)} %copy-done.6), custom_call_target="tpu_custom_call" | custom-call | flops 1048576 | bytes 65536 | tf_op jit(solution)/shard_map/taps/pallas_call | solution.py:357
  21.9 1.2 %copy-done = bf16[128,4096]{1,0:T(8,128)(2,1)S(1)} copy-done((bf16[128,4096]{1,0:T(8,128)(2,1)S(1)}, bf16[128,4096]{1,0:T(8,128)(2,1)}, u32[]{:S(2)}) %copy-start) | copy-done | bytes 1048600
  23.1 1.2 %copy-done.1 = bf16[128,4096]{1,0:T(8,128)(2,1)S(1)} copy-done((bf16[128,4096]{1,0:T(8,128)(2,1)S(1)}, bf16[128,4096]{1,0:T(8,128)(2,1)}, u32[]{:S(2)}) %copy-start.1) | copy-done | bytes 1048600
  24.4 1.2 %copy-done.2 = bf16[128,4096]{1,0:T(8,128)(2,1)S(1)} copy-done((bf16[128,4096]{1,0:T(8,128)(2,1)S(1)}, bf16[128,4096]{1,0:T(8,128)(2,1)}, u32[]{:S(2)}) %copy-start.2) | copy-done | bytes 1048600
  25.6 1.3 %share.1 = (bf16[17,128,128]{2,1,0:T(8,128)(2,1)S(1)}, bf16[17,128,128]{2,1,0:T(8,128)(2,1)S(1)}, bf16[128,4096]{1,0:T(8,128)(2,1)S(1)}) custom-call(s32[4]{0:T(128)S(1)} %pad_add_fusion.facts_ref, bf16[128,4096]{1,0:T(8,128)(2,1)} %collective-permute-done.2.qb_ref, bf16[128,4096]{1,0:T(8,128)(2,1)S(1)} %copy-done.2, ...), custom_call_target="tpu_custom_call" | custom-call | flops 1048576 | bytes 65536 | tf_op jit(solution)/shard_map/share/pallas_call | solution.py:357
  26.9 1.3 %collective-permute-start.5 = (bf16[17,128,128]{2,1,0:T(8,128)(2,1)S(1)}, bf16[17,128,128]{2,1,0:T(8,128)(2,1)S(1)}, u32[]{:S(2)}, u32[]{:S(2)}) collective-permute-start(bf16[17,128,128]{2,1,0:T(8,128)(2,1)S(1)} %get-tuple-element.22), channel_id=1, source_target_pairs={{2,4},{6,8},{10,12},{14,16},{18,20},{22,24},{26,28},{3,5},{7,9},{1... | collective-permute-start | bytes 1671176 | tf_op jit(solution)/shard_map/ppermute | solution.py:22
  28.2 1.3 %collective-permute-start.6 = (bf16[17,128,128]{2,1,0:T(8,128)(2,1)S(1)}, bf16[17,128,128]{2,1,0:T(8,128)(2,1)S(1)}, u32[]{:S(2)}, u32[]{:S(2)}) collective-permute-start(bf16[17,128,128]{2,1,0:T(8,128)(2,1)S(1)} %get-tuple-element.23), channel_id=1, source_target_pairs={{2,4},{6,8},{10,12},{14,16},{18,20},{22,24},{26,28},{3,5},{7,9},{1... | collective-permute-start | bytes 1671176 | tf_op jit(solution)/shard_map/ppermute | solution.py:22
  29.5 1.4 %collective-permute-done.kp_ref = bf16[128,4096]{1,0:T(8,128)(2,1)S(1)} collective-permute-done((bf16[128,4096]{1,0:T(8,128)(2,1)}, bf16[128,4096]{1,0:T(8,128)(2,1)S(1)}, u32[]{:S(2)}, u32[]{:S(2)}) %collective-permute-start) | collective-permute-done | bytes 1048608 | tf_op jit(solution)/shard_map/ppermute | solution.py:22
  30.9 2.5 %collective-permute-start.8 = (bf16[128,4096]{1,0:T(8,128)(2,1)S(1)}, bf16[128,4096]{1,0:T(8,128)(2,1)S(1)}, u32[]{:S(2)}, u32[]{:S(2)}) collective-permute-start(bf16[128,4096]{1,0:T(8,128)(2,1)S(1)} %collective-permute-done.kp_ref), channel_id=1, source_target_pairs={{0,2},{4,6},{8,10},{12,14},{16,18},{20,22},{24,26},{28,30},{1,3},{... | collective-permute-start | bytes 3145736 | tf_op jit(solution)/shard_map/ppermute | solution.py:22
  33.5 1.3 %collective-permute-start.7 = (bf16[128,4096]{1,0:T(8,128)(2,1)S(1)}, bf16[128,4096]{1,0:T(8,128)(2,1)S(1)}, u32[]{:S(2)}, u32[]{:S(2)}) collective-permute-start(bf16[128,4096]{1,0:T(8,128)(2,1)S(1)} %get-tuple-element.24), channel_id=1, source_target_pairs={{2,4},{6,8},{10,12},{14,16},{18,20},{22,24},{26,28},{3,5},{7,9},{1... | collective-permute-start | bytes 3145736 | tf_op jit(solution)/shard_map/ppermute | solution.py:22
  34.8 8.3 %collective-permute-done.5.vp0_ref = bf16[17,128,128]{2,1,0:T(8,128)(2,1)S(1)} collective-permute-done((bf16[17,128,128]{2,1,0:T(8,128)(2,1)S(1)}, bf16[17,128,128]{2,1,0:T(8,128)(2,1)S(1)}, u32[]{:S(2)}, u32[]{:S(2)}) %collective-permute-start.5) | collective-permute-done | bytes 557088 | tf_op jit(solution)/shard_map/ppermute | solution.py:22
  43.1 1.3 %collective-permute-start.9 = (bf16[17,128,128]{2,1,0:T(8,128)(2,1)S(1)}, bf16[17,128,128]{2,1,0:T(8,128)(2,1)S(1)}, u32[]{:S(2)}, u32[]{:S(2)}) collective-permute-start(bf16[17,128,128]{2,1,0:T(8,128)(2,1)S(1)} %collective-permute-done.5.vp0_ref), channel_id=1, source_target_pairs={{0,2},{4,6},{8,10},{12,14},{16,18},{20,22},{24,26},{28,30},{1,3},{... | collective-permute-start | bytes 1671176 | tf_op jit(solution)/shard_map/ppermute | solution.py:22
  44.4 4.6 %collective-permute-done.6.vp1_ref = bf16[17,128,128]{2,1,0:T(8,128)(2,1)S(1)} collective-permute-done((bf16[17,128,128]{2,1,0:T(8,128)(2,1)S(1)}, bf16[17,128,128]{2,1,0:T(8,128)(2,1)S(1)}, u32[]{:S(2)}, u32[]{:S(2)}) %collective-permute-start.6) | collective-permute-done | bytes 557088 | tf_op jit(solution)/shard_map/ppermute | solution.py:22
  49.1 1.3 %collective-permute-start.10 = (bf16[17,128,128]{2,1,0:T(8,128)(2,1)S(1)}, bf16[17,128,128]{2,1,0:T(8,128)(2,1)S(1)}, u32[]{:S(2)}, u32[]{:S(2)}) collective-permute-start(bf16[17,128,128]{2,1,0:T(8,128)(2,1)S(1)} %collective-permute-done.6.vp1_ref), channel_id=1, source_target_pairs={{0,2},{4,6},{8,10},{12,14},{16,18},{20,22},{24,26},{28,30},{1,3},{... | collective-permute-start | bytes 1671176 | tf_op jit(solution)/shard_map/ppermute | solution.py:22
  50.5 7.7 %even.1 = (bf16[32,128,384]{2,1,0:T(8,128)(2,1)S(1)}, bf16[32,128,256]{2,1,0:T(8,128)(2,1)S(1)}, f32[128,4096]{1,0:T(8,128)S(1)}) custom-call(s32[4]{0:T(128)S(1)} %pad_add_fusion.facts_ref, s32[128,1]{1,0:T(8,128)S(1)} %copy.10.st_ref, bf16[128,4096]{1,0:T(8,128)(2,1)S(1)} %copy-done.3, bf16[128,4096]{1,0:T(8,128)(2,1)S(1)} %copy-done.1, ...), custom_call_target="tpu_custom_call" | custom-call | flops 1048576 | bytes 65536 | tf_op jit(solution)/shard_map/even/pallas_call | solution.py:357
  58.7 1.6 %collective-permute-done.7.c_ref = bf16[128,4096]{1,0:T(8,128)(2,1)S(1)} collective-permute-done((bf16[128,4096]{1,0:T(8,128)(2,1)S(1)}, bf16[128,4096]{1,0:T(8,128)(2,1)S(1)}, u32[]{:S(2)}, u32[]{:S(2)}) %collective-permute-start.7) | collective-permute-done | bytes 1048608 | tf_op jit(solution)/shard_map/ppermute | solution.py:22
  60.3 4.9 %finish.1 = bf16[128,4096]{1,0:T(8,128)(2,1)} custom-call(s32[4]{0:T(128)S(1)} %pad_add_fusion.facts_ref, s32[128,1]{1,0:T(8,128)S(1)} %copy.10.st_ref, bf16[128,4096]{1,0:T(8,128)(2,1)S(1)} %collective-permute-done.kp_ref, bf16[17,128,128]{2,1,0:T(8,128)(2,1)S(1)} %collective-permute-done.5.vp0_ref, ...), custom_call_target="tpu_custom_call" | custom-call | flops 1048576 | bytes 65536 | tf_op jit(solution)/shard_map/finish/pallas_call | solution.py:357
  (27 shorter events, 2.9 us)
Async XLA Ops:
  0.0 21.9 %collective-permute-start.2 = (bf16[128,4096]{1,0:T(8,128)(2,1)}, bf16[128,4096]{1,0:T(8,128)(2,1)}, u32[]{:S(2)}, u32[]{:S(2)}) collective-permute-start(bf16[128,4096]{1,0:T(8,128)(2,1)} %q_ref.3), channel_id=1, source_target_pairs={{4,2},{8,6},{12,10},{16,14},{20,18},{24,22},{28,26},{5,3},{9,7},{1... | collective-permute-start | bytes 3145736 | tf_op jit(solution)/shard_map/ppermute | solution.py:22
  3.7 18.2 %collective-permute-start.1 = (bf16[128,4096]{1,0:T(8,128)(2,1)}, bf16[128,4096]{1,0:T(8,128)(2,1)}, u32[]{:S(2)}, u32[]{:S(2)}) collective-permute-start(bf16[128,4096]{1,0:T(8,128)(2,1)} %q_ref.3), channel_id=1, source_target_pairs={{0,2},{4,6},{8,10},{12,14},{16,18},{20,22},{24,26},{28,30},{1,3},{... | collective-permute-start | bytes 3145736 | tf_op jit(solution)/shard_map/ppermute | solution.py:22
  6.0 15.9 %collective-permute-start.3 = (bf16[128,4096]{1,0:T(8,128)(2,1)}, bf16[128,4096]{1,0:T(8,128)(2,1)S(1)}, u32[]{:S(2)}, u32[]{:S(2)}) collective-permute-start(bf16[128,4096]{1,0:T(8,128)(2,1)} %ko_ref.3), channel_id=1, source_target_pairs={{0,2},{4,6},{8,10},{12,14},{16,18},{20,22},{24,26},{28,30},{1,3},{... | collective-permute-start | bytes 3145736 | tf_op jit(solution)/shard_map/ppermute | solution.py:22
  7.3 14.6 %collective-permute-start.4 = (bf16[128,4096]{1,0:T(8,128)(2,1)}, bf16[128,4096]{1,0:T(8,128)(2,1)S(1)}, u32[]{:S(2)}, u32[]{:S(2)}) collective-permute-start(bf16[128,4096]{1,0:T(8,128)(2,1)} %vo_ref.5), channel_id=1, source_target_pairs={{0,2},{4,6},{8,10},{12,14},{16,18},{20,22},{24,26},{28,30},{1,3},{... | collective-permute-start | bytes 3145736 | tf_op jit(solution)/shard_map/ppermute | solution.py:22
  13.7 17.2 %collective-permute-start = (bf16[128,4096]{1,0:T(8,128)(2,1)}, bf16[128,4096]{1,0:T(8,128)(2,1)S(1)}, u32[]{:S(2)}, u32[]{:S(2)}) collective-permute-start(bf16[128,4096]{1,0:T(8,128)(2,1)} %ko_ref.3), channel_id=1, source_target_pairs={{2,4},{6,8},{10,12},{14,16},{18,20},{22,24},{26,28},{3,5},{7,9},{1... | collective-permute-start | bytes 3145736 | tf_op jit(solution)/shard_map/ppermute | solution.py:22
  15.1 0.8 %copy-start.6 = (bf16[256,128]{1,0:T(8,128)(2,1)S(1)}, bf16[256,128]{1,0:T(8,128)(2,1)}, u32[]{:S(2)}) copy-start(bf16[256,128]{1,0:T(8,128)(2,1)} %filters_ref.1) | copy-start | bytes 196612
  21.9 1.2 %copy-start = (bf16[128,4096]{1,0:T(8,128)(2,1)S(1)}, bf16[128,4096]{1,0:T(8,128)(2,1)}, u32[]{:S(2)}) copy-start(bf16[128,4096]{1,0:T(8,128)(2,1)} %vo_ref.5) | copy-start | bytes 3145732
  23.1 1.2 %copy-start.1 = (bf16[128,4096]{1,0:T(8,128)(2,1)S(1)}, bf16[128,4096]{1,0:T(8,128)(2,1)}, u32[]{:S(2)}) copy-start(bf16[128,4096]{1,0:T(8,128)(2,1)} %ko_ref.3) | copy-start | bytes 3145732
  24.4 1.2 %copy-start.2 = (bf16[128,4096]{1,0:T(8,128)(2,1)S(1)}, bf16[128,4096]{1,0:T(8,128)(2,1)}, u32[]{:S(2)}) copy-start(bf16[128,4096]{1,0:T(8,128)(2,1)} %q_ref.3) | copy-start | bytes 3145732
  25.6 24.8 %copy-start.3 = (bf16[128,4096]{1,0:T(8,128)(2,1)S(1)}, bf16[128,4096]{1,0:T(8,128)(2,1)}, u32[]{:S(2)}) copy-start(bf16[128,4096]{1,0:T(8,128)(2,1)} %q_ref.3) | copy-start | bytes 3145732
  25.6 24.8 %copy-start.4 = (f32[4096]{0:T(1024)S(1)}, f32[4096]{0:T(1024)}, u32[]{:S(2)}) copy-start(f32[4096]{0:T(1024)} %param.11) | copy-start | bytes 49156
  25.6 24.8 %copy-start.5 = (f32[4096]{0:T(1024)S(1)}, f32[4096]{0:T(1024)}, u32[]{:S(2)}) copy-start(f32[4096]{0:T(1024)} %param.13) | copy-start | bytes 49156
  26.9 16.2 %collective-permute-start.5 = (bf16[17,128,128]{2,1,0:T(8,128)(2,1)S(1)}, bf16[17,128,128]{2,1,0:T(8,128)(2,1)S(1)}, u32[]{:S(2)}, u32[]{:S(2)}) collective-permute-start(bf16[17,128,128]{2,1,0:T(8,128)(2,1)S(1)} %get-tuple-element.22), channel_id=1, source_target_pairs={{2,4},{6,8},{10,12},{14,16},{18,20},{22,24},{26,28},{3,5},{7,9},{1... | collective-permute-start | bytes 1671176 | tf_op jit(solution)/shard_map/ppermute | solution.py:22
  28.2 20.8 %collective-permute-start.6 = (bf16[17,128,128]{2,1,0:T(8,128)(2,1)S(1)}, bf16[17,128,128]{2,1,0:T(8,128)(2,1)S(1)}, u32[]{:S(2)}, u32[]{:S(2)}) collective-permute-start(bf16[17,128,128]{2,1,0:T(8,128)(2,1)S(1)} %get-tuple-element.23), channel_id=1, source_target_pairs={{2,4},{6,8},{10,12},{14,16},{18,20},{22,24},{26,28},{3,5},{7,9},{1... | collective-permute-start | bytes 1671176 | tf_op jit(solution)/shard_map/ppermute | solution.py:22
  30.9 19.5 %collective-permute-start.8 = (bf16[128,4096]{1,0:T(8,128)(2,1)S(1)}, bf16[128,4096]{1,0:T(8,128)(2,1)S(1)}, u32[]{:S(2)}, u32[]{:S(2)}) collective-permute-start(bf16[128,4096]{1,0:T(8,128)(2,1)S(1)} %collective-permute-done.kp_ref), channel_id=1, source_target_pairs={{0,2},{4,6},{8,10},{12,14},{16,18},{20,22},{24,26},{28,30},{1,3},{... | collective-permute-start | bytes 3145736 | tf_op jit(solution)/shard_map/ppermute | solution.py:22
  33.5 26.8 %collective-permute-start.7 = (bf16[128,4096]{1,0:T(8,128)(2,1)S(1)}, bf16[128,4096]{1,0:T(8,128)(2,1)S(1)}, u32[]{:S(2)}, u32[]{:S(2)}) collective-permute-start(bf16[128,4096]{1,0:T(8,128)(2,1)S(1)} %get-tuple-element.24), channel_id=1, source_target_pairs={{2,4},{6,8},{10,12},{14,16},{18,20},{22,24},{26,28},{3,5},{7,9},{1... | collective-permute-start | bytes 3145736 | tf_op jit(solution)/shard_map/ppermute | solution.py:22
  43.1 15.0 %collective-permute-start.9 = (bf16[17,128,128]{2,1,0:T(8,128)(2,1)S(1)}, bf16[17,128,128]{2,1,0:T(8,128)(2,1)S(1)}, u32[]{:S(2)}, u32[]{:S(2)}) collective-permute-start(bf16[17,128,128]{2,1,0:T(8,128)(2,1)S(1)} %collective-permute-done.5.vp0_ref), channel_id=1, source_target_pairs={{0,2},{4,6},{8,10},{12,14},{16,18},{20,22},{24,26},{28,30},{1,3},{... | collective-permute-start | bytes 1671176 | tf_op jit(solution)/shard_map/ppermute | solution.py:22
  49.1 9.0 %collective-permute-start.10 = (bf16[17,128,128]{2,1,0:T(8,128)(2,1)S(1)}, bf16[17,128,128]{2,1,0:T(8,128)(2,1)S(1)}, u32[]{:S(2)}, u32[]{:S(2)}) collective-permute-start(bf16[17,128,128]{2,1,0:T(8,128)(2,1)S(1)} %collective-permute-done.6.vp1_ref), channel_id=1, source_target_pairs={{0,2},{4,6},{8,10},{12,14},{16,18},{20,22},{24,26},{28,30},{1,3},{... | collective-permute-start | bytes 1671176 | tf_op jit(solution)/shard_map/ppermute | solution.py:22

commit v9 on v8

--- a/solution.py
+++ b/solution.py
@@ -34,7 +34,7 @@
     past = jnp.min(jnp.where(passed[count], jnp.int32(2**30), ends)) - first_row - count
     odd = (first_row // count) % 2
     facts = jnp.stack([odd, -starts[0], count - starts[count], past]).astype(jnp.int32)
-    return starts[:count].astype(jnp.int32).reshape(count, 1), facts
+    return starts[:count].astype(jnp.int32).reshape(count, 1), facts, ends
 
 
 def bias_of(rows, columns, row_first, key_first, start):
@@ -85,14 +85,9 @@
         body(step * UNROLL)
 
 
-def taps_kernel(facts_ref, st_ref, filters_ref, far_ref, near_ref, keep, lines):
-    rows = st_ref.shape[0]
-    tiles = far_ref.shape[0]
+def ring_kernel(place_ref, filters_ref, ring_ref, lines):
+    tiles, rows, _ = ring_ref.shape
     groups = filters_ref.shape[0] // tiles
-    st = st_ref[...]
-    row = lax.broadcasted_iota(jnp.int32, (rows, 2 * rows), 0)
-    key = lax.broadcasted_iota(jnp.int32, (rows, 2 * rows), 1) - rows
-    keep[...] = jnp.where((key >= st) & (key <= row) & (key > row - rows), 1.0, 0.0).astype(jnp.bfloat16)
     tap = lax.broadcasted_iota(jnp.int32, (rows, rows), 0)
     place = lax.broadcasted_iota(jnp.int32, (rows, rows), 1)
     turn = jnp.where((tap + place == 0) | (tap + place == rows), 1.0, 0.0).astype(jnp.bfloat16)
@@ -103,10 +98,16 @@
         some = lines[c]
         for g in range(groups):
             line = jnp.broadcast_to(some[g : g + 1], (rows, rows))
-            ring = pltpu.roll(line, 0, 1, stride=1, stride_axis=0).astype(jnp.bfloat16)
-            cols = slice(g * rows, (g + 1) * rows)
-            far_ref[c, :, cols] = ring * keep[:, :rows]
-            near_ref[c, :, cols] = ring * keep[:, rows:]
+            ring = pltpu.roll(line, 0, 1, stride=1, stride_axis=0)
+            ring_ref[c, :, g * rows : (g + 1) * rows] = ring.astype(jnp.bfloat16)
+
+
+def kept(st, width, far):
+    rows = st.shape[0]
+    row = lax.broadcasted_iota(jnp.int32, (rows, rows), 0)
+    key = lax.broadcasted_iota(jnp.int32, (rows, rows), 1)
+    keep = ((key - rows >= st) & (key > row)) if far else ((key >= st) & (key <= row))
+    return jnp.concatenate([jnp.where(keep, 1.0, 0.0).astype(jnp.bfloat16)] * (width // rows), axis=1)
 
 
 def share_kernel(facts_ref, qb_ref, q_ref, kn_ref, ko_ref, vn_ref, vo_ref, b0_ref, b1_ref, c_ref, bias, stat_ref):
@@ -175,21 +176,22 @@
     return jnp.concatenate([jnp.where(lane_group == g, x, jnp.zeros_like(x)) for g in range(groups)], axis=0)
 
 
-def convolve_own(att, squares, scale, taps_ref, gain_ref, bypass_ref, out_ref):
+def convolve_own(att, st, squares, scale, ring_ref, gain_ref, bypass_ref, out_ref):
     count, rows, _ = att.shape
+    keep = kept(st, ring_ref.shape[2], False)
     scale[...] = scale_of(squares, count * LANES)
 
     def tiles(first):
         for c in range(UNROLL):
             cols = columns(first + c)
             x = (att[first + c].astype(jnp.float32) * scale[...] * gain_ref[:, cols]).astype(jnp.bfloat16)
-            y = jnp.dot(taps_ref[first + c], spread(x, taps_ref.shape[2] // rows), preferred_element_type=jnp.float32)
+            y = jnp.dot(ring_ref[first + c] * keep, spread(x, ring_ref.shape[2] // rows), preferred_element_type=jnp.float32)
             out_ref[:, cols] = y + bypass_ref[:, cols] * x.astype(jnp.float32)
 
     each(count, tiles)
 
 
-def even_kernel(facts_ref, st_ref, q_ref, ko_ref, vo_ref, kp_ref, vp0_ref, vp1_ref, qn_ref, kn_ref, kf_ref, taps_ref, gain_ref, bypass_ref, three_ref, two_ref, out_ref, att, squares, scale, bias_own, bias_prev):
+def even_kernel(facts_ref, st_ref, q_ref, ko_ref, vo_ref, kp_ref, vp0_ref, vp1_ref, qn_ref, kn_ref, kf_ref, ring_ref, gain_ref, bypass_ref, three_ref, two_ref, out_ref, att, squares, scale, bias_own, bias_prev):
     rows = q_ref.shape[0]
     odd = facts_ref[ODD] == 1
     half = vp0_ref.shape[0] - 1
@@ -252,10 +254,10 @@
                 squares[...] = total[0]
 
             each(half, heads)
-        convolve_own(att, squares[...], scale, taps_ref, gain_ref, bypass_ref, out_ref)
-
-
-def odd_kernel(facts_ref, three_ref, two_ref, vo_ref, vn_ref, vf0_ref, vf1_ref, taps_ref, gain_ref, bypass_ref, near_ref, sq_near_ref, out_ref, att, squares, scale):
+        convolve_own(att, st_ref[...], squares[...], scale, ring_ref, gain_ref, bypass_ref, out_ref)
+
+
+def odd_kernel(facts_ref, st_ref, three_ref, two_ref, vo_ref, vn_ref, vf0_ref, vf1_ref, ring_ref, gain_ref, bypass_ref, near_ref, sq_near_ref, out_ref, att, squares, scale):
     rows = vo_ref.shape[0]
     half = vf0_ref.shape[0] - 1
 
@@ -285,10 +287,10 @@
                 sq_near_ref[...] = total_near
 
             each(half, heads)
-        convolve_own(att, squares[...], scale, taps_ref, gain_ref, bypass_ref, out_ref)
-
-
-def finish_kernel(facts_ref, st_ref, kp_ref, vp0_ref, vp1_ref, c_ref, near_ref, sq_ref, even_ref, odd_ref, taps_ref, gain_ref, out_ref, prev, squares, scale, bias):
+        convolve_own(att, st_ref[...], squares[...], scale, ring_ref, gain_ref, bypass_ref, out_ref)
+
+
+def finish_kernel(facts_ref, st_ref, kp_ref, vp0_ref, vp1_ref, c_ref, near_ref, sq_ref, even_ref, odd_ref, ring_ref, gain_ref, out_ref, prev, squares, scale, bias):
     rows = st_ref.shape[0]
     half = vp0_ref.shape[0] - 1
     width = prev.shape[0] * LANES
@@ -340,12 +342,13 @@
             each(half, heads)
 
     scale[...] = scale_of(squares[...], width)
+    keep = kept(st_ref[...], ring_ref.shape[2], True)
 
     def tiles(first):
         for c in range(UNROLL):
             cols = columns(first + c)
             x = (prev[first + c].astype(jnp.float32) * scale[...] * gain_ref[:, cols]).astype(jnp.bfloat16)
-            y = jnp.dot(taps_ref[first + c], spread(x, taps_ref.shape[2] // rows), preferred_element_type=jnp.float32)
+            y = jnp.dot(ring_ref[first + c] * keep, spread(x, ring_ref.shape[2] // rows), preferred_element_type=jnp.float32)
             out_ref[:, cols] = (y + jnp.where(odd, odd_ref[:, cols], even_ref[:, cols])).astype(jnp.bfloat16)
 
     each(2 * half, tiles)
@@ -372,7 +375,7 @@
     half = heads // 2
     groups, taps = filters.shape
     n = lax.axis_size("ctx")
-    st, facts = places(lengths, lax.axis_index("ctx") * rows, rows)
+    st, facts, ends = places(lengths, lax.axis_index("ctx") * rows, rows)
 
     back = [(i, i - 1) for i in range(2, n, 2)]
     within = [(i, i + 1) for i in range(0, n - 1, 2)]
@@ -386,20 +389,20 @@
     value_near = permuted(value_rows, within)
     query_near = permuted(queries, within)
 
-    taps_far, taps_near = run(
-        taps_kernel,
-        "taps",
+    ring = run(
+        ring_kernel,
+        "ring",
         facts,
-        (bf16(heads, rows, groups // heads * rows),) * 2,
-        [pltpu.VMEM((rows, 2 * rows), jnp.bfloat16), pltpu.VMEM((heads, groups // heads, taps), jnp.float32)],
-        (st, filters),
+        bf16(heads, rows, groups // heads * rows),
+        [pltpu.VMEM((heads, groups // heads, taps), jnp.float32)],
+        (filters,),
     )
-    key_across = permuted(after(key_rows, facts), across)
+    key_across = permuted(after(key_rows, ends), across)
 
     slot_b0, slot_b1, slot_c = run(
         share_kernel,
         "share",
-        after(facts, taps_far, query_near),
+        after(facts, ring, query_near),
         (bf16(half + 1, rows, HEAD_DIM), bf16(half + 1, rows, HEAD_DIM), bf16(rows, width)),
         [pltpu.VMEM((2 * rows, 2 * rows), jnp.float32), pltpu.VMEM((rows, LANES), jnp.float32)],
         (query_back, queries, key_near, key_rows, value_near, value_rows),
@@ -422,7 +425,7 @@
         facts,
         (bf16(heads, rows, 3 * rows), bf16(heads, rows, 2 * rows), f32(rows, width)),
         own_scratch + [pltpu.VMEM((rows, 3 * rows), jnp.float32), pltpu.VMEM((rows, 2 * rows), jnp.float32)],
-        (st, queries, key_rows, value_rows, key_across, *b_across, query_near, key_near, key_far, taps_near, gain, skip),
+        (st, queries, key_rows, value_rows, key_across, *b_across, query_near, key_near, key_far, ring, gain, skip),
     )
     near, near_squares, odd_part = run(
         odd_kernel,
@@ -430,7 +433,7 @@
         facts,
         (bf16(heads, rows, HEAD_DIM), f32(rows, LANES), f32(rows, width)),
         own_scratch,
-        (three, two, value_rows, value_near, *value_far, taps_near, gain, skip),
+        (st, three, two, value_rows, value_near, *value_far, ring, gain, skip),
     )
     return run(
         finish_kernel,
@@ -443,7 +446,7 @@
             pltpu.VMEM((rows, LANES), jnp.float32),
             pltpu.VMEM((rows, rows), jnp.float32),
         ],
-        (st, key_across, *b_across, c_across, near, near_squares, even_part, odd_part, taps_far, gain),
+        (st, key_across, *b_across, c_across, near, near_squares, even_part, odd_part, ring, gain),
     )
 
 

time: 65.7 us -> 76.7 us (1.17)
  the two profiles are of different devices: /device:TPU:28 before, /device:TPU:14 now
where the time goes in v9:
time: 76.7 us; the launch traced here: 76.2 us
  starting transfers between devices  32 us (42%)
  Pallas kernels  27.2 us (35%)
  local copies, waits for them, and re-layouts  8.15 us (11%)
  waiting for transfers between devices  4.33 us (6%)
  other arithmetic  2.49 us (3%)
  between operations  2.14 us (3%)
    ppermute x11, starting transfers between devices, permuted(): return lax.ppermute(x, 'ctx', pairs)  32 us
    pallas_call x5, Pallas kernels, run(): pl.pallas_call(kernel, out_shape=out_shape, in_specs=[pl.BlockSpec(memory...  27.2 us
    unnamed x18, local copies, waits for them, and re-layouts  7.45 us
    ppermute x11, waiting for transfers between devices, permuted(): return lax.ppermute(x, 'ctx', pairs)  4.33 us
  transfers between devices with their start and end apart: 11, of which 2 were waited for; matrix products, arithmetic and copies ran while one was open for 4% of the time, Pallas kernels for 24%

profile of v9, /device:TPU:14, one launch (start us, length us, event | category | flops | bytes accessed | tf_op | source)
XLA Modules:
  0.0 76.2 jit_solution(11401208536679105645)
XLA Ops:
  0.0 2.7 %collective-permute-start.1 = (bf16[128,4096]{1,0:T(8,128)(2,1)}, bf16[128,4096]{1,0:T(8,128)(2,1)}, u32[]{:S(2)}, u32[]{:S(2)}) collective-permute-start(bf16[128,4096]{1,0:T(8,128)(2,1)} %q_ref.3), channel_id=1, source_target_pairs={{0,2},{4,6},{8,10},{12,14},{16,18},{20,22},{24,26},{28,30},{1,3},{... | collective-permute-start | bytes 3145736 | tf_op jit(solution)/shard_map/ppermute | solution.py:22
  2.7 2.3 %collective-permute-start.2 = (bf16[128,4096]{1,0:T(8,128)(2,1)}, bf16[128,4096]{1,0:T(8,128)(2,1)}, u32[]{:S(2)}, u32[]{:S(2)}) collective-permute-start(bf16[128,4096]{1,0:T(8,128)(2,1)} %q_ref.3), channel_id=1, source_target_pairs={{4,2},{8,6},{12,10},{16,14},{20,18},{24,22},{28,26},{5,3},{9,7},{1... | collective-permute-start | bytes 3145736 | tf_op jit(solution)/shard_map/ppermute | solution.py:22
  5.1 2.3 %collective-permute-start.3 = (bf16[128,4096]{1,0:T(8,128)(2,1)}, bf16[128,4096]{1,0:T(8,128)(2,1)}, u32[]{:S(2)}, u32[]{:S(2)}) collective-permute-start(bf16[128,4096]{1,0:T(8,128)(2,1)} %ko_ref.3), channel_id=1, source_target_pairs={{0,2},{4,6},{8,10},{12,14},{16,18},{20,22},{24,26},{28,30},{1,3},{... | collective-permute-start | bytes 3145736 | tf_op jit(solution)/shard_map/ppermute | solution.py:22
  7.3 2.3 %collective-permute-start.4 = (bf16[128,4096]{1,0:T(8,128)(2,1)}, bf16[128,4096]{1,0:T(8,128)(2,1)}, u32[]{:S(2)}, u32[]{:S(2)}) collective-permute-start(bf16[128,4096]{1,0:T(8,128)(2,1)} %vo_ref.5), channel_id=1, source_target_pairs={{0,2},{4,6},{8,10},{12,14},{16,18},{20,22},{24,26},{28,30},{1,3},{... | collective-permute-start | bytes 3145736 | tf_op jit(solution)/shard_map/ppermute | solution.py:22
  9.6 0.8 %reduce-window.8 = s32[10,1]{0,1:T(1,128)S(1)} reduce-window(s32[10,1]{0,1:T(1,128)} %bitcast.22, s32[]{:T(128)} %constant.37.clone.1), window={size=10x1 pad=9_0x0_0}, to_apply=%region_0.0 | reduce-window | flops 90 | bytes 84 | tf_op jit(solution)/shard_map/reduce-window.3
  10.4 1.3 %collective-permute-start = (bf16[128,4096]{1,0:T(8,128)(2,1)}, bf16[128,4096]{1,0:T(8,128)(2,1)}, u32[]{:S(2)}, u32[]{:S(2)}) collective-permute-start(bf16[128,4096]{1,0:T(8,128)(2,1)} %ko_ref.3), channel_id=1, source_target_pairs={{2,4},{6,8},{10,12},{14,16},{18,20},{22,24},{26,28},{3,5},{7,9},{1... | collective-permute-start | bytes 3145736 | tf_op jit(solution)/shard_map/ppermute | solution.py:22
  11.8 0.8 %select_reduce_fusion = s32[129]{0:T(256)S(1)} fusion(s32[10]{0:T(128)} %param.10, s32[129]{0:T(256)S(1)} %iota_add_fusion, s32[10]{0:T(128)S(1)} %bitcast.20), kind=kLoop, calls=%fused_computation | loop fusion | flops 3741 | bytes 1112 | tf_op jit(solution)/shard_map/reduce_sum | solution.py:33
  13.9 0.6 fusion.1
  15.9 0.8 %copy-done.7 = bf16[256,128]{1,0:T(8,128)(2,1)S(1)} copy-done((bf16[256,128]{1,0:T(8,128)(2,1)S(1)}, bf16[256,128]{1,0:T(8,128)(2,1)}, u32[]{:S(2)}) %copy-start.7) | copy-done | bytes 65560
  16.8 5.1 %ring.1.ring_ref = bf16[32,128,1024]{2,1,0:T(8,128)(2,1)S(1)} custom-call(s32[4]{0:T(128)S(1)} %pad_add_fusion.place_ref.facts_ref, bf16[256,128]{1,0:T(8,128)(2,1)S(1)} %copy-done.7), custom_call_target="tpu_custom_call" | custom-call | flops 1048576 | bytes 65536 | tf_op jit(solution)/shard_map/ring/pallas_call | solution.py:360
  21.9 3.2 %copy-done = bf16[32,128,1024]{2,1,0:T(8,128)(2,1)} copy-done((bf16[32,128,1024]{2,1,0:T(8,128)(2,1)}, bf16[32,128,1024]{2,1,0:T(8,128)(2,1)S(1)}, u32[]{:S(2)}) %copy-start) | copy-done | bytes 8388632
  25.1 2.8 %collective-permute-done.2.qb_ref = bf16[128,4096]{1,0:T(8,128)(2,1)} collective-permute-done((bf16[128,4096]{1,0:T(8,128)(2,1)}, bf16[128,4096]{1,0:T(8,128)(2,1)}, u32[]{:S(2)}, u32[]{:S(2)}) %collective-permute-start.2) | collective-permute-done | bytes 1048608 | tf_op jit(solution)/shard_map/ppermute | solution.py:22
  27.9 2.9 %share.1 = (bf16[17,128,128]{2,1,0:T(8,128)(2,1)S(1)}, bf16[17,128,128]{2,1,0:T(8,128)(2,1)S(1)}, bf16[128,4096]{1,0:T(8,128)(2,1)}) custom-call(s32[4]{0:T(128)S(1)} %pad_add_fusion.place_ref.facts_ref, bf16[128,4096]{1,0:T(8,128)(2,1)} %collective-permute-done.2.qb_ref, bf16[128,4096]{1,0:T(8,128)(2,1)S(1)} %copy-done.5, ...), custom_call_target="tpu_custom_call" | custom-call | flops 1048576 | bytes 65536 | tf_op jit(solution)/shard_map/share/pallas_call | solution.py:360
  30.7 1.3 %collective-permute-start.5 = (bf16[17,128,128]{2,1,0:T(8,128)(2,1)S(1)}, bf16[17,128,128]{2,1,0:T(8,128)(2,1)}, u32[]{:S(2)}, u32[]{:S(2)}) collective-permute-start(bf16[17,128,128]{2,1,0:T(8,128)(2,1)S(1)} %get-tuple-element.19), channel_id=1, source_target_pairs={{2,4},{6,8},{10,12},{14,16},{18,20},{22,24},{26,28},{3,5},{7,9},{1... | collective-permute-start | bytes 1671176 | tf_op jit(solution)/shard_map/ppermute | solution.py:22
  32.0 1.3 %collective-permute-start.6 = (bf16[17,128,128]{2,1,0:T(8,128)(2,1)S(1)}, bf16[17,128,128]{2,1,0:T(8,128)(2,1)}, u32[]{:S(2)}, u32[]{:S(2)}) collective-permute-start(bf16[17,128,128]{2,1,0:T(8,128)(2,1)S(1)} %get-tuple-element.20), channel_id=1, source_target_pairs={{2,4},{6,8},{10,12},{14,16},{18,20},{22,24},{26,28},{3,5},{7,9},{1... | collective-permute-start | bytes 1671176 | tf_op jit(solution)/shard_map/ppermute | solution.py:22
  33.3 5.5 %collective-permute-start.8 = (bf16[128,4096]{1,0:T(8,128)(2,1)}, bf16[128,4096]{1,0:T(8,128)(2,1)}, u32[]{:S(2)}, u32[]{:S(2)}) collective-permute-start(bf16[128,4096]{1,0:T(8,128)(2,1)} %collective-permute-done.kp_ref), channel_id=1, source_target_pairs={{0,2},{4,6},{8,10},{12,14},{16,18},{20,22},{24,26},{28,30},{1,3},{... | collective-permute-start | bytes 3145736 | tf_op jit(solution)/shard_map/ppermute | solution.py:22
  38.9 1.3 %collective-permute-start.7 = (bf16[128,4096]{1,0:T(8,128)(2,1)}, bf16[128,4096]{1,0:T(8,128)(2,1)}, u32[]{:S(2)}, u32[]{:S(2)}) collective-permute-start(bf16[128,4096]{1,0:T(8,128)(2,1)} %get-tuple-element.21), channel_id=1, source_target_pairs={{2,4},{6,8},{10,12},{14,16},{18,20},{22,24},{26,28},{3,5},{7,9},{1... | collective-permute-start | bytes 3145736 | tf_op jit(solution)/shard_map/ppermute | solution.py:22
  40.1 1.6 %collective-permute-done.5.vp0_ref = bf16[17,128,128]{2,1,0:T(8,128)(2,1)} collective-permute-done((bf16[17,128,128]{2,1,0:T(8,128)(2,1)S(1)}, bf16[17,128,128]{2,1,0:T(8,128)(2,1)}, u32[]{:S(2)}, u32[]{:S(2)}) %collective-permute-start.5) | collective-permute-done | bytes 557088 | tf_op jit(solution)/shard_map/ppermute | solution.py:22
  41.7 9.6 %collective-permute-start.9 = (bf16[17,128,128]{2,1,0:T(8,128)(2,1)}, bf16[17,128,128]{2,1,0:T(8,128)(2,1)}, u32[]{:S(2)}, u32[]{:S(2)}) collective-permute-start(bf16[17,128,128]{2,1,0:T(8,128)(2,1)} %collective-permute-done.5.vp0_ref), channel_id=1, source_target_pairs={{0,2},{4,6},{8,10},{12,14},{16,18},{20,22},{24,26},{28,30},{1,3},{... | collective-permute-start | bytes 1671176 | tf_op jit(solution)/shard_map/ppermute | solution.py:22
  51.3 2.1 %collective-permute-start.10 = (bf16[17,128,128]{2,1,0:T(8,128)(2,1)}, bf16[17,128,128]{2,1,0:T(8,128)(2,1)}, u32[]{:S(2)}, u32[]{:S(2)}) collective-permute-start(bf16[17,128,128]{2,1,0:T(8,128)(2,1)} %collective-permute-done.6.vp1_ref), channel_id=1, source_target_pairs={{0,2},{4,6},{8,10},{12,14},{16,18},{20,22},{24,26},{28,30},{1,3},{... | collective-permute-start | bytes 1671176 | tf_op jit(solution)/shard_map/ppermute | solution.py:22
  53.6 3.4 %copy-done.1 = bf16[32,128,1024]{2,1,0:T(8,128)(2,1)S(1)} copy-done((bf16[32,128,1024]{2,1,0:T(8,128)(2,1)S(1)}, bf16[32,128,1024]{2,1,0:T(8,128)(2,1)}, u32[]{:S(2)}) %copy-start.1) | copy-done | bytes 8388632
  56.9 9.1 %even.1 = (bf16[32,128,384]{2,1,0:T(8,128)(2,1)S(1)}, bf16[32,128,256]{2,1,0:T(8,128)(2,1)S(1)}, f32[128,4096]{1,0:T(8,128)S(1)}) custom-call(s32[4]{0:T(128)S(1)} %pad_add_fusion.place_ref.facts_ref, s32[128,1]{1,0:T(8,128)S(1)} %copy.10.st_ref, bf16[128,4096]{1,0:T(8,128)(2,1)S(1)} %copy-done.5, bf16[128,4096]{1,0:T(8,128)(2,1)S(1)} %copy-done.4, ...), custom_call_target="tpu_custom_call" | custom-call | flops 1048576 | bytes 65536 | tf_op jit(solution)/shard_map/even/pallas_call | solution.py:360
  66.1 1.6 %odd.1 = (bf16[32,128,128]{2,1,0:T(8,128)(2,1)S(1)}, f32[128,128]{1,0:T(8,128)S(1)}, f32[128,4096]{1,0:T(8,128)S(1)}) custom-call(s32[4]{0:T(128)S(1)} %pad_add_fusion.place_ref.facts_ref, s32[128,1]{1,0:T(8,128)S(1)} %copy.10.st_ref, bf16[32,128,384]{2,1,0:T(8,128)(2,1)S(1)} %get-tuple-element.23.three_ref, ...), custom_call_target="tpu_custom_call" | custom-call | flops 1048576 | bytes 65536 | tf_op jit(solution)/shard_map/odd/pallas_call | solution.py:360
  67.7 8.5 %finish.1 = bf16[128,4096]{1,0:T(8,128)(2,1)} custom-call(s32[4]{0:T(128)S(1)} %pad_add_fusion.place_ref.facts_ref, s32[128,1]{1,0:T(8,128)S(1)} %copy.10.st_ref, bf16[128,4096]{1,0:T(8,128)(2,1)} %collective-permute-done.kp_ref, bf16[17,128,128]{2,1,0:T(8,128)(2,1)} %collective-permute-done.5.vp0_ref, bf16[17,128,128]{2,1,0:T(8,128)(2,1)} %collective-permute-done.6.vp1_ref, ...), custom_call_target="tpu_custom_call" | custom-call | flops 1048576 | bytes 65536 | tf_op jit(solution)/shard_map/finish/pallas_call | solution.py:360
  (31 shorter events, 0.9 us)
Async XLA Ops:
  0.0 25.1 %collective-permute-start.1 = (bf16[128,4096]{1,0:T(8,128)(2,1)}, bf16[128,4096]{1,0:T(8,128)(2,1)}, u32[]{:S(2)}, u32[]{:S(2)}) collective-permute-start(bf16[128,4096]{1,0:T(8,128)(2,1)} %q_ref.3), channel_id=1, source_target_pairs={{0,2},{4,6},{8,10},{12,14},{16,18},{20,22},{24,26},{28,30},{1,3},{... | collective-permute-start | bytes 3145736 | tf_op jit(solution)/shard_map/ppermute | solution.py:22
  2.7 25.1 %collective-permute-start.2 = (bf16[128,4096]{1,0:T(8,128)(2,1)}, bf16[128,4096]{1,0:T(8,128)(2,1)}, u32[]{:S(2)}, u32[]{:S(2)}) collective-permute-start(bf16[128,4096]{1,0:T(8,128)(2,1)} %q_ref.3), channel_id=1, source_target_pairs={{4,2},{8,6},{12,10},{16,14},{20,18},{24,22},{28,26},{5,3},{9,7},{1... | collective-permute-start | bytes 3145736 | tf_op jit(solution)/shard_map/ppermute | solution.py:22
  5.1 22.8 %collective-permute-start.3 = (bf16[128,4096]{1,0:T(8,128)(2,1)}, bf16[128,4096]{1,0:T(8,128)(2,1)}, u32[]{:S(2)}, u32[]{:S(2)}) collective-permute-start(bf16[128,4096]{1,0:T(8,128)(2,1)} %ko_ref.3), channel_id=1, source_target_pairs={{0,2},{4,6},{8,10},{12,14},{16,18},{20,22},{24,26},{28,30},{1,3},{... | collective-permute-start | bytes 3145736 | tf_op jit(solution)/shard_map/ppermute | solution.py:22
  7.3 20.5 %collective-permute-start.4 = (bf16[128,4096]{1,0:T(8,128)(2,1)}, bf16[128,4096]{1,0:T(8,128)(2,1)}, u32[]{:S(2)}, u32[]{:S(2)}) collective-permute-start(bf16[128,4096]{1,0:T(8,128)(2,1)} %vo_ref.5), channel_id=1, source_target_pairs={{0,2},{4,6},{8,10},{12,14},{16,18},{20,22},{24,26},{28,30},{1,3},{... | collective-permute-start | bytes 3145736 | tf_op jit(solution)/shard_map/ppermute | solution.py:22
  10.4 22.9 %collective-permute-start = (bf16[128,4096]{1,0:T(8,128)(2,1)}, bf16[128,4096]{1,0:T(8,128)(2,1)}, u32[]{:S(2)}, u32[]{:S(2)}) collective-permute-start(bf16[128,4096]{1,0:T(8,128)(2,1)} %ko_ref.3), channel_id=1, source_target_pairs={{2,4},{6,8},{10,12},{14,16},{18,20},{22,24},{26,28},{3,5},{7,9},{1... | collective-permute-start | bytes 3145736 | tf_op jit(solution)/shard_map/ppermute | solution.py:22
  15.9 0.8 %copy-start.7 = (bf16[256,128]{1,0:T(8,128)(2,1)S(1)}, bf16[256,128]{1,0:T(8,128)(2,1)}, u32[]{:S(2)}) copy-start(bf16[256,128]{1,0:T(8,128)(2,1)} %filters_ref.1) | copy-start | bytes 196612
  16.8 11.1 %copy-start.3 = (bf16[128,4096]{1,0:T(8,128)(2,1)S(1)}, bf16[128,4096]{1,0:T(8,128)(2,1)}, u32[]{:S(2)}) copy-start(bf16[128,4096]{1,0:T(8,128)(2,1)} %vo_ref.5) | copy-start | bytes 3145732
  16.8 11.1 %copy-start.4 = (bf16[128,4096]{1,0:T(8,128)(2,1)S(1)}, bf16[128,4096]{1,0:T(8,128)(2,1)}, u32[]{:S(2)}) copy-start(bf16[128,4096]{1,0:T(8,128)(2,1)} %ko_ref.3) | copy-start | bytes 3145732
  16.8 11.1 %copy-start.5 = (bf16[128,4096]{1,0:T(8,128)(2,1)S(1)}, bf16[128,4096]{1,0:T(8,128)(2,1)}, u32[]{:S(2)}) copy-start(bf16[128,4096]{1,0:T(8,128)(2,1)} %q_ref.3) | copy-start | bytes 3145732
  21.9 3.2 %copy-start = (bf16[32,128,1024]{2,1,0:T(8,128)(2,1)}, bf16[32,128,1024]{2,1,0:T(8,128)(2,1)S(1)}, u32[]{:S(2)}) copy-start(bf16[32,128,1024]{2,1,0:T(8,128)(2,1)S(1)} %ring.1.ring_ref) | copy-start | bytes 25165828
  25.1 28.4 %copy-start.6 = (f32[4096]{0:T(1024)S(1)}, f32[4096]{0:T(1024)}, u32[]{:S(2)}) copy-start(f32[4096]{0:T(1024)} %param.11) | copy-start | bytes 49156
  25.1 28.5 %copy-start.8 = (f32[4096]{0:T(1024)S(1)}, f32[4096]{0:T(1024)}, u32[]{:S(2)}) copy-start(f32[4096]{0:T(1024)} %param.13) | copy-start | bytes 49156
  30.7 10.9 %collective-permute-start.5 = (bf16[17,128,128]{2,1,0:T(8,128)(2,1)S(1)}, bf16[17,128,128]{2,1,0:T(8,128)(2,1)}, u32[]{:S(2)}, u32[]{:S(2)}) collective-permute-start(bf16[17,128,128]{2,1,0:T(8,128)(2,1)S(1)} %get-tuple-element.19), channel_id=1, source_target_pairs={{2,4},{6,8},{10,12},{14,16},{18,20},{22,24},{26,28},{3,5},{7,9},{1... | collective-permute-start | bytes 1671176 | tf_op jit(solution)/shard_map/ppermute | solution.py:22
  32.0 19.3 %collective-permute-start.6 = (bf16[17,128,128]{2,1,0:T(8,128)(2,1)S(1)}, bf16[17,128,128]{2,1,0:T(8,128)(2,1)}, u32[]{:S(2)}, u32[]{:S(2)}) collective-permute-start(bf16[17,128,128]{2,1,0:T(8,128)(2,1)S(1)} %get-tuple-element.20), channel_id=1, source_target_pairs={{2,4},{6,8},{10,12},{14,16},{18,20},{22,24},{26,28},{3,5},{7,9},{1... | collective-permute-start | bytes 1671176 | tf_op jit(solution)/shard_map/ppermute | solution.py:22
  33.3 20.2 %collective-permute-start.8 = (bf16[128,4096]{1,0:T(8,128)(2,1)}, bf16[128,4096]{1,0:T(8,128)(2,1)}, u32[]{:S(2)}, u32[]{:S(2)}) collective-permute-start(bf16[128,4096]{1,0:T(8,128)(2,1)} %collective-permute-done.kp_ref), channel_id=1, source_target_pairs={{0,2},{4,6},{8,10},{12,14},{16,18},{20,22},{24,26},{28,30},{1,3},{... | collective-permute-start | bytes 3145736 | tf_op jit(solution)/shard_map/ppermute | solution.py:22
  38.9 28.8 %collective-permute-start.7 = (bf16[128,4096]{1,0:T(8,128)(2,1)}, bf16[128,4096]{1,0:T(8,128)(2,1)}, u32[]{:S(2)}, u32[]{:S(2)}) collective-permute-start(bf16[128,4096]{1,0:T(8,128)(2,1)} %get-tuple-element.21), channel_id=1, source_target_pairs={{2,4},{6,8},{10,12},{14,16},{18,20},{22,24},{26,28},{3,5},{7,9},{1... | collective-permute-start | bytes 3145736 | tf_op jit(solution)/shard_map/ppermute | solution.py:22
  41.7 24.4 %collective-permute-start.9 = (bf16[17,128,128]{2,1,0:T(8,128)(2,1)}, bf16[17,128,128]{2,1,0:T(8,128)(2,1)}, u32[]{:S(2)}, u32[]{:S(2)}) collective-permute-start(bf16[17,128,128]{2,1,0:T(8,128)(2,1)} %collective-permute-done.5.vp0_ref), channel_id=1, source_target_pairs={{0,2},{4,6},{8,10},{12,14},{16,18},{20,22},{24,26},{28,30},{1,3},{... | collective-permute-start | bytes 1671176 | tf_op jit(solution)/shard_map/ppermute | solution.py:22
  51.3 14.8 %collective-permute-start.10 = (bf16[17,128,128]{2,1,0:T(8,128)(2,1)}, bf16[17,128,128]{2,1,0:T(8,128)(2,1)}, u32[]{:S(2)}, u32[]{:S(2)}) collective-permute-start(bf16[17,128,128]{2,1,0:T(8,128)(2,1)} %collective-permute-done.6.vp1_ref), channel_id=1, source_target_pairs={{0,2},{4,6},{8,10},{12,14},{16,18},{20,22},{24,26},{28,30},{1,3},{... | collective-permute-start | bytes 1671176 | tf_op jit(solution)/shard_map/ppermute | solution.py:22
  53.6 3.4 %copy-start.1 = (bf16[32,128,1024]{2,1,0:T(8,128)(2,1)S(1)}, bf16[32,128,1024]{2,1,0:T(8,128)(2,1)}, u32[]{:S(2)}) copy-start(bf16[32,128,1024]{2,1,0:T(8,128)(2,1)} %copy-done) | copy-start | bytes 25165828
  56.9 9.2 %copy-start.2 = (bf16[32,128,1024]{2,1,0:T(8,128)(2,1)S(1)}, bf16[32,128,1024]{2,1,0:T(8,128)(2,1)}, u32[]{:S(2)}) copy-start(bf16[32,128,1024]{2,1,0:T(8,128)(2,1)} %copy-done) | copy-start | bytes 25165828
